TPU v7x, 32 devices: a whole 2x2x4 slice. The times are simulated.
32 devices in a mesh: section: 2 (over core), batch: 8 (over z, x), tensor: 2 (over y).
Axes of the slice: x: 2, y: 2, z: 4, core: 2. Of those that a mesh axis runs over, the one named last changes fastest.
Arguments:
- section_ends: bfloat16 [2, 16, 512, 768], P('section', 'batch', 'tensor'), may hold values from -6 to 6
- lengths: int32 [16, 4], P('batch'), may hold values from 1 to 256, 512 in all within a row
- w_query: bfloat16 [2, 768, 768], P('section', None, 'tensor'), may hold values from -0.21875 to 0.21875
- b_query: float32 [2, 768], P('section', 'tensor'), may hold values from -3 to 3
- w_key: bfloat16 [2, 768, 768], P('section', None, 'tensor'), may hold values from -0.21875 to 0.21875
- w_value: bfloat16 [2, 768, 768], P('section', None, 'tensor'), may hold values from -0.21875 to 0.21875
- b_value: float32 [2, 768], P('section', 'tensor'), may hold values from -3 to 3
- w_out: bfloat16 [2, 768, 768], P('section', 'tensor'), may hold values from -0.875 to 0.875
- b_out: float32 [2, 768], P('section'), may hold values from -3 to 3
- norm1_gain: float32 [2, 768], P('section'), may hold values from 0.25 to 1.75
- norm1_bias: float32 [2, 768], P('section'), may hold values from -2 to 2
- w_inner: bfloat16 [2, 768, 3072], P('section', None, 'tensor'), may hold values from -0.21875 to 0.21875
- b_inner: float32 [2, 3072], P('section', 'tensor'), may hold values from -3 to 3
- w_outer: bfloat16 [2, 3072, 768], P('section', 'tensor'), may hold values from -0.109375 to 0.109375
- b_outer: float32 [2, 768], P('section'), may hold values from -3 to 3
- norm2_gain: float32 [2, 768], P('section'), may hold values from 0.25 to 1.75
- norm2_bias: float32 [2, 768], P('section'), may hold values from -2 to 2
Outputs:
- section_results: bfloat16 [2, 16, 512, 768], P('section', 'batch', 'tensor')
- grad_w_query: float32 [2, 768, 768], P('section', None, 'tensor')
- grad_b_query: float32 [2, 768], P('section', 'tensor')
- grad_w_key: float32 [2, 768, 768], P('section', None, 'tensor')
- grad_w_value: float32 [2, 768, 768], P('section', None, 'tensor')
- grad_b_value: float32 [2, 768], P('section', 'tensor')
- grad_w_out: float32 [2, 768, 768], P('section', 'tensor')
- grad_b_out: float32 [2, 768], P('section')
- grad_norm1_gain: float32 [2, 768], P('section')
- grad_norm1_bias: float32 [2, 768], P('section')
- grad_w_inner: float32 [2, 768, 3072], P('section', None, 'tensor')
- grad_b_inner: float32 [2, 3072], P('section', 'tensor')
- grad_w_outer: float32 [2, 3072, 768], P('section', 'tensor')
- grad_b_outer: float32 [2, 768], P('section')
- grad_norm2_gain: float32 [2, 768], P('section')
- grad_norm2_bias: float32 [2, 768], P('section')
Inputs may be any that keep to these rules, and one draw needn't show every extreme that they name: Each row of lengths sums to 512; a slot's sentences fill it in order with no padding, and tokens attend only within their own sentence.
All inputs are finite; a program needn't handle non-finite values.
Results may differ from a plain program's by a relative error of at most 0.025.
Values may be sent and summed in bfloat16 or wider, within the bound.
No kernel may reach another device: no remote copies, remote signals or barrier semaphores. Data moves between devices by JAX's collectives and lax.ppermute only.
A program may use at most 128 MiB of HBM per device.

v0:
```python
import functools
import math

import jax
import jax.numpy as jnp
from jax import lax
from jax.experimental import pallas as pl
from jax.experimental.pallas import tpu as pltpu
from jax.sharding import PartitionSpec as P

HD = 64
epsilon = 1e-06
root_half = 0.7071067811865476
inverse_root = 0.3989422804014327
BF = jnp.bfloat16
F32 = jnp.float32
RB = 128
VMEM_BYTES = 56 * 1024 * 1024

V_BQV, V_BO, V_G1, V_B1, V_BI, V_BU, V_G2, V_B2 = 0, 1, 2, 3, 4, 6, 7, 8
V_ROWS = 16


def dot(a, b):
    return lax.dot_general(a, b, (((1,), (0,)), ((), ())), preferred_element_type=F32)


def dot_nt(a, b):
    return lax.dot_general(a, b, (((1,), (1,)), ((), ())), preferred_element_type=F32)


def dot_tn(a, b):
    return lax.dot_general(a, b, (((0,), (0,)), ((), ())), preferred_element_type=F32)


def start_fetch(use_own, own, other, held, sems):
    @pl.when(use_own)
    def _():
        for i in range(len(own)):
            pltpu.make_async_copy(own[i], held[i], sems.at[i]).start()

    @pl.when(jnp.logical_not(use_own))
    def _():
        for i in range(len(own)):
            pltpu.make_async_copy(other[i], held[i], sems.at[i]).start()


def wait_fetch(i, own, held, sems):
    pltpu.make_async_copy(own[i], held[i], sems.at[i]).wait()


def row_blocks(total, body):
    def step(i, carry):
        body(pl.ds(pl.multiple_of(i * RB, RB), RB))
        return carry

    lax.fori_loop(0, total // RB, step, 0)


def loop(count, body, unroll=1):
    def step(i, carry):
        for j in range(unroll):
            body(i * unroll + j)
        return carry

    lax.fori_loop(0, count // unroll, step, 0)


def part_of(i, step):
    return pl.ds(i * step if isinstance(i, int) else pl.multiple_of(i * step, step), step)


def norm_rows(residue):
    center = residue - jnp.mean(residue, axis=-1, keepdims=True)
    inverse = lax.rsqrt(jnp.mean(center * center, axis=-1, keepdims=True) + epsilon)
    return center * inverse, inverse


def norm_back_rows(upstream, normal, inverse, gain):
    scaled = upstream * gain
    centred = scaled - jnp.mean(scaled, axis=-1, keepdims=True)
    return (centred - normal * jnp.mean(scaled * normal, axis=-1, keepdims=True)) * inverse


def column_sum(rows):
    return jnp.sum(rows, axis=0, keepdims=True)


def segment_bias(flags, bias):
    size = bias.shape[0]
    ends = [flags[2]]
    for i in range(3, 5):
        ends.append(ends[-1] + flags[i])
    row = lax.broadcasted_iota(jnp.int32, (1, size), 1)
    row_seg = sum((row >= e).astype(jnp.int32) for e in ends)

    def body(rows):
        col = lax.broadcasted_iota(jnp.int32, (RB, 1), 0) + rows.start
        col_seg = sum((col >= e).astype(jnp.int32) for e in ends)
        bias[rows, :] = jnp.where(col_seg == row_seg, 0.0, -1e30).astype(F32)

    row_blocks(size, body)


def attention_forward(flags, x, vec, weights, wait, outs, scratch):
    wq, wk, wv, wo = weights
    q_out, k_out, v_out, e_out, r_out, o_out, ot_out, *p_outs = outs
    qt_s, kh_s, vt_s, bias = scratch
    size = x.shape[0]
    width = wq.shape[1]
    heads = width // HD
    segment_bias(flags, bias)
    wait(0)
    wait(1)
    wait(2)

    def project(i):
        rows = part_of(i, 256)
        xb = x[rows, :]
        q = (dot(xb, wq[...]) + vec[V_BQV : V_BQV + 1, :width]).astype(BF).astype(F32) * (
            1.0 / math.sqrt(HD)
        )
        q_out[rows, :] = q.astype(BF)
        qt_s[:, rows] = q.T.astype(BF)
        k = dot(xb, wk[...]).astype(BF)
        k_out[rows, :] = k
        for h in range(heads):
            kh_s[h, rows, :] = k[:, h * HD : (h + 1) * HD]
        v = dot(xb, wv[...]) + vec[V_BQV : V_BQV + 1, width : 2 * width]
        v_out[rows, :] = v.astype(BF)
        vt_s[:, rows] = v.T.astype(BF)

    loop(size // 256, project)

    def attend(h):
        hs = part_of(h, HD)
        for j in range(size // 256):
            cols = pl.ds(j * 256, 256)
            scores = dot(kh_s[h], qt_s[hs, cols]) + bias[:, cols]
            highest = jnp.max(scores, axis=0, keepdims=True)
            raised = jnp.exp(scores - highest)
            inverse = 1.0 / jnp.sum(raised, axis=0, keepdims=True)
            raised = raised.astype(BF)
            e_out[h, :, cols] = raised
            r_out[h, :, cols] = inverse
            ot_out[hs, cols] = dot(vt_s[hs, :], raised) * inverse

    loop(heads, attend, 2)
    wait(3)

    for i, p_out in enumerate(p_outs):
        rows = part_of(i, size // 2)
        context = ot_out[:, rows].T.astype(BF)
        o_out[rows, :] = context
        p_out[...] = dot(context, wo[...]).astype(BF)


def attention_first_kernel(
    flags, own, far, peer_a, peer_b, vec,
    wq, wk, wv, wo, wq2, wk2, wv2, wo2,
    x_out, q_out, k_out, v_out, e_out, r_out, o_out, ot_out, p_out, p_out2,
    wq_s, wk_s, wv_s, wo_s, qt_s, kh_s, vt_s, bias, sems,
):
    first = flags[0] == 0
    held = (wq_s, wk_s, wv_s, wo_s)
    source = (wq, wk, wv, wo)
    start_fetch(first, source, (wq2, wk2, wv2, wo2), held, sems)
    half = own.shape[0]
    mine = pl.multiple_of(flags[1] * half, half)
    theirs = pl.multiple_of((1 - flags[1]) * half, half)
    x_out[pl.ds(mine, half), :] = jnp.where(first, own[...], far[...])
    x_out[pl.ds(theirs, half), :] = jnp.where(first, peer_a[...], peer_b[...])
    attention_forward(
        flags, x_out, vec, held, lambda i: wait_fetch(i, source, held, sems),
        (q_out, k_out, v_out, e_out, r_out, o_out, ot_out, p_out, p_out2), (qt_s, kh_s, vt_s, bias),
    )


def attention_next_kernel(
    flags, normal_one, part_a, part_a2, part_b, part_b2, vec_prev, vec,
    wq, wk, wv, wo, wq2, wk2, wv2, wo2,
    n2_out, i2_out, x_out, q_out, k_out, v_out, e_out, r_out, o_out, ot_out, p_out, p_out2,
    wq_s, wk_s, wv_s, wo_s, qt_s, kh_s, vt_s, bias, sems,
):
    held = (wq_s, wk_s, wv_s, wo_s)
    source = (wq, wk, wv, wo)
    start_fetch(flags[0] == 1, source, (wq2, wk2, wv2, wo2), held, sems)

    half = part_a.shape[0]
    for c, (one, two) in enumerate(((part_a, part_b), (part_a2, part_b2))):

        def body(rows, c=c, one=one, two=two):
            place = pl.ds(rows.start + c * half, RB)
            normal, inverse, output = second_norm(normal_one[place, :], one, two, vec_prev, rows)
            n2_out[place, :] = normal
            i2_out[place, :] = inverse
            x_out[place, :] = output.astype(BF)

        row_blocks(half, body)
    attention_forward(
        flags, x_out, vec, held, lambda i: wait_fetch(i, source, held, sems),
        (q_out, k_out, v_out, e_out, r_out, o_out, ot_out, p_out, p_out2), (qt_s, kh_s, vt_s, bias),
    )


def second_norm(normal_one, part_a, part_b, vec, rows):
    normed = normal_one * vec[V_G1 : V_G1 + 1, :] + vec[V_B1 : V_B1 + 1, :]
    total = part_a[rows, :].astype(F32) + part_b[rows, :].astype(F32)
    normal, inverse = norm_rows(total + vec[V_BU : V_BU + 1, :] + normed)
    return normal, inverse, normal * vec[V_G2 : V_G2 + 1, :] + vec[V_B2 : V_B2 + 1, :]


def ffn_forward_kernel(
    layer, flags, x, part_a, part_b, vec, wi, wu, wi2, wu2,
    n1_out, i1_out, n1b_out, a_out, d_out, p_out,
    wi_s, wu_s, sems,
):
    held = (wi_s, wu_s)
    source = (wi, wu)
    start_fetch(flags[0] == layer, source, (wi2, wu2), held, sems)
    size = x.shape[0]
    width = wi_s.shape[1]
    model = wi_s.shape[0]

    def first(rows):
        total = part_a[rows, :].astype(F32) + part_b[rows, :].astype(F32)
        normal, inverse = norm_rows(total + vec[V_BO : V_BO + 1, :] + x[rows, :].astype(F32))
        n1_out[rows, :] = normal
        i1_out[rows, :] = inverse
        n1b_out[rows, :] = (normal * vec[V_G1 : V_G1 + 1, :] + vec[V_B1 : V_B1 + 1, :]).astype(BF)

    row_blocks(size, first)
    wait_fetch(0, source, held, sems)
    block = 256

    def inner(rows):
        rows_in = n1b_out[rows, :]
        for j in range(width // block):
            cols = slice(j * block, (j + 1) * block)
            at = j * block
            bias = vec[V_BI + at // model : V_BI + at // model + 1, at % model : at % model + block]
            hidden = dot(rows_in, wi_s[:, cols]) + bias
            spread = 0.5 + 0.5 * lax.erf(hidden * root_half)
            a_out[rows, cols] = (hidden * spread).astype(BF)
            d_out[rows, cols] = (
                spread + hidden * jnp.exp(-0.5 * hidden * hidden) * inverse_root
            ).astype(BF)

    row_blocks(size, inner)
    wait_fetch(1, source, held, sems)

    def outer(i):
        rows = part_of(i, 256)
        p_out[rows, :] = dot(a_out[rows, :], wu_s[...]).astype(BF)

    loop(size // 256, outer)


def ffn_backward(g2, d, w, outs, wait, small):
    wi_s, wu_s = w
    gh_out, p_out = outs
    size = g2.shape[0]
    model, width = wi_s.shape
    wait(1)
    block = 384

    def hidden(i):
        rows = part_of(i, 256)
        gb = g2[rows, :]
        for j in range(width // block):
            cols = slice(j * block, (j + 1) * block)
            gh = (dot_nt(gb, wu_s[cols, :]) * d[rows, cols].astype(F32)).astype(BF)
            gh_out[rows, cols] = gh
            at = j * block
            small[3 + at // model : 4 + at // model, at % model : at % model + block] += column_sum(
                gh.astype(F32)
            )

    loop(size // 256, hidden)
    wait(0)

    def inner(i):
        rows = part_of(i, 256)
        p_out[rows, :] = dot_nt(gh_out[rows, :], wi_s[...]).astype(BF)

    loop(size // 256, inner)


def ffn_back_last_kernel(
    chunk, flags, normal_one, part_a, part_b, vec, own, far, peer_a, peer_b, d, small_in,
    wi, wu, wi2, wu2,
    y_out, g_out, gb_out, gh_out, p_out, small,
    gy_s, wi_s, wu_s, sems,
):
    held = (wi_s, wu_s)
    source = (wi, wu)
    second = flags[0] == 1
    start_fetch(second, source, (wi2, wu2), held, sems)
    here = flags[1] == chunk
    gy_s[...] = jnp.where(
        here,
        jnp.where(second, own[...], far[...]),
        jnp.where(second, peer_a[...], peer_b[...]),
    )
    small[...] = small_in[...]

    def body(rows):
        normal, inverse, output = second_norm(normal_one[rows, :], part_a, part_b, vec, rows)
        y_out[rows, :] = output.astype(BF)
        ffn_back_rows(gy_s[rows, :].astype(F32), normal, inverse, vec, rows, g_out, gb_out, small)

    row_blocks(y_out.shape[0], body)
    ffn_backward(gb_out, d, held, (gh_out, p_out), lambda i: wait_fetch(i, source, held, sems), small)


def ffn_back_rows(upstream, normal, inverse, vec, rows, g_out, gb_out, small):
    grad = norm_back_rows(upstream, normal, inverse, vec[V_G2 : V_G2 + 1, :])
    g_out[rows, :] = grad
    gb_out[rows, :] = grad.astype(BF)
    small[0:1, :] += column_sum(grad)
    small[1:2, :] += column_sum(upstream * normal)
    small[2:3, :] += column_sum(upstream)


def ffn_back_next_kernel(
    flags, g1, part_a, part_b, normal_two, inverse_two, vec, d, small_in, wi, wu, wi2, wu2,
    g_out, gb_out, gh_out, p_out, small,
    wi_s, wu_s, sems,
):
    held = (wi_s, wu_s)
    source = (wi, wu)
    start_fetch(flags[0] == 0, source, (wi2, wu2), held, sems)
    small[...] = small_in[...]

    def body(rows):
        total = part_a[rows, :].astype(F32) + part_b[rows, :].astype(F32)
        upstream = (g1[rows, :] + total).astype(BF).astype(F32)
        ffn_back_rows(
            upstream, normal_two[rows, :], inverse_two[rows, :], vec, rows, g_out, gb_out, small
        )

    row_blocks(g1.shape[0], body)
    ffn_backward(gb_out, d, held, (gh_out, p_out), lambda i: wait_fetch(i, source, held, sems), small)


def attention_back_kernel(
    layer, flags, g2, part_a, part_a2, part_b, part_b2, normal_one, inverse_one, vec,
    q, k, v, e, r, ot_f,
    wq, wk, wv, wo, wq2, wk2, wv2, wo2,
    g_out, gb_out, gqkv_out, p_out, p_out2, small,
    wq_s, wk_s, wv_s, wo_s, got_s, go_s, kt_s, vh_s, qh_s, gqt_s, sems,
):
    held = (wq_s, wk_s, wv_s, wo_s)
    source = (wq, wk, wv, wo)
    start_fetch(flags[0] == layer, source, (wq2, wk2, wv2, wo2), held, sems)
    size, model = g2.shape
    width = q.shape[1]
    heads = width // HD
    small[...] = jnp.zeros_like(small)

    half = size // 2
    for c, (one, two) in enumerate(((part_a, part_b), (part_a2, part_b2))):

        def body(rows, c=c, one=one, two=two):
            place = pl.ds(rows.start + c * half, RB)
            upstream = g2[place, :] + (one[rows, :].astype(F32) + two[rows, :].astype(F32))
            normal = normal_one[place, :]
            grad = norm_back_rows(upstream, normal, inverse_one[place, :], vec[V_G1 : V_G1 + 1, :])
            g_out[place, :] = grad
            gb_out[place, :] = grad.astype(BF)
            small[0:1, :] += column_sum(grad)
            small[1:2, :] += column_sum(upstream * normal)
            small[2:3, :] += column_sum(upstream)

        row_blocks(half, body)

    def split(i):
        rows = part_of(i, 256)
        kt_s[:, rows] = k[rows, :].astype(F32).T.astype(BF)
        for h in range(heads):
            hs = slice(h * HD, (h + 1) * HD)
            vh_s[h, rows, :] = v[rows, hs]
            qh_s[h, rows, :] = q[rows, hs]

    loop(size // 256, split)
    wait_fetch(3, source, held, sems)

    def context(i):
        rows = part_of(i, 256)
        gqt_s[:, rows] = dot_nt(gb_out[rows, :], wo_s[...]).T

    loop(size // 256, context)

    def attend(h):
        hs = part_of(h, HD)
        scaled = (gqt_s[hs, :] * r[h]).astype(BF)
        got_s[...] = scaled
        scaled = scaled.astype(F32)
        delta = column_sum(scaled * ot_f[hs, :])
        go_s[...] = scaled.T.astype(BF)
        grad_v = jnp.zeros((size, HD), F32)
        grad_k = jnp.zeros((size, HD), F32)
        for j in range(size // 256):
            cols = pl.ds(j * 256, 256)
            raised = e[h, :, cols]
            grad_p = dot(vh_s[h], got_s[:, cols]) - delta[:, j * 256 : (j + 1) * 256]
            grad_s = (raised.astype(F32) * grad_p).astype(BF)
            grad_v = grad_v + dot(raised, go_s[cols, :])
            grad_k = grad_k + dot(grad_s, qh_s[h, cols, :])
            gqt_s[hs, cols] = dot(kt_s[hs, :], grad_s) * (1.0 / math.sqrt(HD))
        vh_s[h] = grad_v.astype(BF)
        qh_s[h] = grad_k.astype(BF)

    loop(heads, attend, 2)
    for i in range(3):
        wait_fetch(i, source, held, sems)

    for i, p in enumerate((p_out, p_out2)):
        rows = pl.ds(i * half, half)
        gq = gqt_s[:, rows].T.astype(BF)
        gk = jnp.concatenate([qh_s[h, rows, :] for h in range(heads)], axis=1)
        gv = jnp.concatenate([vh_s[h, rows, :] for h in range(heads)], axis=1)
        gqkv_out[rows, :width] = gq
        gqkv_out[rows, width : 2 * width] = gk
        gqkv_out[rows, 2 * width :] = gv
        small[3:4, :width] += column_sum(gq.astype(F32))
        small[3:4, width:] += column_sum(gv.astype(F32))
        p[...] = (
            dot_nt(gq, wq_s[...]) + dot_nt(gk, wk_s[...]) + dot_nt(gv, wv_s[...])
        ).astype(BF)


HEAVY, LIGHT = 20, 0
PAD = 16
UNITS = (2, 2)
ORDER = (
    "KC2a", "KC2b", "KWF2", "KD2", "KWA2", "a2gn", "f2gn", "KC1a", "f2ba1", "KC1b", "KWF1",
    "f2aa1", "KD1", "KWA1", "f2aa2", "f1gn", "a2a1", "f2ba2", "a1gn", "f2aa3", "f1aa1", "a2a2",
    "f2ba3", "f1ba1", "f2aa4", "f1aa2", "a2a3", "f2ba4", "a1a1", "f1aa3", "f1ba2", "a2a4", "a1a2",
    "f1ba3", "f1aa4", "a1a3", "f1ba4", "finF", "a1a4", "finA",
)


def send_both(held, outs, sems):
    copies = [pltpu.make_async_copy(held.at[i], outs[i], sems.at[i]) for i in range(2)]
    for copy in copies:
        copy.start()
    for copy in copies:
        copy.wait()


def ffn_rows(units, block):
    if units == 1:
        return (2 * block + PAD,), lambda i, half: half * (2 * block + PAD) + i * block
    return (block + PAD, block), lambda i, half: i * 2 * (block + PAD) + half * (block + PAD * (1 - i))


def ffn_product_kernel(units, flags, a, gb, gh, n1b, small, ours, theirs, held, sems):
    model = gb.shape[1]
    block = model // 2
    extra = jnp.concatenate([small[...], jnp.zeros((PAD - 8, model), F32)], axis=0).astype(BF)
    sizes, start = ffn_rows(units, block)
    for i in range(2):

        def products(j, i=i):
            here = pl.ds(pl.multiple_of(start(i, flags[6] ^ j), 16), block)
            held[flags[0], here, :] = dot_tn(a[:, part_of(2 * j + i, block)], gb[...]).astype(BF)
            held[1 - flags[0], here, :] = dot_tn(
                n1b[:, i * block : (i + 1) * block], gh[:, part_of(j, model)]
            ).astype(BF)

        loop(2, products)
    for i in range(2):
        for half in range(2):
            at = (half + 1) * sizes[0]
            held[i, at - PAD : at, :] = extra
    send_both(held, (ours, theirs), sems)


def attention_product_kernel(flags, x, gqkv, o, gb, small, ours, theirs, held, sems):
    model = gb.shape[1]
    width = o.shape[1]
    rows = model + PAD

    def products(i):
        here = pl.ds(pl.multiple_of((flags[6] ^ (i % 2)) * rows, 16), model)
        held[flags[0] ^ (i // 2), here, :] = dot_tn(x[...], gqkv[:, part_of(i, width)]).astype(BF)

    loop(3, products)
    base = pl.multiple_of((flags[6] ^ 1) * rows, 16)
    for i in range(2):
        held[1 - flags[0], pl.ds(base + i * width, width), :] = dot_tn(
            o[...], gb[:, i * width : (i + 1) * width]
        ).astype(BF)
    extra = jnp.concatenate([small[:, :width], small[:, width:]], axis=0).astype(BF)
    for i in range(2):
        for half in range(2):
            held[i, half * rows + model : (half + 1) * rows, :] = extra
    send_both(held, (ours, theirs), sems)


def fetch_sums(flags, layers, held, sems):
    def copies(layer):
        pieces = layers[layer]
        for u, (sums, row, rows, at) in enumerate(pieces):
            for far in range(2):
                for beside in range(2):
                    slot = 2 * (flags[0] ^ far) + (flags[6] ^ beside)
                    i = 2 * far + beside
                    yield pltpu.make_async_copy(
                        sums[i].at[pl.ds(row, rows), :],
                        held.at[slot, pl.ds(at, rows), :],
                        sems.at[4 * u + i],
                    )

    for layer in range(2):

        @pl.when(flags[0] == layer)
        def _(layer=layer):
            for copy in copies(layer):
                copy.start()
            for copy in copies(layer):
                copy.wait()


def ffn_finish_kernel(units, flags, *refs):
    counts = [4 * n for n in units]
    sums = refs[: sum(counts)]
    outer, inside, bias_outer, gain, bias, bias_inner, held, sems = refs[sum(counts) :]
    model = outer.shape[1]
    block = model // 2
    layers = []
    for n, mine in zip(units, (sums[: counts[0]], sums[counts[0] :])):
        if n == 1:
            layers.append([(mine, 0, 2 * block + PAD, 0)])
        else:
            layers.append(
                [
                    (mine[:4], 0, block, 0),
                    (mine[4:], 0, block, block),
                    (mine[:4], block, PAD, 2 * block),
                ]
            )
    fetch_sums(flags, layers, held, sems)
    for j in range(2):
        outer[j * model : (j + 1) * model, :] = held[j, :model, :].astype(F32)
        inside[:, j * model : (j + 1) * model] = held[2 + j, :model, :].astype(F32)
    small = held[0, model : model + PAD, :].astype(F32)
    for i, out in enumerate((bias_outer, gain, bias)):
        out[...] = small[i : i + 1, :]
    for i in range(bias_inner.shape[1] // model):
        bias_inner[:, i * model : (i + 1) * model] = small[3 + i : 4 + i, :]


def attention_finish_kernel(flags, *refs):
    sums, (q, k, v, out, bias_out, gain, bias, bias_q, bias_v) = refs[:8], refs[8:17]
    held, sems = refs[17], refs[18]
    model, width = q.shape
    rows = model + PAD
    fetch_sums(flags, [[(sums[:4], 0, rows, 0)], [(sums[4:], 0, rows, 0)]], held, sems)
    q[...] = held[0, :model, :].astype(F32)
    k[...] = held[1, :model, :].astype(F32)
    v[...] = held[2, :model, :].astype(F32)
    for i in range(2):
        out[:, i * width : (i + 1) * width] = held[3, i * width : (i + 1) * width, :].astype(F32)
    left = held[0, model : model + PAD, :].astype(F32)
    for i, row in enumerate((bias_out, gain, bias)):
        row[:, :width] = left[i : i + 1, :]
        row[:, width:] = left[8 + i : 9 + i, :]
    bias_q[...] = left[3:4, :]
    bias_v[...] = left[11:12, :]


def ordered(array, after):
    return lax.optimization_barrier((array,) + tuple(after))[0] if after else array


def call(
    kernel, operands, spaces, outs, scratch, flops, after=(), out_space="v", chunk=0, before=(),
    weight=LIGHT,
):
    count = len(operands)
    out_space = out_space * len(outs) if len(out_space) == 1 else out_space
    passed = [i for i, c in enumerate(out_space) if c == "c" and before]
    extra = [before[i] for i in passed]
    operands = (ordered(operands[0], after),) + tuple(operands[1:])

    def body(*refs):
        kernel(*refs[:count], *refs[count + len(extra) :])

    def spec(letter, shape):
        if letter == "c":
            return pl.BlockSpec((shape[0] // 2, shape[1]), lambda i: (chunk, 0))
        return pl.BlockSpec(memory_space={"s": pltpu.SMEM, "v": pltpu.VMEM, "a": pl.ANY}[letter])

    return pl.pallas_call(
        body,
        grid=(1,) if "c" in spaces else (),
        out_shape=[jax.ShapeDtypeStruct(s, t) for s, t in outs],
        in_specs=[spec(c, x.shape) for c, x in zip(spaces, operands)]
        + [pl.BlockSpec(memory_space=pl.ANY)] * len(extra),
        out_specs=[spec(c, s) for c, (s, _) in zip(out_space, outs)],
        scratch_shapes=scratch,
        input_output_aliases={count + i: o for i, o in enumerate(passed)},
        compiler_params=pltpu.CompilerParams(vmem_limit_bytes=VMEM_BYTES),
        cost_estimate=pl.CostEstimate(
            flops=flops * weight, bytes_accessed=(8 << 20) * weight, transcendentals=0
        ),
    )(*operands, *extra)


def attention_call(
    flags, lead, lead_spaces, weights, size, model, width, kernel, extra_outs, after=()
):
    heads = width // HD
    outs = extra_outs + [
        ((size, model), BF),
        ((size, width), BF),
        ((size, width), BF),
        ((size, width), BF),
        ((heads, size, size), BF),
        ((heads, 1, size), F32),
        ((size, width), BF),
        ((width, size), F32),
        ((size // 2, model), BF),
        ((size // 2, model), BF),
    ]
    scratch = [pltpu.VMEM((model, width), BF)] * 3 + [
        pltpu.VMEM((width, model), BF),
        pltpu.VMEM((width, size), BF),
        pltpu.VMEM((heads, size, HD), BF),
        pltpu.VMEM((width, size), BF),
        pltpu.VMEM((size, size), F32),
        pltpu.SemaphoreType.DMA((4,)),
    ]
    return call(
        kernel, (flags,) + lead + weights, "s" + lead_spaces + "a" * 8, outs, scratch,
        2 * size * width * model * 4 + 4 * heads * size * size * HD, after, weight=HEAVY,
    )


def swap(block, axis):
    return lax.ppermute(block, axis, [(0, 1), (1, 0)])


def across(block, routes):
    return lax.ppermute(
        block, ("section", "tensor"), [(a[0] * 2 + a[1], b[0] * 2 + b[1]) for a, b in routes]
    )


def batch_pairs():
    return [(i, i ^ 1) for i in range(lax.axis_size("batch"))]


def pair_swap(block):
    return lax.ppermute(block, "batch", batch_pairs())


def line_end():
    line = lax.axis_index("batch") // 2
    return (line == 0) | (line == 3)


STAGES = (
    ("in", ((0, 2), (1, 3), (6, 4), (7, 5))),
    ("middle", ((2, 4), (3, 5), (4, 2), (5, 3))),
    ("out", ((2, 0), (3, 1), (4, 6), (5, 7))),
)


def rest_of_line(mine):
    count = lax.axis_size("batch")
    if count & (count - 1):
        lines = [list(range(i, count, 2)) for i in range(2)]
        return lax.psum(mine, "batch", axis_index_groups=lines)
    step = 2
    while step < count:
        mine = mine + lax.ppermute(mine, "batch", [(i, i ^ step) for i in range(count)])
        step *= 2
    return mine


def pad_rows(rows, count):
    return jnp.concatenate([rows, jnp.zeros((count - rows.shape[0], rows.shape[1]), rows.dtype)], 0)


def shards(
    section_ends, lengths, w_query, b_query, w_key, w_value, b_value, w_out, b_out,
    norm1_gain, norm1_bias, w_inner, b_inner, w_outer, b_outer, norm2_gain, norm2_bias,
):
    section = lax.axis_index("section")
    tensor = lax.axis_index("tensor")
    first = section == 0
    held = section_ends[0]
    half, model = held.shape[1], held.shape[2]
    size = 2 * half
    width = w_query.shape[2]
    inner = w_inner.shape[2]
    heads = width // HD
    flags = jnp.concatenate(
        [
            jnp.stack([section, tensor]).astype(jnp.int32),
            lax.dynamic_slice_in_dim(lengths, section, 1, 0)[0],
            (lax.axis_index("batch") % 2).astype(jnp.int32)[None],
        ]
    )

    x_peer_a = across(held[0], [((0, 0), (0, 1)), ((0, 1), (0, 0))])
    x_peer_b = across(held[1], [((0, 0), (1, 1)), ((0, 1), (1, 0))])
    x_far = across(held[1], [((0, 0), (1, 0)), ((0, 1), (1, 1))])

    attention_own = (w_query[0], w_key[0], w_value[0], w_out[0])
    ffn_own = (w_inner[0], w_outer[0])
    vec_own = pad_rows(
        jnp.concatenate(
            [
                jnp.concatenate([b_query, b_value], axis=1),
                b_out, norm1_gain, norm1_bias, b_inner.reshape(-1, model), b_outer,
                norm2_gain, norm2_bias,
            ],
            axis=0,
        ),
        V_ROWS,
    )
    vec_far = swap(vec_own, "section")
    attention_far = tuple(swap(w, "section") for w in attention_own)
    ffn_far = tuple(swap(w, "section") for w in ffn_own)
    attention_w = attention_own + attention_far
    ffn_w = ffn_own + ffn_far
    vec_one = jnp.where(first, vec_own, vec_far)
    vec_two = jnp.where(first, vec_far, vec_own)

    def send(parts):
        return [swap(part, "tensor") for part in parts]

    def ffn_forward(layer, x, parts, vec, after=()):
        outs = ()
        sums = []
        for c, (part, got) in enumerate(zip(parts, send(parts))):
            outs = call(
                functools.partial(ffn_forward_kernel, layer),
                (flags, x, part, got, vec) + ffn_w,
                "scvvvaaaa",
                [
                    ((size, model), F32), ((size, 1), F32), ((size, model), BF),
                    ((size, inner), BF), ((size, inner), BF), ((half, model), BF),
                ],
                [
                    pltpu.VMEM((model, inner), BF), pltpu.VMEM((inner, model), BF),
                    pltpu.SemaphoreType.DMA((2,)),
                ],
                2 * size * model * inner, after, "cccccv", c, outs,
            )
            sums.append(outs[-1])
        return *outs[:-1], sums

    x_one, *heads_one, part, part2 = attention_call(
        flags, (held[0], x_far, x_peer_a, x_peer_b, vec_one), "vvvvv", attention_w,
        size, model, width, attention_first_kernel, [], ffn_far,
    )
    n1_one, i1_one, n1b_one, a_one, d_one, parts = ffn_forward(
        0, x_one, (part, part2), vec_one
    )
    later = [ordered(held[i], (n1b_one,)) for i in range(2)]
    gy_peer_a = across(later[1], [((1, 0), (1, 1)), ((1, 1), (1, 0))])
    gy_peer_b = across(later[0], [((1, 0), (0, 1)), ((1, 1), (0, 0))])
    gy_far = across(later[0], [((1, 0), (0, 0)), ((1, 1), (0, 1))])

    n2_one, i2_one, x_two, *heads_two, part, part2 = attention_call(
        flags, (n1_one, *parts, *send(parts), vec_one, vec_two), "vvvvvvv", attention_w,
        size, model, width, attention_next_kernel, [((size, model), F32), ((size, 1), F32)],
    )
    n1_two, i1_two, n1b_two, a_two, d_two, parts_two = ffn_forward(
        1, x_two, (part, part2), vec_two, (gy_peer_a, gy_peer_b, gy_far)
    )

    ffn_outs = [
        ((size, model), F32), ((size, model), BF), ((size, inner), BF), ((half, model), BF),
        ((8, model), F32),
    ]
    ffn_scratch = [
        pltpu.VMEM((model, inner), BF), pltpu.VMEM((inner, model), BF),
        pltpu.SemaphoreType.DMA((2,)),
    ]

    def attention_back(layer, g2, parts, got, n1, i1, vec, saved, after):
        q, k, v, e, r, o, ot_f = saved
        *outs, part, part2, small = call(
            functools.partial(attention_back_kernel, layer),
            (flags, g2, *parts, *got, n1, i1, vec, q, k, v, e, r, ot_f) + attention_w,
            "s" + "v" * 14 + "a" * 8,
            [
                ((size, model), F32), ((size, model), BF), ((size, 3 * width), BF),
                ((half, model), BF), ((half, model), BF), ((8, model), F32),
            ],
            [pltpu.VMEM((model, width), BF)] * 3
            + [
                pltpu.VMEM((width, model), BF),
                pltpu.VMEM((HD, size), BF),
                pltpu.VMEM((size, HD), BF),
                pltpu.VMEM((width, size), BF),
                pltpu.VMEM((heads, size, HD), BF),
                pltpu.VMEM((heads, size, HD), BF),
                pltpu.VMEM((width, size), F32),
                pltpu.SemaphoreType.DMA((4,)),
            ],
            2 * size * width * model * 4 + 8 * heads * size * size * HD,
            after, weight=HEAVY,
        )
        return *outs, [part, part2], small

    state = {}
    last = ()
    chunked = [()]

    def add(groups, arrays, shapes):
        sums = []
        for group, (rows, _) in zip(groups, shapes):
            terms = [arrays[i][row : row + rows] for i, row in group]
            sums.append(sum(terms[1:], ordered(terms[0], last)))
        return sums

    def back_last(c):
        part = parts_two[c]
        outs = call(
            functools.partial(ffn_back_last_kernel, c),
            (flags, n1_two, part, got_two[c], vec_two, held[1], gy_far, gy_peer_a, gy_peer_b,
             d_two, small_zero if c == 0 else state["small_f2"]) + ffn_w,
            "sc" + "v" * 7 + "cv" + "a" * 4,
            [((size, model), BF)] + ffn_outs,
            [pltpu.VMEM((half, model), BF)] + ffn_scratch,
            2 * size * model * inner, last, "ccccvv", c, chunked[0],
        )
        chunked[0] = outs if c == 0 else ()
        state["small_f2"] = outs[-1]
        state["y_two"], state["g2_two"], state["g2b_two"], state["gh_two"] = outs[:4]
        state.setdefault("sums_two", []).append(outs[-2])
        state.setdefault("sums_two_got", []).append(swap(outs[-2], "tensor"))
        return outs[-1]

    def back_next(c):
        outs = call(
            ffn_back_next_kernel,
            (flags, state["g1_two"], state["p4_two"][c], state["p4_two_got"][c], n2_one, i2_one,
             vec_one, d_one, small_zero if c == 0 else state["small_f1"]) + ffn_w,
            "scvvccvcv" + "a" * 4,
            ffn_outs,
            ffn_scratch,
            2 * size * model * inner, last, "cccvv", c, chunked[0],
        )
        chunked[0] = outs if c == 0 else ()
        state["small_f1"] = outs[-1]
        state["g2_one"], state["g2b_one"], state["gh_one"] = outs[:3]
        state.setdefault("sums_one", []).append(outs[-2])
        state.setdefault("sums_one_got", []).append(swap(outs[-2], "tensor"))
        return outs[-1]

    def back_attention(name, layer, *rest):
        grad, rows, gqkv, parts, small = attention_back(
            layer, state["g2_" + name], state["sums_" + name], state["sums_" + name + "_got"],
            *rest, last,
        )
        state["g1_" + name], state["g1b_" + name], state["gqkv_" + name] = grad, rows, gqkv
        state["p4_" + name], state["small_a_" + name] = parts, small
        if name == "two":
            state["p4_two_got"] = send(parts)
        return small

    def put(base, ours, theirs):
        state[base] = ours
        state[base + "_got"] = swap(theirs, "section")

    def ffn_products(base, units, a, gb, gh, n1b, small):
        rows = 2 * (model + PAD)
        ours, theirs = call(
            functools.partial(ffn_product_kernel, units), (flags, a, gb, gh, n1b, small), "svvvvv",
            [((rows, model), BF)] * 2,
            [pltpu.VMEM((2, rows, model), BF), pltpu.SemaphoreType.DMA((2,))],
            4 * size * model * inner, last, "a",
        )
        put(base, ours, theirs)
        return ours

    def attention_products(base, gqkv, x, o, gb, small):
        rows = 2 * (model + PAD)
        ours, theirs = call(
            attention_product_kernel, (flags, x, gqkv, o, gb, small), "svvvvv",
            [((rows, width), BF)] * 2,
            [pltpu.VMEM((2, rows, width), BF), pltpu.SemaphoreType.DMA((2,))],
            8 * size * model * width, last, "a",
        )
        put(base, ours, theirs)
        return ours

    units = {}
    for base, count in (("f1", UNITS[0]), ("f2", UNITS[1])):
        row = 0
        for name, rows in zip("ab", ffn_rows(count, model // 2)[0]):
            units[base + name] = (base, row, rows, model)
            row += 2 * rows
    for base in ("a1", "a2"):
        units[base] = (base, 0, model + PAD, width)

    def give(base):
        names = [n for n in units if units[n][0] == base]
        outs = add(
            [[(0, units[n][1] + units[n][2]), (1, units[n][1] + units[n][2])] for n in names],
            (state[base], state[base + "_got"]),
            [units[n][2:] for n in names],
        )
        for n, out in zip(names, outs):
            state[n + "x"] = pair_swap(out)
        return outs[0]

    def step(name, stage):
        base, row, rows, columns = units[name]
        shape = (rows, columns)
        if stage == 0:
            (mine,) = add(
                [[(0, row), (1, row), (2, 0)]],
                (state[base], state[base + "_got"], state[name + "x"]), [shape],
            )
        elif lax.axis_size("batch") != 8:
            mine = rest_of_line(state[name]) if stage == 1 else state[name]
        elif stage < 3:
            (mine,) = add([[(0, 0), (1, 0)]], (state[name], state[name + "s"]), [shape])
        else:
            mine = jnp.where(at_end, state[name + "s"], ordered(state[name], last))
        state[name] = mine
        if stage < 3:
            state[name + "s"] = lax.ppermute(mine, "batch", STAGES[stage][1]) if lax.axis_size("batch") == 8 else None
        else:
            both = (mine, pair_swap(mine))
            route = (1, 0) if base[1] == "1" else (0, 1)
            state[name] = both + tuple(lax.ppermute(b, "section", [route]) for b in both)
        return mine

    def finish_ffn():
        sums = sum((state[n] for n in sorted(units) if n[0] == "f"), ())
        outs = call(
            functools.partial(ffn_finish_kernel, UNITS), (flags,) + sums, "s" + "a" * len(sums),
            [((inner, model), F32), ((model, inner), F32)] + [((1, model), F32)] * 3
            + [((1, inner), F32)],
            [pltpu.VMEM((4, model + PAD, model), BF), pltpu.SemaphoreType.DMA((12,))],
            size * model, last,
        )
        state["ffn"] = outs
        return outs[-1]

    def finish_attention():
        outs = call(
            attention_finish_kernel, (flags,) + state["a1"] + state["a2"], "s" + "a" * 8,
            [((model, width), F32)] * 3 + [((width, model), F32)] + [((1, model), F32)] * 3
            + [((1, width), F32)] * 2,
            [pltpu.VMEM((4, model + PAD, width), BF), pltpu.SemaphoreType.DMA((4,))],
            size * model, last,
        )
        state["attention"] = outs
        return outs[-1]

    at_end = line_end()
    small_zero = jnp.zeros((8, model), F32)
    got_two = send(parts_two)
    tasks = {
        "KC2a": lambda: back_last(0),
        "KC2b": lambda: back_last(1),
        "KWF2": lambda: ffn_products(
            "f2", UNITS[1], a_two, state["g2b_two"], state["gh_two"], n1b_two, state["small_f2"]
        ),
        "KD2": lambda: back_attention("two", 1, n1_two, i1_two, vec_two, heads_two),
        "KWA2": lambda: attention_products(
            "a2", state["gqkv_two"], x_two, heads_two[5], state["g1b_two"], state["small_a_two"]
        ),
        "KC1a": lambda: back_next(0),
        "KC1b": lambda: back_next(1),
        "KWF1": lambda: ffn_products(
            "f1", UNITS[0], a_one, state["g2b_one"], state["gh_one"], n1b_one, state["small_f1"]
        ),
        "KD1": lambda: back_attention("one", 0, n1_one, i1_one, vec_one, heads_one),
        "KWA1": lambda: attention_products(
            "a1", state["gqkv_one"], x_one, heads_one[5], state["g1b_one"], state["small_a_one"]
        ),
        "finF": finish_ffn,
        "finA": finish_attention,
    }
    for base in ("f1", "f2", "a1", "a2"):
        tasks[base + "gn"] = functools.partial(give, base)
    for name in units:
        for stage in range(4):
            tasks[name + "a" + str(stage + 1)] = functools.partial(step, name, stage)
    for name in ORDER:
        last = (tasks[name](),)

    part_one, part_one2 = state["p4_one"]
    part_mine = jnp.where(tensor == 0, part_one, part_one2)
    part_theirs = jnp.where(tensor == 0, part_one2, part_one)
    total = part_mine.astype(F32) + swap(part_theirs, "tensor").astype(F32)
    gx = (lax.dynamic_slice_in_dim(state["g1_one"], tensor * half, half, 0) + total).astype(BF)
    y_mine = lax.dynamic_slice_in_dim(state["y_two"], tensor * half, half, 0)
    y_far = lax.ppermute(y_mine, "section", [(0, 1)])
    gx_far = lax.ppermute(gx, "section", [(1, 0)])
    section_results = jnp.stack(
        [jnp.where(first, gx, y_far), jnp.where(first, gx_far, y_mine)], axis=0
    )[None]
    grad_outer, grad_inner, bias_outer, gain_two, bias_two, bias_inner = state["ffn"]
    grad_q, grad_k, grad_v, grad_out, bias_out, gain_one, bias_one, bias_q, bias_v = state["attention"]
    return (
        section_results,
        grad_q[None],
        bias_q,
        grad_k[None],
        grad_v[None],
        bias_v,
        grad_out[None],
        bias_out,
        gain_one,
        bias_one,
        grad_inner[None],
        bias_inner,
        grad_outer[None],
        bias_outer,
        gain_two,
        bias_two,
    )


def solution(mesh):
    in_specs = (
        P("section", "batch", "tensor", None),
        P("batch", None),
        P("section", None, "tensor"),
        P("section", "tensor"),
        P("section", None, "tensor"),
        P("section", None, "tensor"),
        P("section", "tensor"),
        P("section", "tensor", None),
        P("section", None),
        P("section", None),
        P("section", None),
        P("section", None, "tensor"),
        P("section", "tensor"),
        P("section", "tensor", None),
        P("section", None),
        P("section", None),
        P("section", None),
    )
    out_specs = (
        P("section", "batch", "tensor", None),
        P("section", None, "tensor"),
        P("section", "tensor"),
        P("section", None, "tensor"),
        P("section", None, "tensor"),
        P("section", "tensor"),
        P("section", "tensor", None),
        P("section", None),
        P("section", None),
        P("section", None),
        P("section", None, "tensor"),
        P("section", "tensor"),
        P("section", "tensor", None),
        P("section", None),
        P("section", None),
        P("section", None),
    )
    return jax.shard_map(shards, mesh=mesh, in_specs=in_specs, out_specs=out_specs, check_vma=False)
```

profile of v0, /device:TPU:11, one launch (start us, length us, event | category | flops | bytes accessed | tf_op | source)
XLA Modules:
  0.0 402.5 jit_solution(16718785602751744939)
XLA Ops:
  2.8 1.4 collective-permute-start.3
  5.7 3.3 collective-permute-start.5
  10.2 2.8 collective-permute-start.7
  13.0 3.5 collective-permute-done.4.refs_4_
  20.8 12.7 %shard_map.288 = (bf16[512,768]{1,0:T(8,128)(2,1)}, bf16[512,384]{1,0:T(8,128)(2,1)}, bf16[512,384]{1,0:T(8,128)(2,1)}, bf16[512,384]{1,0:T(8,128)(2,1)}, bf16[6...) custom-call(s32[7]{0:T(128)} %pad_add_fusion.refs_0_, ...), custom_call_target="tpu_custom_call" | custom-call | flops 32212254720 | bytes 167772160 | tf_op jit(solution)/shard_map/pallas_call | solution.py:596
  35.1 8.7 %collective-permute-done.11.refs_3_ = bf16[256,768]{1,0:T(8,128)(2,1)S(1)} collective-permute-done((bf16[256,768]{1,0:T(8,128)(2,1)}, bf16[256,768]{1,0:T(8,128)(2,1)S(1)}, u32[]{:S(2)}, u32[]{:S(2)}) %collective-permute-start.11) | collective-permute-done | bytes 393248 | tf_op jit(solution)/shard_map/ppermute | solution.py:643
  44.5 5.9 %shard_map.289 = (f32[512,768]{1,0:T(8,128)}, f32[512,1]{1,0:T(8,128)}, bf16[512,768]{1,0:T(8,128)(2,1)}, bf16[512,1536]{1,0:T(8,128)(2,1)}, bf16[512,1536]{1,0:T(8,128)(2,1)}, /*index=5*/bf16[256,768]{1,0:T(8,128)(2,1)}) custom-call(s32[7]{0:T(128)} %pad_add_fusion.refs_0_, bf16[512,768]{1,0:T(8,128)(2,1)} %get-tuple-element.165.refs_1_, ...), custom_call_target="tpu_custom_call" | custom-call | tf_op jit(solution)/shard_map/pallas_call | solution.py:596
  50.4 1.8 collective-permute-done.10.refs_3_
  52.9 6.0 %shard_map.290 = (f32[512,768]{1,0:T(8,128)}, f32[512,1]{1,0:T(8,128)}, bf16[512,768]{1,0:T(8,128)(2,1)}, bf16[512,1536]{1,0:T(8,128)(2,1)}, bf16[512,1536]{1,0:T(8,128)(2,1)}, /*index=5*/bf16[256,768]{1,0:T(8,128)(2,1)}) custom-call(s32[7]{0:T(128)} %pad_add_fusion.refs_0_, ...), custom_call_target="tpu_custom_call", output_to_operand_aliasing={{0}: (9, {}), {1}: (10, {}), {2}: (11, {}), {3}: (12, {}), ... | custom-call | tf_op jit(solution)/shard_map/pallas_call | solution.py:596
  60.5 4.1 %collective-permute-start.14 = (bf16[256,768]{1,0:T(8,128)(2,1)S(1)}, bf16[256,768]{1,0:T(8,128)(2,1)S(1)}, u32[]{:S(2)}, u32[]{:S(2)}) collective-permute-start(bf16[256,768]{1,0:T(8,128)(2,1)S(1)} %copy-done.40), channel_id=1, source_target_pairs={{16,0},{17,1},{18,2},{19,3},{20,4},{21,5},{22,6},{23,7},{24,8},{25... | collective-permute-start | bytes 1179656 | tf_op jit(solution)/shard_map/ppermute | solution.py:647
  64.6 2.4 collective-permute-start.13
  67.0 2.3 collective-permute-start.12
  69.3 7.3 %collective-permute-done.15.refs_4_ = bf16[256,768]{1,0:T(8,128)(2,1)S(1)} collective-permute-done((bf16[256,768]{1,0:T(8,128)(2,1)S(1)}, bf16[256,768]{1,0:T(8,128)(2,1)S(1)}, u32[]{:S(2)}, u32[]{:S(2)}) %collective-permute-start.15) | collective-permute-done | bytes 393248 | tf_op jit(solution)/shard_map/ppermute | solution.py:643
  77.3 13.7 %shard_map.291 = (f32[512,768]{1,0:T(8,128)}, f32[512,1]{1,0:T(8,128)}, bf16[512,768]{1,0:T(8,128)(2,1)}, bf16[512,384]{1,0:T(8,128)(2,1)}, bf16[512,384]{1,0:T(...) custom-call(s32[7]{0:T(128)} %pad_add_fusion.refs_0_, ...), custom_call_target="tpu_custom_call" | custom-call | flops 32212254720 | bytes 167772160 | tf_op jit(solution)/shard_map/pallas_call | solution.py:596
  92.7 5.3 %collective-permute-done.18.refs_3_ = bf16[256,768]{1,0:T(8,128)(2,1)S(1)} collective-permute-done((bf16[256,768]{1,0:T(8,128)(2,1)}, bf16[256,768]{1,0:T(8,128)(2,1)S(1)}, u32[]{:S(2)}, u32[]{:S(2)}) %collective-permute-start.18) | collective-permute-done | bytes 393248 | tf_op jit(solution)/shard_map/ppermute | solution.py:643
  98.8 5.9 %shard_map.292 = (f32[512,768]{1,0:T(8,128)}, f32[512,1]{1,0:T(8,128)}, bf16[512,768]{1,0:T(8,128)(2,1)}, bf16[512,1536]{1,0:T(8,128)(2,1)}, bf16[512,1536]{1,0:T(8,128)(2,1)}, /*index=5*/bf16[256,768]{1,0:T(8,128)(2,1)}) custom-call(s32[7]{0:T(128)} %pad_add_fusion.refs_0_, bf16[512,768]{1,0:T(8,128)(2,1)} %get-tuple-element.180.refs_1_, ...), custom_call_target="tpu_custom_call" | custom-call | tf_op jit(solution)/shard_map/pallas_call | solution.py:596
  106.8 5.9 %shard_map.293 = (f32[512,768]{1,0:T(8,128)}, f32[512,1]{1,0:T(8,128)}, bf16[512,768]{1,0:T(8,128)(2,1)}, bf16[512,1536]{1,0:T(8,128)(2,1)}, bf16[512,1536]{1,0:T(8,128)(2,1)}, /*index=5*/bf16[256,768]{1,0:T(8,128)(2,1)}) custom-call(s32[7]{0:T(128)} %pad_add_fusion.refs_0_, ...), custom_call_target="tpu_custom_call", output_to_operand_aliasing={{0}: (9, {}), {1}: (10, {}), {2}: (11, {}), {3}: (12, {}), ... | custom-call | tf_op jit(solution)/shard_map/pallas_call | solution.py:596
  115.6 7.4 %shard_map.294 = (bf16[512,768]{1,0:T(8,128)(2,1)}, f32[512,768]{1,0:T(8,128)}, bf16[512,768]{1,0:T(8,128)(2,1)}, bf16[512,1536]{1,0:T(8,128)(2,1)}, bf16[256,768]{1,0:T(8,128)(2,1)}, /*index=5*/f32[8,768]{1,0:T(8,128)}) custom-call(s32[7]{0:T(128)} %pad_add_fusion.refs_0_, f32[512,768]{1,0:T(8,128)} %get-tuple-element.188.refs_1_.refs_6_, ...), custom_call_target="tpu_custom_call" | custom-call | tf_op jit(solution)/shard_map/pallas_call | solution.py:596
  123.8 7.4 %shard_map.295 = (bf16[512,768]{1,0:T(8,128)(2,1)}, f32[512,768]{1,0:T(8,128)}, bf16[512,768]{1,0:T(8,128)(2,1)}, bf16[512,1536]{1,0:T(8,128)(2,1)}, bf16[256,768]{1,0:T(8,128)(2,1)}, /*index=5*/f32[8,768]{1,0:T(8,128)}) custom-call(s32[7]{0:T(128)} %pad_add_fusion.refs_0_, ...), custom_call_target="tpu_custom_call", output_to_operand_aliasing={{0}: (15, {}), {1}: (16, {}), {2}: (17, {}), {3}: (18, {})} | custom-call | tf_op jit(solution)/shard_map/pallas_call | solution.py:596
  132.8 7.8 %shard_map.296 = (bf16[1568,768]{1,0:T(8,128)(2,1)}, bf16[1568,768]{1,0:T(8,128)(2,1)}) custom-call(s32[7]{0:T(128)} %pad_add_fusion.refs_0_, bf16[512,1536]{1,0:T(8,128)(2,1)} %get-tuple-element.200.refs_1_, bf16[512,768]{1,0:T(8,128)(2,1)} %get-tuple-element.201.refs_2_, bf16[512,1536]{1,0:T(8,128)(2,1)} %get-tuple-element.202.refs_3_, ...), custom_call_target="tpu_custom_call" | custom-call | tf_op jit(solution)/shard_map/pallas_call | solution.py:596
  140.6 10.3 %collective-permute-start.24 = (bf16[1568,768]{1,0:T(8,128)(2,1)}, bf16[1568,768]{1,0:T(8,128)(2,1)S(1)}, u32[]{:S(2)}, u32[]{:S(2)}) collective-permute-start(bf16[1568,768]{1,0:T(8,128)(2,1)} %get-tuple-element.225), channel_id=1, source_target_pairs={{0,16},{16,0},{1,17},{17,1},{2,18},{18,2},{3,19},{19,3},{4,20},{20... | collective-permute-start | bytes 7225352 | tf_op jit(solution)/shard_map/ppermute | solution.py:643
  151.8 13.9 %shard_map.297 = (f32[512,768]{1,0:T(8,128)}, bf16[512,768]{1,0:T(8,128)(2,1)}, bf16[512,1152]{1,0:T(8,128)(2,1)}, bf16[256,768]{1,0:T(8,128)(2,1)}, bf16[256,768]{1,0:T(8,128)(2,1)}, /*index=5*/f32[8,768]{1,0:T(8,128)}) custom-call(s32[7]{0:T(128)} %pad_add_fusion.refs_0_, f32[512,768]{1,0:T(8,128)} %get-tuple-element.206.refs_1_, ...), custom_call_target="tpu_custom_call" | custom-call | flops 40265318400 | bytes 167772160 | tf_op jit(solution)/shard_map/pallas_call | solution.py:596
  165.8 5.9 %shard_map.298 = (bf16[1568,384]{1,0:T(8,128)(2,1)}, bf16[1568,384]{1,0:T(8,128)(2,1)}) custom-call(s32[7]{0:T(128)} %pad_add_fusion.refs_0_, bf16[512,768]{1,0:T(8,128)(2,1)} %get-tuple-element.180.refs_1_, bf16[512,1152]{1,0:T(8,128)(2,1)} %get-tuple-element.218.refs_2_, bf16[512,384]{1,0:T(8,128)(2,1)} %get-tuple-element.219.refs_3_, ...), custom_call_target="tpu_custom_call" | custom-call | tf_op jit(solution)/shard_map/pallas_call | solution.py:596
  171.6 2.2 collective-permute-start.23
  175.0 1.5 collective-permute-done.23
  181.3 2.5 collective-permute-done.25.refs_3_
  184.6 7.2 %shard_map.299 = (f32[512,768]{1,0:T(8,128)}, bf16[512,768]{1,0:T(8,128)(2,1)}, bf16[512,1536]{1,0:T(8,128)(2,1)}, bf16[256,768]{1,0:T(8,128)(2,1)}, f32[8,768]{1,0:T(8,128)}) custom-call(s32[7]{0:T(128)} %pad_add_fusion.refs_0_, f32[512,768]{1,0:T(8,128)} %get-tuple-element.227.refs_1_, bf16[256,768]{1,0:T(8,128)(2,1)} %get-tuple-element.228.refs_2_, ...), custom_call_target="tpu_custom_call" | custom-call | tf_op jit(solution)/shard_map/pallas_call | solution.py:596
  195.8 7.2 %shard_map.300 = (f32[512,768]{1,0:T(8,128)}, bf16[512,768]{1,0:T(8,128)(2,1)}, bf16[512,1536]{1,0:T(8,128)(2,1)}, bf16[256,768]{1,0:T(8,128)(2,1)}, f32[8,768]{1,0:T(8,128)}) custom-call(s32[7]{0:T(128)} %pad_add_fusion.refs_0_, f32[512,768]{1,0:T(8,128)} %get-tuple-element.227.refs_1_, ...), custom_call_target="tpu_custom_call", output_to_operand_aliasing={{0}: (13, {}), {1}: (14, {}), {2}: (15, {})} | custom-call | tf_op jit(solution)/shard_map/pallas_call | solution.py:596
  203.6 7.9 %shard_map.301 = (bf16[1568,768]{1,0:T(8,128)(2,1)}, bf16[1568,768]{1,0:T(8,128)(2,1)}) custom-call(s32[7]{0:T(128)} %pad_add_fusion.refs_0_, bf16[512,1536]{1,0:T(8,128)(2,1)} %get-tuple-element.242.refs_1_, bf16[512,768]{1,0:T(8,128)(2,1)} %get-tuple-element.243.refs_2_, bf16[512,1536]{1,0:T(8,128)(2,1)} %get-tuple-element.244.refs_3_, ...), custom_call_target="tpu_custom_call" | custom-call | tf_op jit(solution)/shard_map/pallas_call | solution.py:596
  211.5 1.3 fusion.8
  212.8 3.5 collective-permute-start.35
  219.7 14.1 %shard_map.302 = (f32[512,768]{1,0:T(8,128)}, bf16[512,768]{1,0:T(8,128)(2,1)}, bf16[512,1152]{1,0:T(8,128)(2,1)}, bf16[256,768]{1,0:T(8,128)(2,1)}, bf16[256,768]{1,0:T(8,128)(2,1)}, /*index=5*/f32[8,768]{1,0:T(8,128)}) custom-call(s32[7]{0:T(128)} %pad_add_fusion.refs_0_, f32[512,768]{1,0:T(8,128)} %get-tuple-element.248.refs_1_, ...), custom_call_target="tpu_custom_call" | custom-call | flops 40265318400 | bytes 167772160 | tf_op jit(solution)/shard_map/pallas_call | solution.py:596
  233.8 5.7 %shard_map.303 = (bf16[1568,384]{1,0:T(8,128)(2,1)}, bf16[1568,384]{1,0:T(8,128)(2,1)}) custom-call(s32[7]{0:T(128)} %pad_add_fusion.refs_0_, bf16[512,768]{1,0:T(8,128)(2,1)} %get-tuple-element.165.refs_1_, bf16[512,1152]{1,0:T(8,128)(2,1)} %get-tuple-element.264.refs_2_, bf16[512,384]{1,0:T(8,128)(2,1)} %get-tuple-element.265.refs_3_, ...), custom_call_target="tpu_custom_call" | custom-call | tf_op jit(solution)/shard_map/pallas_call | solution.py:596
  239.6 2.2 fusion.7
  242.1 3.3 collective-permute-start.39
  245.9 1.6 fusion.3
  248.9 1.4 add.124
  250.3 2.1 collective-permute-start.42
  254.9 4.2 %collective-permute-done.39 = bf16[400,768]{1,0:T(8,128)(2,1)S(1)} collective-permute-done((bf16[400,768]{1,0:T(8,128)(2,1)S(1)}, bf16[400,768]{1,0:T(8,128)(2,1)S(1)}, u32[]{:S(2)}, u32[]{:S(2)}) %collective-permute-start.39) | collective-permute-done | bytes 614432 | tf_op jit(solution)/shard_map/ppermute | solution.py:932
  259.4 2.1 collective-permute-start.44
  264.2 3.2 collective-permute-start.47
  267.4 4.5 %collective-permute-done.42 = bf16[384,768]{1,0:T(8,128)(2,1)} collective-permute-done((bf16[384,768]{1,0:T(8,128)(2,1)S(1)}, bf16[384,768]{1,0:T(8,128)(2,1)}, u32[]{:S(2)}, u32[]{:S(2)}) %collective-permute-start.42) | collective-permute-done | bytes 589856 | tf_op jit(solution)/shard_map/ppermute | solution.py:932
  273.4 2.6 collective-permute-start.43
  276.0 1.4 fusion.4
  279.2 3.3 collective-permute-start.50
  286.1 3.1 collective-permute-start.49
  290.7 6.2 %collective-permute-done.50 = bf16[400,768]{1,0:T(8,128)(2,1)S(1)} collective-permute-done((bf16[400,768]{1,0:T(8,128)(2,1)S(1)}, bf16[400,768]{1,0:T(8,128)(2,1)S(1)}, u32[]{:S(2)}, u32[]{:S(2)}) %collective-permute-start.50) | collective-permute-done | bytes 614432 | tf_op jit(solution)/shard_map/ppermute | solution.py:932
  297.2 3.2 collective-permute-start.54
  300.4 1.3 collective-permute-start.53
  302.2 6.7 %collective-permute-done.52 = bf16[784,384]{1,0:T(8,128)(2,1)S(1)} collective-permute-done((bf16[784,384]{1,0:T(8,128)(2,1)S(1)}, bf16[784,384]{1,0:T(8,128)(2,1)S(1)}, u32[]{:S(2)}, u32[]{:S(2)}) %collective-permute-start.52) | collective-permute-done | bytes 602144 | tf_op jit(solution)/shard_map/ppermute | solution.py:932
  309.0 2.1 collective-permute-start.55
  314.4 1.4 collective-permute-start.68
  315.8 10.8 %collective-permute-done.67.refs_14_ = bf16[384,768]{1,0:T(8,128)(2,1)S(1)} collective-permute-done((bf16[384,768]{1,0:T(8,128)(2,1)S(1)}, bf16[384,768]{1,0:T(8,128)(2,1)S(1)}, u32[]{:S(2)}, u32[]{:S(2)}) %collective-permute-start.67) | collective-permute-done | bytes 589856 | tf_op jit(solution)/shard_map/ppermute | solution.py:657
  332.0 7.5 %collective-permute-start.59 = (bf16[400,768]{1,0:T(8,128)(2,1)S(1)}, bf16[400,768]{1,0:T(8,128)(2,1)}, u32[]{:S(2)}, u32[]{:S(2)}) collective-permute-start(bf16[400,768]{1,0:T(8,128)(2,1)S(1)} %broadcast_select_fusion.refs_1_), channel_id=1, source_target_pairs={{16,0},{17,1},{18,2},{19,3},{20,4},{21,5},{22,6},{23,7},{24,8},{25... | collective-permute-start | bytes 1843208 | tf_op jit(solution)/shard_map/ppermute | solution.py:936
  340.7 12.5 %collective-permute-start.60 = (bf16[400,768]{1,0:T(8,128)(2,1)}, bf16[400,768]{1,0:T(8,128)(2,1)}, u32[]{:S(2)}, u32[]{:S(2)}) collective-permute-start(bf16[400,768]{1,0:T(8,128)(2,1)} %collective-permute-done.58.refs_2_), channel_id=1, source_target_pairs={{16,0},{17,1},{18,2},{19,3},{20,4},{21,5},{22,6},{23,7},{24,8},{25... | collective-permute-start | bytes 1843208 | tf_op jit(solution)/shard_map/ppermute | solution.py:936
  353.3 2.1 collective-permute-start.56
  355.4 2.1 collective-permute-start.62
  357.5 3.7 collective-permute-start.63
  363.9 7.3 %shard_map.304 = (f32[1536,768]{1,0:T(8,128)}, f32[768,1536]{1,0:T(8,128)}, f32[1,768]{1,0:T(1,128)}, f32[1,768]{1,0:T(1,128)}, f32[1,768]{1,0:T(1,128)}, /*index=5*/f32[1,1536]{1,0:T(1,128)}) custom-call(s32[7]{0:T(128)} %pad_add_fusion.refs_0_, bf16[400,768]{1,0:T(8,128)(2,1)} %copy-done.6, bf16[400,768]{1,0:T(8,128)(2,1)} %collective-permute-done.58.refs_2_, ...), custom_call_target="tpu_custom_call" | custom-call | tf_op jit(solution)/shard_map/pallas_call | solution.py:596
  373.2 3.7 collective-permute-start.33
  379.5 5.4 %collective-permute-start.71 = (bf16[784,384]{1,0:T(8,128)(2,1)S(1)}, bf16[784,384]{1,0:T(8,128)(2,1)S(1)}, u32[]{:S(2)}, u32[]{:S(2)}) collective-permute-start(bf16[784,384]{1,0:T(8,128)(2,1)S(1)} %broadcast_select_fusion.2.refs_1_), channel_id=1, source_target_pairs={{16,0},{17,1},{18,2},{19,3},{20,4},{21,5},{22,6},{23,7},{24,8},{25... | collective-permute-start | bytes 1806344 | tf_op jit(solution)/shard_map/ppermute | solution.py:936
  384.9 5.3 %collective-permute-done.70.refs_2_ = bf16[784,384]{1,0:T(8,128)(2,1)S(1)} collective-permute-done((bf16[784,384]{1,0:T(8,128)(2,1)S(1)}, bf16[784,384]{1,0:T(8,128)(2,1)S(1)}, u32[]{:S(2)}, u32[]{:S(2)}) %collective-permute-start.70) | collective-permute-done | bytes 602144 | tf_op jit(solution)/shard_map/ppermute | solution.py:657
  390.2 4.3 %collective-permute-start.72 = (bf16[784,384]{1,0:T(8,128)(2,1)S(1)}, bf16[784,384]{1,0:T(8,128)(2,1)S(1)}, u32[]{:S(2)}, u32[]{:S(2)}) collective-permute-start(bf16[784,384]{1,0:T(8,128)(2,1)S(1)} %collective-permute-done.70.refs_2_), channel_id=1, source_target_pairs={{16,0},{17,1},{18,2},{19,3},{20,4},{21,5},{22,6},{23,7},{24,8},{25... | collective-permute-start | bytes 1806344 | tf_op jit(solution)/shard_map/ppermute | solution.py:936
  397.7 4.6 %shard_map.305 = (f32[768,384]{1,0:T(8,128)}, f32[768,384]{1,0:T(8,128)}, f32[768,384]{1,0:T(8,128)}, f32[384,768]{1,0:T(8,128)}, f32[1,768]{1,0:T(1,128)}, /*in...) custom-call(s32[7]{0:T(128)} %pad_add_fusion.refs_0_, bf16[784,384]{1,0:T(8,128)(2,1)} %copy-done.10, ...), custom_call_target="tpu_custom_call" | custom-call | tf_op jit(solution)/shard_map/pallas_call | solution.py:596
  (287 shorter events, 76.1 us)
Async XLA Ops:
  0.8 15.7 %collective-permute-start = (bf16[768,1536]{1,0:T(8,128)(2,1)}, bf16[768,1536]{1,0:T(8,128)(2,1)S(1)}, u32[]{:S(2)}, u32[]{:S(2)}) collective-permute-start(bf16[768,1536]{1,0:T(8,128)(2,1)} %bitcast.27), channel_id=1, source_target_pairs={{0,16},{16,0},{1,17},{17,1},{2,18},{18,2},{3,19},{19,3},{4,20},{20... | collective-permute-start | bytes 7077896 | tf_op jit(solution)/shard_map/ppermute | solution.py:643
  1.5 15.5 %collective-permute-start.1 = (bf16[1536,768]{1,0:T(8,128)(2,1)}, bf16[1536,768]{1,0:T(8,128)(2,1)}, u32[]{:S(2)}, u32[]{:S(2)}) collective-permute-start(bf16[1536,768]{1,0:T(8,128)(2,1)} %bitcast.36), channel_id=1, source_target_pairs={{0,16},{16,0},{1,17},{17,1},{2,18},{18,2},{3,19},{19,3},{4,20},{20... | collective-permute-start | bytes 7077896 | tf_op jit(solution)/shard_map/ppermute | solution.py:643
  4.2 12.3 %collective-permute-start.4 = (bf16[256,768]{1,0:T(8,128)(2,1)S(1)}, bf16[256,768]{1,0:T(8,128)(2,1)}, u32[]{:S(2)}, u32[]{:S(2)}) collective-permute-start(bf16[256,768]{1,0:T(8,128)(2,1)S(1)} %get-tuple-element.174.refs_5_), channel_id=1, source_target_pairs={{0,17},{1,16},{2,19},{3,18},{4,21},{5,20},{6,23},{7,22},{8,25},{9,... | collective-permute-start | bytes 1179656 | tf_op jit(solution)/shard_map/ppermute | solution.py:647
  9.9 10.9 %collective-permute-start.6 = (bf16[768,384]{1,0:T(8,128)(2,1)}, bf16[768,384]{1,0:T(8,128)(2,1)}, u32[]{:S(2)}, u32[]{:S(2)}) collective-permute-start(bf16[768,384]{1,0:T(8,128)(2,1)} %bitcast.51), channel_id=1, source_target_pairs={{0,16},{16,0},{1,17},{17,1},{2,18},{18,2},{3,19},{19,3},{4,20},{20... | collective-permute-start | bytes 1769480 | tf_op jit(solution)/shard_map/ppermute | solution.py:643
  10.2 10.6 %collective-permute-start.7 = (bf16[768,384]{1,0:T(8,128)(2,1)}, bf16[768,384]{1,0:T(8,128)(2,1)}, u32[]{:S(2)}, u32[]{:S(2)}) collective-permute-start(bf16[768,384]{1,0:T(8,128)(2,1)} %bitcast.56), channel_id=1, source_target_pairs={{0,16},{16,0},{1,17},{17,1},{2,18},{18,2},{3,19},{19,3},{4,20},{20... | collective-permute-start | bytes 1769480 | tf_op jit(solution)/shard_map/ppermute | solution.py:643
  33.6 10.2 %collective-permute-start.11 = (bf16[256,768]{1,0:T(8,128)(2,1)}, bf16[256,768]{1,0:T(8,128)(2,1)S(1)}, u32[]{:S(2)}, u32[]{:S(2)}) collective-permute-start(bf16[256,768]{1,0:T(8,128)(2,1)} %get-tuple-element.167.refs_2_), channel_id=1, source_target_pairs={{0,1},{1,0},{2,3},{3,2},{4,5},{5,4},{6,7},{7,6},{8,9},{9,8},{10,11... | collective-permute-start | bytes 1179656 | tf_op jit(solution)/shard_map/ppermute | solution.py:643
  34.9 17.3 %collective-permute-start.10 = (bf16[256,768]{1,0:T(8,128)(2,1)}, bf16[256,768]{1,0:T(8,128)(2,1)S(1)}, u32[]{:S(2)}, u32[]{:S(2)}) collective-permute-start(bf16[256,768]{1,0:T(8,128)(2,1)} %get-tuple-element.166.refs_2_), channel_id=1, source_target_pairs={{0,1},{1,0},{2,3},{3,2},{4,5},{5,4},{6,7},{7,6},{8,9},{9,8},{10,11... | collective-permute-start | bytes 1179656 | tf_op jit(solution)/shard_map/ppermute | solution.py:643
  58.9 10.4 %collective-permute-start.16 = (bf16[256,768]{1,0:T(8,128)(2,1)}, bf16[256,768]{1,0:T(8,128)(2,1)S(1)}, u32[]{:S(2)}, u32[]{:S(2)}) collective-permute-start(bf16[256,768]{1,0:T(8,128)(2,1)} %get-tuple-element.179.refs_3_), channel_id=1, source_target_pairs={{0,1},{1,0},{2,3},{3,2},{4,5},{5,4},{6,7},{7,6},{8,9},{9,8},{10,11... | collective-permute-start | bytes 1179656 | tf_op jit(solution)/shard_map/ppermute | solution.py:643
  60.2 16.4 %collective-permute-start.15 = (bf16[256,768]{1,0:T(8,128)(2,1)S(1)}, bf16[256,768]{1,0:T(8,128)(2,1)S(1)}, u32[]{:S(2)}, u32[]{:S(2)}) collective-permute-start(bf16[256,768]{1,0:T(8,128)(2,1)S(1)} %copy-done.60), channel_id=1, source_target_pairs={{0,1},{1,0},{2,3},{3,2},{4,5},{5,4},{6,7},{7,6},{8,9},{9,8},{10,11... | collective-permute-start | bytes 1179656 | tf_op jit(solution)/shard_map/ppermute | solution.py:643
  60.5 32.2 %collective-permute-start.14 = (bf16[256,768]{1,0:T(8,128)(2,1)S(1)}, bf16[256,768]{1,0:T(8,128)(2,1)S(1)}, u32[]{:S(2)}, u32[]{:S(2)}) collective-permute-start(bf16[256,768]{1,0:T(8,128)(2,1)S(1)} %copy-done.40), channel_id=1, source_target_pairs={{16,0},{17,1},{18,2},{19,3},{20,4},{21,5},{22,6},{23,7},{24,8},{25... | collective-permute-start | bytes 1179656 | tf_op jit(solution)/shard_map/ppermute | solution.py:647
  64.6 28.1 %collective-permute-start.13 = (bf16[256,768]{1,0:T(8,128)(2,1)S(1)}, bf16[256,768]{1,0:T(8,128)(2,1)S(1)}, u32[]{:S(2)}, u32[]{:S(2)}) collective-permute-start(bf16[256,768]{1,0:T(8,128)(2,1)S(1)} %copy-done.40), channel_id=1, source_target_pairs={{16,1},{17,0},{18,3},{19,2},{20,5},{21,4},{22,7},{23,6},{24,9},{25... | collective-permute-start | bytes 1179656 | tf_op jit(solution)/shard_map/ppermute | solution.py:647
  67.0 25.6 %collective-permute-start.12 = (bf16[256,768]{1,0:T(8,128)(2,1)S(1)}, bf16[256,768]{1,0:T(8,128)(2,1)S(1)}, u32[]{:S(2)}, u32[]{:S(2)}) collective-permute-start(bf16[256,768]{1,0:T(8,128)(2,1)S(1)} %get-tuple-element.174.refs_5_), channel_id=1, source_target_pairs={{16,17},{17,16},{18,19},{19,18},{20,21},{21,20},{22,23},{23,22},{2... | collective-permute-start | bytes 1179656 | tf_op jit(solution)/shard_map/ppermute | solution.py:647
  92.4 13.6 %collective-permute-start.17 = (bf16[256,768]{1,0:T(8,128)(2,1)}, bf16[256,768]{1,0:T(8,128)(2,1)S(1)}, u32[]{:S(2)}, u32[]{:S(2)}) collective-permute-start(bf16[256,768]{1,0:T(8,128)(2,1)} %get-tuple-element.181.refs_2_), channel_id=1, source_target_pairs={{0,1},{1,0},{2,3},{3,2},{4,5},{5,4},{6,7},{7,6},{8,9},{9,8},{10,11... | collective-permute-start | bytes 1179656 | tf_op jit(solution)/shard_map/ppermute | solution.py:643
  104.7 10.2 %collective-permute-start.19 = (bf16[256,768]{1,0:T(8,128)(2,1)}, bf16[256,768]{1,0:T(8,128)(2,1)S(1)}, u32[]{:S(2)}, u32[]{:S(2)}) collective-permute-start(bf16[256,768]{1,0:T(8,128)(2,1)} %get-tuple-element.189.refs_2_), channel_id=1, source_target_pairs={{0,1},{1,0},{2,3},{3,2},{4,5},{5,4},{6,7},{7,6},{8,9},{9,8},{10,11... | collective-permute-start | bytes 1179656 | tf_op jit(solution)/shard_map/ppermute | solution.py:643
  112.7 10.4 %collective-permute-start.20 = (bf16[256,768]{1,0:T(8,128)(2,1)}, bf16[256,768]{1,0:T(8,128)(2,1)S(1)}, u32[]{:S(2)}, u32[]{:S(2)}) collective-permute-start(bf16[256,768]{1,0:T(8,128)(2,1)} %get-tuple-element.193.refs_2_), channel_id=1, source_target_pairs={{0,1},{1,0},{2,3},{3,2},{4,5},{5,4},{6,7},{7,6},{8,9},{9,8},{10,11... | collective-permute-start | bytes 1179656 | tf_op jit(solution)/shard_map/ppermute | solution.py:643
  131.3 19.7 %collective-permute-start.22 = (bf16[256,768]{1,0:T(8,128)(2,1)}, bf16[256,768]{1,0:T(8,128)(2,1)S(1)}, u32[]{:S(2)}, u32[]{:S(2)}) collective-permute-start(bf16[256,768]{1,0:T(8,128)(2,1)} %get-tuple-element.208.refs_3_), channel_id=1, source_target_pairs={{0,1},{1,0},{2,3},{3,2},{4,5},{5,4},{6,7},{7,6},{8,9},{9,8},{10,11... | collective-permute-start | bytes 1179656 | tf_op jit(solution)/shard_map/ppermute | solution.py:643
  132.6 18.4 %collective-permute-start.21 = (bf16[256,768]{1,0:T(8,128)(2,1)S(1)}, bf16[256,768]{1,0:T(8,128)(2,1)S(1)}, u32[]{:S(2)}, u32[]{:S(2)}) collective-permute-start(bf16[256,768]{1,0:T(8,128)(2,1)S(1)} %copy-done.58), channel_id=1, source_target_pairs={{0,1},{1,0},{2,3},{3,2},{4,5},{5,4},{6,7},{7,6},{8,9},{9,8},{10,11... | collective-permute-start | bytes 1179656 | tf_op jit(solution)/shard_map/ppermute | solution.py:643
  140.6 36.8 %collective-permute-start.24 = (bf16[1568,768]{1,0:T(8,128)(2,1)}, bf16[1568,768]{1,0:T(8,128)(2,1)S(1)}, u32[]{:S(2)}, u32[]{:S(2)}) collective-permute-start(bf16[1568,768]{1,0:T(8,128)(2,1)} %get-tuple-element.225), channel_id=1, source_target_pairs={{0,16},{16,0},{1,17},{17,1},{2,18},{18,2},{3,19},{19,3},{4,20},{20... | collective-permute-start | bytes 7225352 | tf_op jit(solution)/shard_map/ppermute | solution.py:643
  177.8 15.1 %collective-permute-start.26 = (bf16[384,768]{1,0:T(8,128)(2,1)S(1)}, bf16[384,768]{1,0:T(8,128)(2,1)S(1)}, u32[]{:S(2)}, u32[]{:S(2)}) collective-permute-start(bf16[384,768]{1,0:T(8,128)(2,1)S(1)} %slice_add_fusion.10), channel_id=1, source_target_pairs={{0,2},{2,0},{4,6},{6,4},{8,10},{10,8},{12,14},{14,12},{1,3},{3,1},... | collective-permute-start | bytes 1769480 | tf_op jit(solution)/shard_map/ppermute | solution.py:657
  178.8 16.3 %collective-permute-start.27 = (bf16[256,768]{1,0:T(8,128)(2,1)S(1)}, bf16[256,768]{1,0:T(8,128)(2,1)S(1)}, u32[]{:S(2)}, u32[]{:S(2)}) collective-permute-start(bf16[256,768]{1,0:T(8,128)(2,1)S(1)} %copy-done.41), channel_id=1, source_target_pairs={{0,1},{1,0},{2,3},{3,2},{4,5},{5,4},{6,7},{7,6},{8,9},{9,8},{10,11... | collective-permute-start | bytes 1179656 | tf_op jit(solution)/shard_map/ppermute | solution.py:643
  179.8 33.0 %collective-permute-start.28 = (bf16[400,768]{1,0:T(8,128)(2,1)S(1)}, bf16[400,768]{1,0:T(8,128)(2,1)}, u32[]{:S(2)}, u32[]{:S(2)}) collective-permute-start(bf16[400,768]{1,0:T(8,128)(2,1)S(1)} %slice_add_fusion.3), channel_id=1, source_target_pairs={{0,2},{2,0},{4,6},{6,4},{8,10},{10,8},{12,14},{14,12},{1,3},{3,1},... | collective-permute-start | bytes 1843208 | tf_op jit(solution)/shard_map/ppermute | solution.py:657
  180.5 65.4 %collective-permute-start.36 = (bf16[784,384]{1,0:T(8,128)(2,1)}, bf16[784,384]{1,0:T(8,128)(2,1)}, u32[]{:S(2)}, u32[]{:S(2)}) collective-permute-start(bf16[784,384]{1,0:T(8,128)(2,1)} %slice_add_fusion.7), channel_id=1, source_target_pairs={{0,2},{2,0},{4,6},{6,4},{8,10},{10,8},{12,14},{14,12},{1,3},{3,1},... | collective-permute-start | bytes 1806344 | tf_op jit(solution)/shard_map/ppermute | solution.py:657
  191.8 25.8 %collective-permute-start.29 = (bf16[256,768]{1,0:T(8,128)(2,1)}, bf16[256,768]{1,0:T(8,128)(2,1)}, u32[]{:S(2)}, u32[]{:S(2)}) collective-permute-start(bf16[256,768]{1,0:T(8,128)(2,1)} %get-tuple-element.249.refs_2_), channel_id=1, source_target_pairs={{0,1},{1,0},{2,3},{3,2},{4,5},{5,4},{6,7},{7,6},{8,9},{9,8},{10,11... | collective-permute-start | bytes 1179656 | tf_op jit(solution)/shard_map/ppermute | solution.py:643
  193.7 55.1 %collective-permute-start.37 = (bf16[384,768]{1,0:T(8,128)(2,1)}, bf16[384,768]{1,0:T(8,128)(2,1)}, u32[]{:S(2)}, u32[]{:S(2)}) collective-permute-start(bf16[384,768]{1,0:T(8,128)(2,1)} %fusion.5), channel_id=1, source_target_pairs={{0,4},{2,6},{12,8},{14,10},{1,5},{3,7},{13,9},{15,11},{16,20},{18,... | collective-permute-start | bytes 1769480 | tf_op jit(solution)/shard_map/ppermute | solution.py:932
  203.0 15.9 %collective-permute-start.30 = (bf16[256,768]{1,0:T(8,128)(2,1)}, bf16[256,768]{1,0:T(8,128)(2,1)S(1)}, u32[]{:S(2)}, u32[]{:S(2)}) collective-permute-start(bf16[256,768]{1,0:T(8,128)(2,1)} %get-tuple-element.250.refs_3_), channel_id=1, source_target_pairs={{0,1},{1,0},{2,3},{3,2},{4,5},{5,4},{6,7},{7,6},{8,9},{9,8},{10,11... | collective-permute-start | bytes 1179656 | tf_op jit(solution)/shard_map/ppermute | solution.py:643
  212.8 32.6 %collective-permute-start.35 = (bf16[1568,768]{1,0:T(8,128)(2,1)}, bf16[1568,768]{1,0:T(8,128)(2,1)S(1)}, u32[]{:S(2)}, u32[]{:S(2)}) collective-permute-start(bf16[1568,768]{1,0:T(8,128)(2,1)} %get-tuple-element.270), channel_id=1, source_target_pairs={{0,16},{16,0},{1,17},{17,1},{2,18},{18,2},{3,19},{19,3},{4,20},{20... | collective-permute-start | bytes 7225352 | tf_op jit(solution)/shard_map/ppermute | solution.py:643
  217.6 24.4 %collective-permute-start.34 = (bf16[400,768]{1,0:T(8,128)(2,1)S(1)}, bf16[400,768]{1,0:T(8,128)(2,1)S(1)}, u32[]{:S(2)}, u32[]{:S(2)}) collective-permute-start(bf16[400,768]{1,0:T(8,128)(2,1)S(1)} %fusion.1), channel_id=1, source_target_pairs={{0,4},{2,6},{12,8},{14,10},{1,5},{3,7},{13,9},{15,11},{16,20},{18,... | collective-permute-start | bytes 1843208 | tf_op jit(solution)/shard_map/ppermute | solution.py:932
  239.5 13.7 %collective-permute-start.38 = (bf16[1568,384]{1,0:T(8,128)(2,1)}, bf16[1568,384]{1,0:T(8,128)(2,1)S(1)}, u32[]{:S(2)}, u32[]{:S(2)}) collective-permute-start(bf16[1568,384]{1,0:T(8,128)(2,1)} %get-tuple-element.274), channel_id=1, source_target_pairs={{0,16},{16,0},{1,17},{17,1},{2,18},{18,2},{3,19},{19,3},{4,20},{20... | collective-permute-start | bytes 3612680 | tf_op jit(solution)/shard_map/ppermute | solution.py:643
  242.1 17.0 %collective-permute-start.39 = (bf16[400,768]{1,0:T(8,128)(2,1)S(1)}, bf16[400,768]{1,0:T(8,128)(2,1)S(1)}, u32[]{:S(2)}, u32[]{:S(2)}) collective-permute-start(bf16[400,768]{1,0:T(8,128)(2,1)S(1)} %add.120), channel_id=1, source_target_pairs={{4,8},{6,10},{8,4},{10,6},{5,9},{7,11},{9,5},{11,7},{20,24},{22,26... | collective-permute-start | bytes 1843208 | tf_op jit(solution)/shard_map/ppermute | solution.py:932
  245.6 15.9 %collective-permute-start.40 = (bf16[400,768]{1,0:T(8,128)(2,1)S(1)}, bf16[400,768]{1,0:T(8,128)(2,1)S(1)}, u32[]{:S(2)}, u32[]{:S(2)}) collective-permute-start(bf16[400,768]{1,0:T(8,128)(2,1)S(1)} %slice_add_fusion.1), channel_id=1, source_target_pairs={{0,2},{2,0},{4,6},{6,4},{8,10},{10,8},{12,14},{14,12},{1,3},{3,1},... | collective-permute-start | bytes 1843208 | tf_op jit(solution)/shard_map/ppermute | solution.py:657
  247.6 16.5 %collective-permute-start.41 = (bf16[784,384]{1,0:T(8,128)(2,1)S(1)}, bf16[784,384]{1,0:T(8,128)(2,1)S(1)}, u32[]{:S(2)}, u32[]{:S(2)}) collective-permute-start(bf16[784,384]{1,0:T(8,128)(2,1)S(1)} %fusion.3), channel_id=1, source_target_pairs={{0,4},{2,6},{12,8},{14,10},{1,5},{3,7},{13,9},{15,11},{16,20},{18,... | collective-permute-start | bytes 1806344 | tf_op jit(solution)/shard_map/ppermute | solution.py:932
  250.3 21.7 %collective-permute-start.42 = (bf16[384,768]{1,0:T(8,128)(2,1)S(1)}, bf16[384,768]{1,0:T(8,128)(2,1)}, u32[]{:S(2)}, u32[]{:S(2)}) collective-permute-start(bf16[384,768]{1,0:T(8,128)(2,1)S(1)} %add.124), channel_id=1, source_target_pairs={{4,8},{6,10},{8,4},{10,6},{5,9},{7,11},{9,5},{11,7},{20,24},{22,26... | collective-permute-start | bytes 1769480 | tf_op jit(solution)/shard_map/ppermute | solution.py:932
  253.2 20.2 %collective-permute-start.45 = (bf16[384,768]{1,0:T(8,128)(2,1)}, bf16[384,768]{1,0:T(8,128)(2,1)}, u32[]{:S(2)}, u32[]{:S(2)}) collective-permute-start(bf16[384,768]{1,0:T(8,128)(2,1)} %slice_add_fusion.8), channel_id=1, source_target_pairs={{0,2},{2,0},{4,6},{6,4},{8,10},{10,8},{12,14},{14,12},{1,3},{3,1},... | collective-permute-start | bytes 1769480 | tf_op jit(solution)/shard_map/ppermute | solution.py:657
  259.4 18.1 %collective-permute-start.44 = (bf16[400,768]{1,0:T(8,128)(2,1)S(1)}, bf16[400,768]{1,0:T(8,128)(2,1)}, u32[]{:S(2)}, u32[]{:S(2)}) collective-permute-start(bf16[400,768]{1,0:T(8,128)(2,1)S(1)} %add.126), channel_id=1, source_target_pairs={{4,0},{6,2},{8,12},{10,14},{5,1},{7,3},{9,13},{11,15},{20,16},{22,... | collective-permute-start | bytes 1843208 | tf_op jit(solution)/shard_map/ppermute | solution.py:932
  262.7 15.2 %collective-permute-start.46 = (bf16[400,768]{1,0:T(8,128)(2,1)S(1)}, bf16[400,768]{1,0:T(8,128)(2,1)}, u32[]{:S(2)}, u32[]{:S(2)}) collective-permute-start(bf16[400,768]{1,0:T(8,128)(2,1)S(1)} %fusion), channel_id=1, source_target_pairs={{0,4},{2,6},{12,8},{14,10},{1,5},{3,7},{13,9},{15,11},{16,20},{18,... | collective-permute-start | bytes 1843208 | tf_op jit(solution)/shard_map/ppermute | solution.py:932
  264.2 20.6 %collective-permute-start.47 = (bf16[784,384]{1,0:T(8,128)(2,1)S(1)}, bf16[784,384]{1,0:T(8,128)(2,1)}, u32[]{:S(2)}, u32[]{:S(2)}) collective-permute-start(bf16[784,384]{1,0:T(8,128)(2,1)S(1)} %add.129), channel_id=1, source_target_pairs={{4,8},{6,10},{8,4},{10,6},{5,9},{7,11},{9,5},{11,7},{20,24},{22,26... | collective-permute-start | bytes 1806344 | tf_op jit(solution)/shard_map/ppermute | solution.py:932
  271.9 17.3 %collective-permute-start.48 = (bf16[784,384]{1,0:T(8,128)(2,1)}, bf16[784,384]{1,0:T(8,128)(2,1)S(1)}, u32[]{:S(2)}, u32[]{:S(2)}) collective-permute-start(bf16[784,384]{1,0:T(8,128)(2,1)} %slice_add_fusion.5), channel_id=1, source_target_pairs={{0,2},{2,0},{4,6},{6,4},{8,10},{10,8},{12,14},{14,12},{1,3},{3,1},... | collective-permute-start | bytes 1806344 | tf_op jit(solution)/shard_map/ppermute | solution.py:657
  273.4 15.7 %collective-permute-start.43 = (bf16[384,768]{1,0:T(8,128)(2,1)S(1)}, bf16[384,768]{1,0:T(8,128)(2,1)S(1)}, u32[]{:S(2)}, u32[]{:S(2)}) collective-permute-start(bf16[384,768]{1,0:T(8,128)(2,1)S(1)} %add.130), channel_id=1, source_target_pairs={{4,0},{6,2},{8,12},{10,14},{5,1},{7,3},{9,13},{11,15},{20,16},{22,... | collective-permute-start | bytes 1769480 | tf_op jit(solution)/shard_map/ppermute | solution.py:932
  279.2 17.7 %collective-permute-start.50 = (bf16[400,768]{1,0:T(8,128)(2,1)S(1)}, bf16[400,768]{1,0:T(8,128)(2,1)S(1)}, u32[]{:S(2)}, u32[]{:S(2)}) collective-permute-start(bf16[400,768]{1,0:T(8,128)(2,1)S(1)} %add.134), channel_id=1, source_target_pairs={{4,8},{6,10},{8,4},{10,6},{5,9},{7,11},{9,5},{11,7},{20,24},{22,26... | collective-permute-start | bytes 1843208 | tf_op jit(solution)/shard_map/ppermute | solution.py:932
  282.5 14.5 %collective-permute-start.51 = (bf16[384,768]{1,0:T(8,128)(2,1)S(1)}, bf16[384,768]{1,0:T(8,128)(2,1)S(1)}, u32[]{:S(2)}, u32[]{:S(2)}) collective-permute-start(bf16[384,768]{1,0:T(8,128)(2,1)S(1)} %fusion.4), channel_id=1, source_target_pairs={{0,4},{2,6},{12,8},{14,10},{1,5},{3,7},{13,9},{15,11},{16,20},{18,... | collective-permute-start | bytes 1769480 | tf_op jit(solution)/shard_map/ppermute | solution.py:932
  286.1 16.0 %collective-permute-start.49 = (bf16[784,384]{1,0:T(8,128)(2,1)S(1)}, bf16[784,384]{1,0:T(8,128)(2,1)S(1)}, u32[]{:S(2)}, u32[]{:S(2)}) collective-permute-start(bf16[784,384]{1,0:T(8,128)(2,1)S(1)} %add.135), channel_id=1, source_target_pairs={{4,0},{6,2},{8,12},{10,14},{5,1},{7,3},{9,13},{11,15},{20,16},{22,... | collective-permute-start | bytes 1806344 | tf_op jit(solution)/shard_map/ppermute | solution.py:932
  289.4 19.5 %collective-permute-start.52 = (bf16[784,384]{1,0:T(8,128)(2,1)S(1)}, bf16[784,384]{1,0:T(8,128)(2,1)S(1)}, u32[]{:S(2)}, u32[]{:S(2)}) collective-permute-start(bf16[784,384]{1,0:T(8,128)(2,1)S(1)} %fusion.2), channel_id=1, source_target_pairs={{0,4},{2,6},{12,8},{14,10},{1,5},{3,7},{13,9},{15,11},{16,20},{18,... | collective-permute-start | bytes 1806344 | tf_op jit(solution)/shard_map/ppermute | solution.py:932
  297.2 14.3 %collective-permute-start.54 = (bf16[384,768]{1,0:T(8,128)(2,1)S(1)}, bf16[384,768]{1,0:T(8,128)(2,1)S(1)}, u32[]{:S(2)}, u32[]{:S(2)}) collective-permute-start(bf16[384,768]{1,0:T(8,128)(2,1)S(1)} %add.139), channel_id=1, source_target_pairs={{4,8},{6,10},{8,4},{10,6},{5,9},{7,11},{9,5},{11,7},{20,24},{22,26... | collective-permute-start | bytes 1769480 | tf_op jit(solution)/shard_map/ppermute | solution.py:932
  300.4 12.6 %collective-permute-start.53 = (bf16[400,768]{1,0:T(8,128)(2,1)S(1)}, bf16[400,768]{1,0:T(8,128)(2,1)S(1)}, u32[]{:S(2)}, u32[]{:S(2)}) collective-permute-start(bf16[400,768]{1,0:T(8,128)(2,1)S(1)} %add.138), channel_id=1, source_target_pairs={{4,0},{6,2},{8,12},{10,14},{5,1},{7,3},{9,13},{11,15},{20,16},{22,... | collective-permute-start | bytes 1843208 | tf_op jit(solution)/shard_map/ppermute | solution.py:932
  301.7 12.6 %collective-permute-start.64 = (bf16[400,768]{1,0:T(8,128)(2,1)S(1)}, bf16[400,768]{1,0:T(8,128)(2,1)S(1)}, u32[]{:S(2)}, u32[]{:S(2)}) collective-permute-start(bf16[400,768]{1,0:T(8,128)(2,1)S(1)} %broadcast_select_fusion.1.refs_9_), channel_id=1, source_target_pairs={{0,2},{2,0},{4,6},{6,4},{8,10},{10,8},{12,14},{14,12},{1,3},{3,1},... | collective-permute-start | bytes 1843208 | tf_op jit(solution)/shard_map/ppermute | solution.py:657
  309.0 18.9 %collective-permute-start.55 = (bf16[784,384]{1,0:T(8,128)(2,1)S(1)}, bf16[784,384]{1,0:T(8,128)(2,1)S(1)}, u32[]{:S(2)}, u32[]{:S(2)}) collective-permute-start(bf16[784,384]{1,0:T(8,128)(2,1)S(1)} %add.140), channel_id=1, source_target_pairs={{4,8},{6,10},{8,4},{10,6},{5,9},{7,11},{9,5},{11,7},{20,24},{22,26... | collective-permute-start | bytes 1806344 | tf_op jit(solution)/shard_map/ppermute | solution.py:932
  311.1 15.5 %collective-permute-start.67 = (bf16[384,768]{1,0:T(8,128)(2,1)S(1)}, bf16[384,768]{1,0:T(8,128)(2,1)S(1)}, u32[]{:S(2)}, u32[]{:S(2)}) collective-permute-start(bf16[384,768]{1,0:T(8,128)(2,1)S(1)} %broadcast_select_fusion.5.refs_13_), channel_id=1, source_target_pairs={{0,2},{2,0},{4,6},{6,4},{8,10},{10,8},{12,14},{14,12},{1,3},{3,1},... | collective-permute-start | bytes 1769480 | tf_op jit(solution)/shard_map/ppermute | solution.py:657
  311.6 17.8 %collective-permute-start.57 = (bf16[384,768]{1,0:T(8,128)(2,1)S(1)}, bf16[384,768]{1,0:T(8,128)(2,1)S(1)}, u32[]{:S(2)}, u32[]{:S(2)}) collective-permute-start(bf16[384,768]{1,0:T(8,128)(2,1)S(1)} %add.141), channel_id=1, source_target_pairs={{4,0},{6,2},{8,12},{10,14},{5,1},{7,3},{9,13},{11,15},{20,16},{22,... | collective-permute-start | bytes 1769480 | tf_op jit(solution)/shard_map/ppermute | solution.py:932
  313.0 17.7 %collective-permute-start.65 = (bf16[400,768]{1,0:T(8,128)(2,1)S(1)}, bf16[400,768]{1,0:T(8,128)(2,1)S(1)}, u32[]{:S(2)}, u32[]{:S(2)}) collective-permute-start(bf16[400,768]{1,0:T(8,128)(2,1)S(1)} %broadcast_select_fusion.1.refs_9_), channel_id=1, source_target_pairs={{0,16},{1,17},{2,18},{3,19},{4,20},{5,21},{6,22},{7,23},{8,24},{9,... | collective-permute-start | bytes 1843208 | tf_op jit(solution)/shard_map/ppermute | solution.py:936
  314.4 17.5 %collective-permute-start.68 = (bf16[384,768]{1,0:T(8,128)(2,1)S(1)}, bf16[384,768]{1,0:T(8,128)(2,1)S(1)}, u32[]{:S(2)}, u32[]{:S(2)}) collective-permute-start(bf16[384,768]{1,0:T(8,128)(2,1)S(1)} %broadcast_select_fusion.5.refs_13_), channel_id=1, source_target_pairs={{0,16},{1,17},{2,18},{3,19},{4,20},{5,21},{6,22},{7,23},{8,24},{9,... | collective-permute-start | bytes 1769480 | tf_op jit(solution)/shard_map/ppermute | solution.py:936
  326.6 26.7 %collective-permute-start.66 = (bf16[400,768]{1,0:T(8,128)(2,1)S(1)}, bf16[400,768]{1,0:T(8,128)(2,1)S(1)}, u32[]{:S(2)}, u32[]{:S(2)}) collective-permute-start(bf16[400,768]{1,0:T(8,128)(2,1)S(1)} %collective-permute-done.64.refs_10_), channel_id=1, source_target_pairs={{0,16},{1,17},{2,18},{3,19},{4,20},{5,21},{6,22},{7,23},{8,24},{9,... | collective-permute-start | bytes 1843208 | tf_op jit(solution)/shard_map/ppermute | solution.py:936
  327.9 27.5 %collective-permute-start.69 = (bf16[384,768]{1,0:T(8,128)(2,1)S(1)}, bf16[384,768]{1,0:T(8,128)(2,1)S(1)}, u32[]{:S(2)}, u32[]{:S(2)}) collective-permute-start(bf16[384,768]{1,0:T(8,128)(2,1)S(1)} %collective-permute-done.67.refs_14_), channel_id=1, source_target_pairs={{0,16},{1,17},{2,18},{3,19},{4,20},{5,21},{6,22},{7,23},{8,24},{9,... | collective-permute-start | bytes 1769480 | tf_op jit(solution)/shard_map/ppermute | solution.py:936
  329.4 11.3 %collective-permute-start.58 = (bf16[400,768]{1,0:T(8,128)(2,1)S(1)}, bf16[400,768]{1,0:T(8,128)(2,1)}, u32[]{:S(2)}, u32[]{:S(2)}) collective-permute-start(bf16[400,768]{1,0:T(8,128)(2,1)S(1)} %broadcast_select_fusion.refs_1_), channel_id=1, source_target_pairs={{0,2},{2,0},{4,6},{6,4},{8,10},{10,8},{12,14},{14,12},{1,3},{3,1},... | collective-permute-start | bytes 1843208 | tf_op jit(solution)/shard_map/ppermute | solution.py:657
  330.7 26.9 %collective-permute-start.61 = (bf16[384,768]{1,0:T(8,128)(2,1)}, bf16[384,768]{1,0:T(8,128)(2,1)}, u32[]{:S(2)}, u32[]{:S(2)}) collective-permute-start(bf16[384,768]{1,0:T(8,128)(2,1)} %broadcast_select_fusion.4.refs_5_), channel_id=1, source_target_pairs={{0,2},{2,0},{4,6},{6,4},{8,10},{10,8},{12,14},{14,12},{1,3},{3,1},... | collective-permute-start | bytes 1769480 | tf_op jit(solution)/shard_map/ppermute | solution.py:657
  332.0 29.3 %collective-permute-start.59 = (bf16[400,768]{1,0:T(8,128)(2,1)S(1)}, bf16[400,768]{1,0:T(8,128)(2,1)}, u32[]{:S(2)}, u32[]{:S(2)}) collective-permute-start(bf16[400,768]{1,0:T(8,128)(2,1)S(1)} %broadcast_select_fusion.refs_1_), channel_id=1, source_target_pairs={{16,0},{17,1},{18,2},{19,3},{20,4},{21,5},{22,6},{23,7},{24,8},{25... | collective-permute-start | bytes 1843208 | tf_op jit(solution)/shard_map/ppermute | solution.py:936
  340.7 22.9 %collective-permute-start.60 = (bf16[400,768]{1,0:T(8,128)(2,1)}, bf16[400,768]{1,0:T(8,128)(2,1)}, u32[]{:S(2)}, u32[]{:S(2)}) collective-permute-start(bf16[400,768]{1,0:T(8,128)(2,1)} %collective-permute-done.58.refs_2_), channel_id=1, source_target_pairs={{16,0},{17,1},{18,2},{19,3},{20,4},{21,5},{22,6},{23,7},{24,8},{25... | collective-permute-start | bytes 1843208 | tf_op jit(solution)/shard_map/ppermute | solution.py:936
  353.3 18.0 %collective-permute-start.56 = (bf16[784,384]{1,0:T(8,128)(2,1)S(1)}, bf16[784,384]{1,0:T(8,128)(2,1)}, u32[]{:S(2)}, u32[]{:S(2)}) collective-permute-start(bf16[784,384]{1,0:T(8,128)(2,1)S(1)} %add.142), channel_id=1, source_target_pairs={{4,0},{6,2},{8,12},{10,14},{5,1},{7,3},{9,13},{11,15},{20,16},{22,... | collective-permute-start | bytes 1806344 | tf_op jit(solution)/shard_map/ppermute | solution.py:932
  361.3 11.3 %collective-permute-start.32 = (bf16[256,768]{1,0:T(8,128)(2,1)S(1)}, bf16[256,768]{1,0:T(8,128)(2,1)S(1)}, u32[]{:S(2)}, u32[]{:S(2)}) collective-permute-start(bf16[256,768]{1,0:T(8,128)(2,1)S(1)} %constant_dynamic-slice_fusion), channel_id=1, source_target_pairs={{0,16},{1,17},{2,18},{3,19},{4,20},{5,21},{6,22},{7,23},{8,24},{9,... | collective-permute-start | bytes 1179656 | tf_op jit(solution)/shard_map/ppermute | solution.py:1001
  363.6 14.5 %collective-permute-start.73 = (bf16[784,384]{1,0:T(8,128)(2,1)S(1)}, bf16[784,384]{1,0:T(8,128)(2,1)S(1)}, u32[]{:S(2)}, u32[]{:S(2)}) collective-permute-start(bf16[784,384]{1,0:T(8,128)(2,1)S(1)} %broadcast_select_fusion.3.refs_5_), channel_id=1, source_target_pairs={{0,2},{2,0},{4,6},{6,4},{8,10},{10,8},{12,14},{14,12},{1,3},{3,1},... | collective-permute-start | bytes 1806344 | tf_op jit(solution)/shard_map/ppermute | solution.py:657
  371.4 18.8 %collective-permute-start.70 = (bf16[784,384]{1,0:T(8,128)(2,1)S(1)}, bf16[784,384]{1,0:T(8,128)(2,1)S(1)}, u32[]{:S(2)}, u32[]{:S(2)}) collective-permute-start(bf16[784,384]{1,0:T(8,128)(2,1)S(1)} %broadcast_select_fusion.2.refs_1_), channel_id=1, source_target_pairs={{0,2},{2,0},{4,6},{6,4},{8,10},{10,8},{12,14},{14,12},{1,3},{3,1},... | collective-permute-start | bytes 1806344 | tf_op jit(solution)/shard_map/ppermute | solution.py:657
  373.2 21.3 %collective-permute-start.33 = (bf16[256,768]{1,0:T(8,128)(2,1)S(1)}, bf16[256,768]{1,0:T(8,128)(2,1)S(1)}, u32[]{:S(2)}, u32[]{:S(2)}) collective-permute-start(bf16[256,768]{1,0:T(8,128)(2,1)S(1)} %get-tuple-element.313), channel_id=1, source_target_pairs={{16,0},{17,1},{18,2},{19,3},{20,4},{21,5},{22,6},{23,7},{24,8},{25... | collective-permute-start | bytes 1179656 | tf_op jit(solution)/shard_map/ppermute | solution.py:1002
  376.8 18.7 %collective-permute-start.74 = (bf16[784,384]{1,0:T(8,128)(2,1)S(1)}, bf16[784,384]{1,0:T(8,128)(2,1)S(1)}, u32[]{:S(2)}, u32[]{:S(2)}) collective-permute-start(bf16[784,384]{1,0:T(8,128)(2,1)S(1)} %broadcast_select_fusion.3.refs_5_), channel_id=1, source_target_pairs={{0,16},{1,17},{2,18},{3,19},{4,20},{5,21},{6,22},{7,23},{8,24},{9,... | collective-permute-start | bytes 1806344 | tf_op jit(solution)/shard_map/ppermute | solution.py:936
  378.2 17.4 %collective-permute-start.75 = (bf16[784,384]{1,0:T(8,128)(2,1)S(1)}, bf16[784,384]{1,0:T(8,128)(2,1)S(1)}, u32[]{:S(2)}, u32[]{:S(2)}) collective-permute-start(bf16[784,384]{1,0:T(8,128)(2,1)S(1)} %collective-permute-done.73.refs_6_), channel_id=1, source_target_pairs={{0,16},{1,17},{2,18},{3,19},{4,20},{5,21},{6,22},{7,23},{8,24},{9,... | collective-permute-start | bytes 1806344 | tf_op jit(solution)/shard_map/ppermute | solution.py:936
  379.5 16.1 %collective-permute-start.71 = (bf16[784,384]{1,0:T(8,128)(2,1)S(1)}, bf16[784,384]{1,0:T(8,128)(2,1)S(1)}, u32[]{:S(2)}, u32[]{:S(2)}) collective-permute-start(bf16[784,384]{1,0:T(8,128)(2,1)S(1)} %broadcast_select_fusion.2.refs_1_), channel_id=1, source_target_pairs={{16,0},{17,1},{18,2},{19,3},{20,4},{21,5},{22,6},{23,7},{24,8},{25... | collective-permute-start | bytes 1806344 | tf_op jit(solution)/shard_map/ppermute | solution.py:936
  (77 other events, 745.1 us)
where the time goes:
time: 410 us; the launch traced here: 402 us
  Pallas kernels  147 us (36%)
  starting transfers between devices  142 us (35%)
  waiting for transfers between devices  74.6 us (18%)
  other arithmetic  19.9 us (5%)
  local copies, waits for them, and re-layouts  16.6 us (4%)
    pallas_call x18, Pallas kernels, call(): pl.pallas_call(body, grid=(1,) if 'c' in spaces else (), out_shape=[jax.S...  147 us
    ppermute x12, starting transfers between devices, step(): lax.ppermute(b, 'section', [route])  43.4 us
    ppermute x18, starting transfers between devices, step(): lax.ppermute(mine, 'batch', STAGES[stage][1])  37.5 us
    ppermute x26, starting transfers between devices, swap(): return lax.ppermute(block, axis, [(0, 1), (1, 0)])  36.7 us
    ppermute x26, waiting for transfers between devices, swap(): return lax.ppermute(block, axis, [(0, 1), (1, 0)])  29.1 us
    ppermute x18, waiting for transfers between devices, step(): lax.ppermute(mine, 'batch', STAGES[stage][1])  23 us
    ppermute x12, waiting for transfers between devices, pair_swap(): return lax.ppermute(block, 'batch', batch_pairs())  17.4 us
    add x24, other arithmetic, add(): sums.append(sum(terms[1:], ordered(terms[0], last)))  15.8 us
  transfers between devices with their start and end apart: 76, of which 20 were waited for; matrix products, arithmetic and copies ran while one was open for 6% of the time, Pallas kernels for 29%

commit v1 on v0

--- a/solution.py
+++ b/solution.py
@@ -432,12 +432,12 @@
 
 HEAVY, LIGHT = 20, 0
 PAD = 16
-UNITS = (2, 2)
 ORDER = (
     "KC2a", "KC2b", "KWF2", "KD2", "KWA2", "a2gn", "f2gn", "KC1a", "f2ba1", "KC1b", "KWF1",
-    "f2aa1", "KD1", "KWA1", "f2aa2", "f1gn", "a2a1", "f2ba2", "a1gn", "f2aa3", "f1aa1", "a2a2",
-    "f2ba3", "f1ba1", "f2aa4", "f1aa2", "a2a3", "f2ba4", "a1a1", "f1aa3", "f1ba2", "a2a4", "a1a2",
-    "f1ba3", "f1aa4", "a1a3", "f1ba4", "finF", "a1a4", "finA",
+    "f2aa1", "KD1", "KWA1", "f2aa2", "f1gn", "a2a1", "f2ba2", "a1gn", "a2a2", "f2aa3", "f1aa1",
+    "f1ba1", "f2ba3", "f2aa4", "f1aa2", "a2a3", "a1a1", "f2ba4", "f1aa3", "f1ba2", "a2a4", "a1a2",
+    "f2bg", "f1ba3", "f1aa4", "a1a3", "a2g", "f1ag", "f1ba4", "f2ag", "a1a4", "f1bg", "finF",
+    "a1g", "finA",
 )
 
 
@@ -449,17 +449,15 @@
         copy.wait()
 
 
-def ffn_rows(units, block):
-    if units == 1:
-        return (2 * block + PAD,), lambda i, half: half * (2 * block + PAD) + i * block
+def ffn_rows(block):
     return (block + PAD, block), lambda i, half: i * 2 * (block + PAD) + half * (block + PAD * (1 - i))
 
 
-def ffn_product_kernel(units, flags, a, gb, gh, n1b, small, ours, theirs, held, sems):
+def ffn_product_kernel(flags, a, gb, gh, n1b, small, ours, theirs, held, sems):
     model = gb.shape[1]
     block = model // 2
     extra = jnp.concatenate([small[...], jnp.zeros((PAD - 8, model), F32)], axis=0).astype(BF)
-    sizes, start = ffn_rows(units, block)
+    sizes, start = ffn_rows(block)
     for i in range(2):
 
         def products(j, i=i):
@@ -500,75 +498,95 @@
 
 
 def fetch_sums(flags, layers, held, sems):
-    def copies(layer):
-        pieces = layers[layer]
-        for u, (sums, row, rows, at) in enumerate(pieces):
-            for far in range(2):
-                for beside in range(2):
-                    slot = 2 * (flags[0] ^ far) + (flags[6] ^ beside)
-                    i = 2 * far + beside
-                    yield pltpu.make_async_copy(
-                        sums[i].at[pl.ds(row, rows), :],
-                        held.at[slot, pl.ds(at, rows), :],
-                        sems.at[4 * u + i],
-                    )
-
     for layer in range(2):
 
         @pl.when(flags[0] == layer)
         def _(layer=layer):
-            for copy in copies(layer):
-                copy.start()
-            for copy in copies(layer):
-                copy.wait()
-
-
-def ffn_finish_kernel(units, flags, *refs):
-    counts = [4 * n for n in units]
-    sums = refs[: sum(counts)]
-    outer, inside, bias_outer, gain, bias, bias_inner, held, sems = refs[sum(counts) :]
+            for u, (sums, row, rows, at) in enumerate(layers[layer]):
+                for far in range(2):
+                    for beside in range(2):
+                        slot = 2 * (flags[0] ^ far) + (flags[6] ^ beside)
+                        pltpu.make_async_copy(
+                            sums[2 * far + beside].at[pl.ds(row, rows), :],
+                            held.at[slot, pl.ds(at, rows), :],
+                            sems.at[4 * u + slot],
+                        ).start()
+
+    def wait(u, slot):
+        sums, row, rows, at = layers[0][u]
+        pltpu.make_async_copy(
+            sums[0].at[pl.ds(row, rows), :], held.at[slot, pl.ds(at, rows), :],
+            sems.at[4 * u + slot],
+        ).wait()
+
+    return wait
+
+
+def ffn_finish_kernel(flags, *refs):
+    sums = refs[:16]
+    outer, inside, bias_outer, gain, bias, bias_inner = refs[16:22]
+    held, outer_s, inside_s, sems, out_sems = refs[22:]
     model = outer.shape[1]
     block = model // 2
-    layers = []
-    for n, mine in zip(units, (sums[: counts[0]], sums[counts[0] :])):
-        if n == 1:
-            layers.append([(mine, 0, 2 * block + PAD, 0)])
-        else:
-            layers.append(
-                [
-                    (mine[:4], 0, block, 0),
-                    (mine[4:], 0, block, block),
-                    (mine[:4], block, PAD, 2 * block),
-                ]
-            )
-    fetch_sums(flags, layers, held, sems)
-    for j in range(2):
-        outer[j * model : (j + 1) * model, :] = held[j, :model, :].astype(F32)
-        inside[:, j * model : (j + 1) * model] = held[2 + j, :model, :].astype(F32)
+    layers = [
+        [(mine[:4], 0, block, 0), (mine[4:], 0, block, block), (mine[:4], block, PAD, 2 * block)]
+        for mine in (sums[:8], sums[8:])
+    ]
+    wait = fetch_sums(flags, layers, held, sems)
+    copies = []
+    for u in range(2):
+        rows = slice(u * block, (u + 1) * block)
+        for j in range(2):
+            at = pl.ds(j * model + u * block, block)
+            wait(u, j)
+            outer_s[at, :] = held[j, rows, :].astype(F32)
+            copies.append((outer_s.at[at, :], outer.at[at, :]))
+            columns = pl.ds(j * model, model)
+            wait(u, 2 + j)
+            inside_s[rows, columns] = held[2 + j, rows, :].astype(F32)
+            place = pl.ds(u * block, block)
+            copies.append((inside_s.at[place, columns], inside.at[place, columns]))
+            for i in (len(copies) - 2, len(copies) - 1):
+                pltpu.make_async_copy(*copies[i], out_sems.at[i]).start()
+    for slot in range(4):
+        wait(2, slot)
     small = held[0, model : model + PAD, :].astype(F32)
     for i, out in enumerate((bias_outer, gain, bias)):
         out[...] = small[i : i + 1, :]
     for i in range(bias_inner.shape[1] // model):
         bias_inner[:, i * model : (i + 1) * model] = small[3 + i : 4 + i, :]
+    for i, copy in enumerate(copies):
+        pltpu.make_async_copy(*copy, out_sems.at[i]).wait()
 
 
 def attention_finish_kernel(flags, *refs):
     sums, (q, k, v, out, bias_out, gain, bias, bias_q, bias_v) = refs[:8], refs[8:17]
-    held, sems = refs[17], refs[18]
+    held, sums_s, out_s, sems, out_sems = refs[17:]
     model, width = q.shape
     rows = model + PAD
-    fetch_sums(flags, [[(sums[:4], 0, rows, 0)], [(sums[4:], 0, rows, 0)]], held, sems)
-    q[...] = held[0, :model, :].astype(F32)
-    k[...] = held[1, :model, :].astype(F32)
-    v[...] = held[2, :model, :].astype(F32)
-    for i in range(2):
-        out[:, i * width : (i + 1) * width] = held[3, i * width : (i + 1) * width, :].astype(F32)
+    wait = fetch_sums(flags, [[(sums[:4], 0, rows, 0)], [(sums[4:], 0, rows, 0)]], held, sems)
+    copies = []
+    for slot, target in enumerate((q, k, v, out)):
+        wait(0, slot)
+        if slot < 3:
+            source = sums_s.at[slot]
+            source[...] = held[slot, :model, :].astype(F32)
+        else:
+            source = out_s
+            for i in range(2):
+                source[:, i * width : (i + 1) * width] = held[
+                    slot, i * width : (i + 1) * width, :
+                ].astype(F32)
+        copies.append(pltpu.make_async_copy(source, target, out_sems.at[slot]))
+        copies[-1].start()
     left = held[0, model : model + PAD, :].astype(F32)
     for i, row in enumerate((bias_out, gain, bias)):
         row[:, :width] = left[i : i + 1, :]
         row[:, width:] = left[8 + i : 9 + i, :]
     bias_q[...] = left[3:4, :]
     bias_v[...] = left[11:12, :]
+    for copy in copies:
+        copy.wait()
 
 
 def ordered(array, after):
@@ -871,10 +889,10 @@
         state[base] = ours
         state[base + "_got"] = swap(theirs, "section")
 
-    def ffn_products(base, units, a, gb, gh, n1b, small):
+    def ffn_products(base, a, gb, gh, n1b, small):
         rows = 2 * (model + PAD)
         ours, theirs = call(
-            functools.partial(ffn_product_kernel, units), (flags, a, gb, gh, n1b, small), "svvvvv",
+            ffn_product_kernel, (flags, a, gb, gh, n1b, small), "svvvvv",
             [((rows, model), BF)] * 2,
             [pltpu.VMEM((2, rows, model), BF), pltpu.SemaphoreType.DMA((2,))],
             4 * size * model * inner, last, "a",
@@ -894,9 +912,9 @@
         return ours
 
     units = {}
-    for base, count in (("f1", UNITS[0]), ("f2", UNITS[1])):
+    for base in ("f1", "f2"):
         row = 0
-        for name, rows in zip("ab", ffn_rows(count, model // 2)[0]):
+        for name, rows in zip("ab", ffn_rows(model // 2)[0]):
             units[base + name] = (base, row, rows, model)
             row += 2 * rows
     for base in ("a1", "a2"):
@@ -931,19 +949,30 @@
         if stage < 3:
             state[name + "s"] = lax.ppermute(mine, "batch", STAGES[stage][1]) if lax.axis_size("batch") == 8 else None
         else:
-            both = (mine, pair_swap(mine))
-            route = (1, 0) if base[1] == "1" else (0, 1)
-            state[name] = both + tuple(lax.ppermute(b, "section", [route]) for b in both)
+            state[name] = (mine, pair_swap(mine))
         return mine
+
+    def share(name):
+        both = state[name]
+        route = (1, 0) if name[1] == "1" else (0, 1)
+        first_half = ordered(both[0], last)
+        state[name] = both + tuple(
+            lax.ppermute(part, "section", [route]) for part in (first_half, ordered(both[1], last))
+        )
+        return first_half
 
     def finish_ffn():
         sums = sum((state[n] for n in sorted(units) if n[0] == "f"), ())
         outs = call(
-            functools.partial(ffn_finish_kernel, UNITS), (flags,) + sums, "s" + "a" * len(sums),
+            ffn_finish_kernel, (flags,) + sums, "s" + "a" * len(sums),
             [((inner, model), F32), ((model, inner), F32)] + [((1, model), F32)] * 3
             + [((1, inner), F32)],
-            [pltpu.VMEM((4, model + PAD, model), BF), pltpu.SemaphoreType.DMA((12,))],
-            size * model, last,
+            [
+                pltpu.VMEM((4, model + PAD, model), BF), pltpu.VMEM((inner, model), F32),
+                pltpu.VMEM((model, inner), F32), pltpu.SemaphoreType.DMA((12,)),
+                pltpu.SemaphoreType.DMA((8,)),
+            ],
+            size * model, last, "aavvvv",
         )
         state["ffn"] = outs
         return outs[-1]
@@ -953,8 +982,12 @@
             attention_finish_kernel, (flags,) + state["a1"] + state["a2"], "s" + "a" * 8,
             [((model, width), F32)] * 3 + [((width, model), F32)] + [((1, model), F32)] * 3
             + [((1, width), F32)] * 2,
-            [pltpu.VMEM((4, model + PAD, width), BF), pltpu.SemaphoreType.DMA((4,))],
-            size * model, last,
+            [
+                pltpu.VMEM((4, model + PAD, width), BF), pltpu.VMEM((3, model, width), F32),
+                pltpu.VMEM((width, model), F32), pltpu.SemaphoreType.DMA((4,)),
+                pltpu.SemaphoreType.DMA((4,)),
+            ],
+            size * model, last, "aaaavvvvv",
         )
         state["attention"] = outs
         return outs[-1]
@@ -966,7 +999,7 @@
         "KC2a": lambda: back_last(0),
         "KC2b": lambda: back_last(1),
         "KWF2": lambda: ffn_products(
-            "f2", UNITS[1], a_two, state["g2b_two"], state["gh_two"], n1b_two, state["small_f2"]
+            "f2", a_two, state["g2b_two"], state["gh_two"], n1b_two, state["small_f2"]
         ),
         "KD2": lambda: back_attention("two", 1, n1_two, i1_two, vec_two, heads_two),
         "KWA2": lambda: attention_products(
@@ -975,7 +1008,7 @@
         "KC1a": lambda: back_next(0),
         "KC1b": lambda: back_next(1),
         "KWF1": lambda: ffn_products(
-            "f1", UNITS[0], a_one, state["g2b_one"], state["gh_one"], n1b_one, state["small_f1"]
+            "f1", a_one, state["g2b_one"], state["gh_one"], n1b_one, state["small_f1"]
         ),
         "KD1": lambda: back_attention("one", 0, n1_one, i1_one, vec_one, heads_one),
         "KWA1": lambda: attention_products(
@@ -989,6 +1022,7 @@
     for name in units:
         for stage in range(4):
             tasks[name + "a" + str(stage + 1)] = functools.partial(step, name, stage)
+        tasks[name + "g"] = functools.partial(share, name)
     for name in ORDER:
         last = (tasks[name](),)
 

time: 410 us -> 406 us (level)
    ppermute x12, waiting for transfers between devices: 17.4 us -> 7.91 us  [pair_swap(): return lax.ppermute(block, 'batch', batch_pairs())]
    ppermute x18, waiting for transfers between devices: 23 us -> 29.2 us  [step(): lax.ppermute(mine, 'batch', STAGES[stage][1])]
    unnamed x130 -> x136, local copies, waits for them, and re-layouts: 10.7 us -> 10.2 us
  transfers between devices with their start and end apart: 76 -> 76, of which waited for: 20 -> 22; matrix products, arithmetic and copies ran while one was open for 6% -> 7% of each run, Pallas kernels for 29% -> 29%
where the time goes in v1:
time: 406 us; the launch traced here: 399 us
  Pallas kernels  147 us (36%)
  starting transfers between devices  140 us (34%)
  waiting for transfers between devices  70.8 us (17%)
  other arithmetic  23.7 us (6%)
  local copies, waits for them, and re-layouts  15.2 us (4%)
    pallas_call x18, Pallas kernels, call(): pl.pallas_call(body, grid=(1,) if 'c' in spaces else (), out_shape=[jax.S...  147 us
    ppermute x12, starting transfers between devices, share(): lax.ppermute(part, 'section', [route])  44.7 us
    ppermute x18, starting transfers between devices, step(): lax.ppermute(mine, 'batch', STAGES[stage][1])  39.4 us
    ppermute x26, starting transfers between devices, swap(): return lax.ppermute(block, axis, [(0, 1), (1, 0)])  36.8 us
    ppermute x18, waiting for transfers between devices, step(): lax.ppermute(mine, 'batch', STAGES[stage][1])  29.2 us
    ppermute x26, waiting for transfers between devices, swap(): return lax.ppermute(block, axis, [(0, 1), (1, 0)])  28.5 us
    add x24, other arithmetic, add(): sums.append(sum(terms[1:], ordered(terms[0], last)))  19.5 us
    ppermute x6, starting transfers between devices, across(): lax.ppermute(block, ('section', 'tensor'), [(a[0] * 2 + a[1], b[0] * 2 +...  12.8 us
  transfers between devices with their start and end apart: 76, of which 22 were waited for; matrix products, arithmetic and copies ran while one was open for 7% of the time, Pallas kernels for 29%

profile of v1, /device:TPU:11, one launch (start us, length us, event | category | flops | bytes accessed | tf_op | source)
XLA Modules:
  0.0 398.8 jit_solution(17739011737583725294)
XLA Ops:
  2.8 1.4 collective-permute-start.3
  5.7 3.2 collective-permute-start.5
  10.2 2.8 collective-permute-start.7
  13.0 3.5 collective-permute-done.4.refs_4_
  20.8 12.7 %shard_map.288 = (bf16[512,768]{1,0:T(8,128)(2,1)}, bf16[512,384]{1,0:T(8,128)(2,1)}, bf16[512,384]{1,0:T(8,128)(2,1)}, bf16[512,384]{1,0:T(8,128)(2,1)}, bf16[6...) custom-call(s32[7]{0:T(128)} %pad_add_fusion.refs_0_, ...), custom_call_target="tpu_custom_call" | custom-call | flops 32212254720 | bytes 167772160 | tf_op jit(solution)/shard_map/pallas_call | solution.py:614
  35.0 8.7 %collective-permute-done.11.refs_3_ = bf16[256,768]{1,0:T(8,128)(2,1)S(1)} collective-permute-done((bf16[256,768]{1,0:T(8,128)(2,1)}, bf16[256,768]{1,0:T(8,128)(2,1)S(1)}, u32[]{:S(2)}, u32[]{:S(2)}) %collective-permute-start.11) | collective-permute-done | bytes 393248 | tf_op jit(solution)/shard_map/ppermute | solution.py:661
  44.5 5.9 %shard_map.289 = (f32[512,768]{1,0:T(8,128)}, f32[512,1]{1,0:T(8,128)}, bf16[512,768]{1,0:T(8,128)(2,1)}, bf16[512,1536]{1,0:T(8,128)(2,1)}, bf16[512,1536]{1,0:T(8,128)(2,1)}, /*index=5*/bf16[256,768]{1,0:T(8,128)(2,1)}) custom-call(s32[7]{0:T(128)} %pad_add_fusion.refs_0_, bf16[512,768]{1,0:T(8,128)(2,1)} %get-tuple-element.177.refs_1_, ...), custom_call_target="tpu_custom_call" | custom-call | tf_op jit(solution)/shard_map/pallas_call | solution.py:614
  50.5 1.7 collective-permute-done.10.refs_3_
  52.9 6.0 %shard_map.290 = (f32[512,768]{1,0:T(8,128)}, f32[512,1]{1,0:T(8,128)}, bf16[512,768]{1,0:T(8,128)(2,1)}, bf16[512,1536]{1,0:T(8,128)(2,1)}, bf16[512,1536]{1,0:T(8,128)(2,1)}, /*index=5*/bf16[256,768]{1,0:T(8,128)(2,1)}) custom-call(s32[7]{0:T(128)} %pad_add_fusion.refs_0_, ...), custom_call_target="tpu_custom_call", output_to_operand_aliasing={{0}: (9, {}), {1}: (10, {}), {2}: (11, {}), {3}: (12, {}), ... | custom-call | tf_op jit(solution)/shard_map/pallas_call | solution.py:614
  60.5 4.0 %collective-permute-start.14 = (bf16[256,768]{1,0:T(8,128)(2,1)S(1)}, bf16[256,768]{1,0:T(8,128)(2,1)S(1)}, u32[]{:S(2)}, u32[]{:S(2)}) collective-permute-start(bf16[256,768]{1,0:T(8,128)(2,1)S(1)} %copy-done.43), channel_id=1, source_target_pairs={{16,0},{17,1},{18,2},{19,3},{20,4},{21,5},{22,6},{23,7},{24,8},{25... | collective-permute-start | bytes 1179656 | tf_op jit(solution)/shard_map/ppermute | solution.py:665
  64.5 2.4 collective-permute-start.13
  67.0 2.3 collective-permute-start.12
  69.3 7.4 %collective-permute-done.15.refs_4_ = bf16[256,768]{1,0:T(8,128)(2,1)S(1)} collective-permute-done((bf16[256,768]{1,0:T(8,128)(2,1)S(1)}, bf16[256,768]{1,0:T(8,128)(2,1)S(1)}, u32[]{:S(2)}, u32[]{:S(2)}) %collective-permute-start.15) | collective-permute-done | bytes 393248 | tf_op jit(solution)/shard_map/ppermute | solution.py:661
  77.4 13.7 %shard_map.291 = (f32[512,768]{1,0:T(8,128)}, f32[512,1]{1,0:T(8,128)}, bf16[512,768]{1,0:T(8,128)(2,1)}, bf16[512,384]{1,0:T(8,128)(2,1)}, bf16[512,384]{1,0:T(...) custom-call(s32[7]{0:T(128)} %pad_add_fusion.refs_0_, ...), custom_call_target="tpu_custom_call" | custom-call | flops 32212254720 | bytes 167772160 | tf_op jit(solution)/shard_map/pallas_call | solution.py:614
  92.7 5.3 %collective-permute-done.18.refs_3_ = bf16[256,768]{1,0:T(8,128)(2,1)S(1)} collective-permute-done((bf16[256,768]{1,0:T(8,128)(2,1)}, bf16[256,768]{1,0:T(8,128)(2,1)S(1)}, u32[]{:S(2)}, u32[]{:S(2)}) %collective-permute-start.18) | collective-permute-done | bytes 393248 | tf_op jit(solution)/shard_map/ppermute | solution.py:661
  98.8 5.9 %shard_map.292 = (f32[512,768]{1,0:T(8,128)}, f32[512,1]{1,0:T(8,128)}, bf16[512,768]{1,0:T(8,128)(2,1)}, bf16[512,1536]{1,0:T(8,128)(2,1)}, bf16[512,1536]{1,0:T(8,128)(2,1)}, /*index=5*/bf16[256,768]{1,0:T(8,128)(2,1)}) custom-call(s32[7]{0:T(128)} %pad_add_fusion.refs_0_, bf16[512,768]{1,0:T(8,128)(2,1)} %get-tuple-element.192.refs_1_, ...), custom_call_target="tpu_custom_call" | custom-call | tf_op jit(solution)/shard_map/pallas_call | solution.py:614
  106.8 5.9 %shard_map.293 = (f32[512,768]{1,0:T(8,128)}, f32[512,1]{1,0:T(8,128)}, bf16[512,768]{1,0:T(8,128)(2,1)}, bf16[512,1536]{1,0:T(8,128)(2,1)}, bf16[512,1536]{1,0:T(8,128)(2,1)}, /*index=5*/bf16[256,768]{1,0:T(8,128)(2,1)}) custom-call(s32[7]{0:T(128)} %pad_add_fusion.refs_0_, ...), custom_call_target="tpu_custom_call", output_to_operand_aliasing={{0}: (9, {}), {1}: (10, {}), {2}: (11, {}), {3}: (12, {}), ... | custom-call | tf_op jit(solution)/shard_map/pallas_call | solution.py:614
  115.7 7.4 %shard_map.294 = (bf16[512,768]{1,0:T(8,128)(2,1)}, f32[512,768]{1,0:T(8,128)}, bf16[512,768]{1,0:T(8,128)(2,1)}, bf16[512,1536]{1,0:T(8,128)(2,1)}, bf16[256,768]{1,0:T(8,128)(2,1)}, /*index=5*/f32[8,768]{1,0:T(8,128)}) custom-call(s32[7]{0:T(128)} %pad_add_fusion.refs_0_, f32[512,768]{1,0:T(8,128)} %get-tuple-element.200.refs_1_.refs_6_, ...), custom_call_target="tpu_custom_call" | custom-call | tf_op jit(solution)/shard_map/pallas_call | solution.py:614
  123.8 7.5 %shard_map.295 = (bf16[512,768]{1,0:T(8,128)(2,1)}, f32[512,768]{1,0:T(8,128)}, bf16[512,768]{1,0:T(8,128)(2,1)}, bf16[512,1536]{1,0:T(8,128)(2,1)}, bf16[256,768]{1,0:T(8,128)(2,1)}, /*index=5*/f32[8,768]{1,0:T(8,128)}) custom-call(s32[7]{0:T(128)} %pad_add_fusion.refs_0_, ...), custom_call_target="tpu_custom_call", output_to_operand_aliasing={{0}: (15, {}), {1}: (16, {}), {2}: (17, {}), {3}: (18, {})} | custom-call | tf_op jit(solution)/shard_map/pallas_call | solution.py:614
  132.8 7.9 %shard_map.296 = (bf16[1568,768]{1,0:T(8,128)(2,1)}, bf16[1568,768]{1,0:T(8,128)(2,1)}) custom-call(s32[7]{0:T(128)} %pad_add_fusion.refs_0_, bf16[512,1536]{1,0:T(8,128)(2,1)} %get-tuple-element.212.refs_1_, bf16[512,768]{1,0:T(8,128)(2,1)} %get-tuple-element.213.refs_2_, bf16[512,1536]{1,0:T(8,128)(2,1)} %get-tuple-element.214.refs_3_, ...), custom_call_target="tpu_custom_call" | custom-call | tf_op jit(solution)/shard_map/pallas_call | solution.py:614
  140.7 10.3 %collective-permute-start.24 = (bf16[1568,768]{1,0:T(8,128)(2,1)}, bf16[1568,768]{1,0:T(8,128)(2,1)S(1)}, u32[]{:S(2)}, u32[]{:S(2)}) collective-permute-start(bf16[1568,768]{1,0:T(8,128)(2,1)} %get-tuple-element.237), channel_id=1, source_target_pairs={{0,16},{16,0},{1,17},{17,1},{2,18},{18,2},{3,19},{19,3},{4,20},{20... | collective-permute-start | bytes 7225352 | tf_op jit(solution)/shard_map/ppermute | solution.py:661
  151.9 14.1 %shard_map.297 = (f32[512,768]{1,0:T(8,128)}, bf16[512,768]{1,0:T(8,128)(2,1)}, bf16[512,1152]{1,0:T(8,128)(2,1)}, bf16[256,768]{1,0:T(8,128)(2,1)}, bf16[256,768]{1,0:T(8,128)(2,1)}, /*index=5*/f32[8,768]{1,0:T(8,128)}) custom-call(s32[7]{0:T(128)} %pad_add_fusion.refs_0_, f32[512,768]{1,0:T(8,128)} %get-tuple-element.218.refs_1_, ...), custom_call_target="tpu_custom_call" | custom-call | flops 40265318400 | bytes 167772160 | tf_op jit(solution)/shard_map/pallas_call | solution.py:614
  166.0 5.9 %shard_map.298 = (bf16[1568,384]{1,0:T(8,128)(2,1)}, bf16[1568,384]{1,0:T(8,128)(2,1)}) custom-call(s32[7]{0:T(128)} %pad_add_fusion.refs_0_, bf16[512,768]{1,0:T(8,128)(2,1)} %get-tuple-element.192.refs_1_, bf16[512,1152]{1,0:T(8,128)(2,1)} %get-tuple-element.230.refs_2_, bf16[512,384]{1,0:T(8,128)(2,1)} %get-tuple-element.231.refs_3_, ...), custom_call_target="tpu_custom_call" | custom-call | tf_op jit(solution)/shard_map/pallas_call | solution.py:614
  171.9 2.2 collective-permute-start.23
  175.4 1.4 collective-permute-done.23
  182.2 2.0 collective-permute-done.25.refs_3_
  185.0 7.2 %shard_map.299 = (f32[512,768]{1,0:T(8,128)}, bf16[512,768]{1,0:T(8,128)(2,1)}, bf16[512,1536]{1,0:T(8,128)(2,1)}, bf16[256,768]{1,0:T(8,128)(2,1)}, f32[8,768]{1,0:T(8,128)}) custom-call(s32[7]{0:T(128)} %pad_add_fusion.refs_0_, f32[512,768]{1,0:T(8,128)} %get-tuple-element.239.refs_1_, bf16[256,768]{1,0:T(8,128)(2,1)} %get-tuple-element.240.refs_2_, ...), custom_call_target="tpu_custom_call" | custom-call | tf_op jit(solution)/shard_map/pallas_call | solution.py:614
  193.5 2.0 fusion.5
  197.5 7.2 %shard_map.300 = (f32[512,768]{1,0:T(8,128)}, bf16[512,768]{1,0:T(8,128)(2,1)}, bf16[512,1536]{1,0:T(8,128)(2,1)}, bf16[256,768]{1,0:T(8,128)(2,1)}, f32[8,768]{1,0:T(8,128)}) custom-call(s32[7]{0:T(128)} %pad_add_fusion.refs_0_, f32[512,768]{1,0:T(8,128)} %get-tuple-element.239.refs_1_, ...), custom_call_target="tpu_custom_call", output_to_operand_aliasing={{0}: (13, {}), {1}: (14, {}), {2}: (15, {})} | custom-call | tf_op jit(solution)/shard_map/pallas_call | solution.py:614
  205.8 7.9 %shard_map.301 = (bf16[1568,768]{1,0:T(8,128)(2,1)}, bf16[1568,768]{1,0:T(8,128)(2,1)}) custom-call(s32[7]{0:T(128)} %pad_add_fusion.refs_0_, bf16[512,1536]{1,0:T(8,128)(2,1)} %get-tuple-element.254.refs_1_, bf16[512,768]{1,0:T(8,128)(2,1)} %get-tuple-element.255.refs_2_, bf16[512,1536]{1,0:T(8,128)(2,1)} %get-tuple-element.256.refs_3_, ...), custom_call_target="tpu_custom_call" | custom-call | tf_op jit(solution)/shard_map/pallas_call | solution.py:614
  213.7 1.3 fusion.8
  215.1 2.6 collective-permute-start.35
  220.9 13.8 %shard_map.302 = (f32[512,768]{1,0:T(8,128)}, bf16[512,768]{1,0:T(8,128)(2,1)}, bf16[512,1152]{1,0:T(8,128)(2,1)}, bf16[256,768]{1,0:T(8,128)(2,1)}, bf16[256,768]{1,0:T(8,128)(2,1)}, /*index=5*/f32[8,768]{1,0:T(8,128)}) custom-call(s32[7]{0:T(128)} %pad_add_fusion.refs_0_, f32[512,768]{1,0:T(8,128)} %get-tuple-element.260.refs_1_, ...), custom_call_target="tpu_custom_call" | custom-call | flops 40265318400 | bytes 167772160 | tf_op jit(solution)/shard_map/pallas_call | solution.py:614
  234.8 5.7 %shard_map.303 = (bf16[1568,384]{1,0:T(8,128)(2,1)}, bf16[1568,384]{1,0:T(8,128)(2,1)}) custom-call(s32[7]{0:T(128)} %pad_add_fusion.refs_0_, bf16[512,768]{1,0:T(8,128)(2,1)} %get-tuple-element.177.refs_1_, bf16[512,1152]{1,0:T(8,128)(2,1)} %get-tuple-element.276.refs_2_, bf16[512,384]{1,0:T(8,128)(2,1)} %get-tuple-element.277.refs_3_, ...), custom_call_target="tpu_custom_call" | custom-call | tf_op jit(solution)/shard_map/pallas_call | solution.py:614
  242.0 3.3 collective-permute-start.40
  245.8 1.6 fusion.3
  249.9 1.4 add.124
  251.3 2.1 collective-permute-start.44
  254.3 9.5 %collective-permute-done.39 = bf16[784,384]{1,0:T(8,128)(2,1)S(1)} collective-permute-done((bf16[784,384]{1,0:T(8,128)(2,1)S(1)}, bf16[784,384]{1,0:T(8,128)(2,1)S(1)}, u32[]{:S(2)}, u32[]{:S(2)}) %collective-permute-start.39) | collective-permute-done | bytes 602144 | tf_op jit(solution)/shard_map/ppermute | solution.py:950
  264.1 2.1 collective-permute-start.42
  267.6 2.1 collective-permute-start.46
  269.7 3.1 collective-permute-done.43
  275.0 3.9 collective-permute-start.49
  280.3 1.6 collective-permute-done.45
  284.9 1.7 collective-permute-done.47
  289.0 2.6 collective-permute-start.50
  292.8 4.8 %collective-permute-start.48 = (bf16[784,384]{1,0:T(8,128)(2,1)S(1)}, bf16[784,384]{1,0:T(8,128)(2,1)}, u32[]{:S(2)}, u32[]{:S(2)}) collective-permute-start(bf16[784,384]{1,0:T(8,128)(2,1)S(1)} %add.135), channel_id=1, source_target_pairs={{4,0},{6,2},{8,12},{10,14},{5,1},{7,3},{9,13},{11,15},{20,16},{22,... | collective-permute-start | bytes 1806344 | tf_op jit(solution)/shard_map/ppermute | solution.py:950
  297.6 6.1 %collective-permute-done.50 = bf16[400,768]{1,0:T(8,128)(2,1)} collective-permute-done((bf16[400,768]{1,0:T(8,128)(2,1)S(1)}, bf16[400,768]{1,0:T(8,128)(2,1)}, u32[]{:S(2)}, u32[]{:S(2)}) %collective-permute-start.50) | collective-permute-done | bytes 614432 | tf_op jit(solution)/shard_map/ppermute | solution.py:950
  305.1 1.5 collective-permute-start.53
  306.5 1.4 add.139
  307.9 3.1 collective-permute-start.54
  313.7 1.5 add.140
  315.1 6.0 %collective-permute-done.54 = bf16[384,768]{1,0:T(8,128)(2,1)S(1)} collective-permute-done((bf16[384,768]{1,0:T(8,128)(2,1)S(1)}, bf16[384,768]{1,0:T(8,128)(2,1)S(1)}, u32[]{:S(2)}, u32[]{:S(2)}) %collective-permute-start.54) | collective-permute-done | bytes 589856 | tf_op jit(solution)/shard_map/ppermute | solution.py:950
  321.1 3.5 collective-permute-start.55
  329.0 5.0 %collective-permute-done.55 = bf16[784,384]{1,0:T(8,128)(2,1)S(1)} collective-permute-done((bf16[784,384]{1,0:T(8,128)(2,1)S(1)}, bf16[784,384]{1,0:T(8,128)(2,1)S(1)}, u32[]{:S(2)}, u32[]{:S(2)}) %collective-permute-start.55) | collective-permute-done | bytes 602144 | tf_op jit(solution)/shard_map/ppermute | solution.py:950
  334.2 1.5 collective-permute-start.56
  336.1 11.2 %collective-permute-start.59 = (bf16[400,768]{1,0:T(8,128)(2,1)S(1)}, bf16[400,768]{1,0:T(8,128)(2,1)S(1)}, u32[]{:S(2)}, u32[]{:S(2)}) collective-permute-start(bf16[400,768]{1,0:T(8,128)(2,1)S(1)} %broadcast_select_fusion.refs_1_), channel_id=1, source_target_pairs={{16,0},{17,1},{18,2},{19,3},{20,4},{21,5},{22,6},{23,7},{24,8},{25... | collective-permute-start | bytes 1843208 | tf_op jit(solution)/shard_map/ppermute | solution.py:960
  348.8 2.9 collective-permute-done.73.refs_6_
  353.1 11.9 %collective-permute-start.60 = (bf16[400,768]{1,0:T(8,128)(2,1)S(1)}, bf16[400,768]{1,0:T(8,128)(2,1)S(1)}, u32[]{:S(2)}, u32[]{:S(2)}) collective-permute-start(bf16[400,768]{1,0:T(8,128)(2,1)S(1)} %collective-permute-done.58.refs_2_), channel_id=1, source_target_pairs={{16,0},{17,1},{18,2},{19,3},{20,4},{21,5},{22,6},{23,7},{24,8},{25... | collective-permute-start | bytes 1843208 | tf_op jit(solution)/shard_map/ppermute | solution.py:960
  365.2 7.3 %collective-permute-start.62 = (bf16[384,768]{1,0:T(8,128)(2,1)S(1)}, bf16[384,768]{1,0:T(8,128)(2,1)S(1)}, u32[]{:S(2)}, u32[]{:S(2)}) collective-permute-start(bf16[384,768]{1,0:T(8,128)(2,1)S(1)} %broadcast_select_fusion.4.refs_5_), channel_id=1, source_target_pairs={{16,0},{17,1},{18,2},{19,3},{20,4},{21,5},{22,6},{23,7},{24,8},{25... | collective-permute-start | bytes 1769480 | tf_op jit(solution)/shard_map/ppermute | solution.py:960
  372.5 2.1 collective-permute-start.63
  379.0 6.8 %shard_map.304 = (f32[1536,768]{1,0:T(8,128)}, f32[768,1536]{1,0:T(8,128)}, f32[1,768]{1,0:T(1,128)}, f32[1,768]{1,0:T(1,128)}, f32[1,768]{1,0:T(1,128)}, /*index=5*/f32[1,1536]{1,0:T(1,128)}) custom-call(s32[7]{0:T(128)} %pad_add_fusion.refs_0_, bf16[400,768]{1,0:T(8,128)(2,1)} %copy-done.6, bf16[400,768]{1,0:T(8,128)(2,1)} %copy-done.26, ...), custom_call_target="tpu_custom_call" | custom-call | tf_op jit(solution)/shard_map/pallas_call | solution.py:614
  385.9 3.1 collective-permute-start.71
  393.4 5.2 %shard_map.305 = (f32[768,384]{1,0:T(8,128)}, f32[768,384]{1,0:T(8,128)}, f32[768,384]{1,0:T(8,128)}, f32[384,768]{1,0:T(8,128)}, f32[1,768]{1,0:T(1,128)}, /*in...) custom-call(s32[7]{0:T(128)} %pad_add_fusion.refs_0_, bf16[784,384]{1,0:T(8,128)(2,1)} %copy-done.11, ...), custom_call_target="tpu_custom_call" | custom-call | tf_op jit(solution)/shard_map/pallas_call | solution.py:614
  (293 shorter events, 77.3 us)
Async XLA Ops:
  0.8 15.7 %collective-permute-start = (bf16[768,1536]{1,0:T(8,128)(2,1)}, bf16[768,1536]{1,0:T(8,128)(2,1)S(1)}, u32[]{:S(2)}, u32[]{:S(2)}) collective-permute-start(bf16[768,1536]{1,0:T(8,128)(2,1)} %bitcast.27), channel_id=1, source_target_pairs={{0,16},{16,0},{1,17},{17,1},{2,18},{18,2},{3,19},{19,3},{4,20},{20... | collective-permute-start | bytes 7077896 | tf_op jit(solution)/shard_map/ppermute | solution.py:661
  1.5 15.5 %collective-permute-start.1 = (bf16[1536,768]{1,0:T(8,128)(2,1)}, bf16[1536,768]{1,0:T(8,128)(2,1)}, u32[]{:S(2)}, u32[]{:S(2)}) collective-permute-start(bf16[1536,768]{1,0:T(8,128)(2,1)} %bitcast.36), channel_id=1, source_target_pairs={{0,16},{16,0},{1,17},{17,1},{2,18},{18,2},{3,19},{19,3},{4,20},{20... | collective-permute-start | bytes 7077896 | tf_op jit(solution)/shard_map/ppermute | solution.py:661
  4.2 12.3 %collective-permute-start.4 = (bf16[256,768]{1,0:T(8,128)(2,1)S(1)}, bf16[256,768]{1,0:T(8,128)(2,1)}, u32[]{:S(2)}, u32[]{:S(2)}) collective-permute-start(bf16[256,768]{1,0:T(8,128)(2,1)S(1)} %get-tuple-element.186.refs_5_), channel_id=1, source_target_pairs={{0,17},{1,16},{2,19},{3,18},{4,21},{5,20},{6,23},{7,22},{8,25},{9,... | collective-permute-start | bytes 1179656 | tf_op jit(solution)/shard_map/ppermute | solution.py:665
  9.9 10.9 %collective-permute-start.6 = (bf16[768,384]{1,0:T(8,128)(2,1)}, bf16[768,384]{1,0:T(8,128)(2,1)}, u32[]{:S(2)}, u32[]{:S(2)}) collective-permute-start(bf16[768,384]{1,0:T(8,128)(2,1)} %bitcast.51), channel_id=1, source_target_pairs={{0,16},{16,0},{1,17},{17,1},{2,18},{18,2},{3,19},{19,3},{4,20},{20... | collective-permute-start | bytes 1769480 | tf_op jit(solution)/shard_map/ppermute | solution.py:661
  10.2 10.6 %collective-permute-start.7 = (bf16[768,384]{1,0:T(8,128)(2,1)}, bf16[768,384]{1,0:T(8,128)(2,1)}, u32[]{:S(2)}, u32[]{:S(2)}) collective-permute-start(bf16[768,384]{1,0:T(8,128)(2,1)} %bitcast.56), channel_id=1, source_target_pairs={{0,16},{16,0},{1,17},{17,1},{2,18},{18,2},{3,19},{19,3},{4,20},{20... | collective-permute-start | bytes 1769480 | tf_op jit(solution)/shard_map/ppermute | solution.py:661
  33.5 10.2 %collective-permute-start.11 = (bf16[256,768]{1,0:T(8,128)(2,1)}, bf16[256,768]{1,0:T(8,128)(2,1)S(1)}, u32[]{:S(2)}, u32[]{:S(2)}) collective-permute-start(bf16[256,768]{1,0:T(8,128)(2,1)} %get-tuple-element.179.refs_2_), channel_id=1, source_target_pairs={{0,1},{1,0},{2,3},{3,2},{4,5},{5,4},{6,7},{7,6},{8,9},{9,8},{10,11... | collective-permute-start | bytes 1179656 | tf_op jit(solution)/shard_map/ppermute | solution.py:661
  34.8 17.4 %collective-permute-start.10 = (bf16[256,768]{1,0:T(8,128)(2,1)}, bf16[256,768]{1,0:T(8,128)(2,1)S(1)}, u32[]{:S(2)}, u32[]{:S(2)}) collective-permute-start(bf16[256,768]{1,0:T(8,128)(2,1)} %get-tuple-element.178.refs_2_), channel_id=1, source_target_pairs={{0,1},{1,0},{2,3},{3,2},{4,5},{5,4},{6,7},{7,6},{8,9},{9,8},{10,11... | collective-permute-start | bytes 1179656 | tf_op jit(solution)/shard_map/ppermute | solution.py:661
  58.9 10.3 %collective-permute-start.16 = (bf16[256,768]{1,0:T(8,128)(2,1)}, bf16[256,768]{1,0:T(8,128)(2,1)S(1)}, u32[]{:S(2)}, u32[]{:S(2)}) collective-permute-start(bf16[256,768]{1,0:T(8,128)(2,1)} %get-tuple-element.191.refs_3_), channel_id=1, source_target_pairs={{0,1},{1,0},{2,3},{3,2},{4,5},{5,4},{6,7},{7,6},{8,9},{9,8},{10,11... | collective-permute-start | bytes 1179656 | tf_op jit(solution)/shard_map/ppermute | solution.py:661
  60.3 16.4 %collective-permute-start.15 = (bf16[256,768]{1,0:T(8,128)(2,1)S(1)}, bf16[256,768]{1,0:T(8,128)(2,1)S(1)}, u32[]{:S(2)}, u32[]{:S(2)}) collective-permute-start(bf16[256,768]{1,0:T(8,128)(2,1)S(1)} %copy-done.63), channel_id=1, source_target_pairs={{0,1},{1,0},{2,3},{3,2},{4,5},{5,4},{6,7},{7,6},{8,9},{9,8},{10,11... | collective-permute-start | bytes 1179656 | tf_op jit(solution)/shard_map/ppermute | solution.py:661
  60.5 32.2 %collective-permute-start.14 = (bf16[256,768]{1,0:T(8,128)(2,1)S(1)}, bf16[256,768]{1,0:T(8,128)(2,1)S(1)}, u32[]{:S(2)}, u32[]{:S(2)}) collective-permute-start(bf16[256,768]{1,0:T(8,128)(2,1)S(1)} %copy-done.43), channel_id=1, source_target_pairs={{16,0},{17,1},{18,2},{19,3},{20,4},{21,5},{22,6},{23,7},{24,8},{25... | collective-permute-start | bytes 1179656 | tf_op jit(solution)/shard_map/ppermute | solution.py:665
  64.5 28.2 %collective-permute-start.13 = (bf16[256,768]{1,0:T(8,128)(2,1)S(1)}, bf16[256,768]{1,0:T(8,128)(2,1)S(1)}, u32[]{:S(2)}, u32[]{:S(2)}) collective-permute-start(bf16[256,768]{1,0:T(8,128)(2,1)S(1)} %copy-done.43), channel_id=1, source_target_pairs={{16,1},{17,0},{18,3},{19,2},{20,5},{21,4},{22,7},{23,6},{24,9},{25... | collective-permute-start | bytes 1179656 | tf_op jit(solution)/shard_map/ppermute | solution.py:665
  67.0 25.7 %collective-permute-start.12 = (bf16[256,768]{1,0:T(8,128)(2,1)S(1)}, bf16[256,768]{1,0:T(8,128)(2,1)S(1)}, u32[]{:S(2)}, u32[]{:S(2)}) collective-permute-start(bf16[256,768]{1,0:T(8,128)(2,1)S(1)} %get-tuple-element.186.refs_5_), channel_id=1, source_target_pairs={{16,17},{17,16},{18,19},{19,18},{20,21},{21,20},{22,23},{23,22},{2... | collective-permute-start | bytes 1179656 | tf_op jit(solution)/shard_map/ppermute | solution.py:665
  92.5 13.6 %collective-permute-start.17 = (bf16[256,768]{1,0:T(8,128)(2,1)}, bf16[256,768]{1,0:T(8,128)(2,1)S(1)}, u32[]{:S(2)}, u32[]{:S(2)}) collective-permute-start(bf16[256,768]{1,0:T(8,128)(2,1)} %get-tuple-element.193.refs_2_), channel_id=1, source_target_pairs={{0,1},{1,0},{2,3},{3,2},{4,5},{5,4},{6,7},{7,6},{8,9},{9,8},{10,11... | collective-permute-start | bytes 1179656 | tf_op jit(solution)/shard_map/ppermute | solution.py:661
  104.8 10.1 %collective-permute-start.19 = (bf16[256,768]{1,0:T(8,128)(2,1)}, bf16[256,768]{1,0:T(8,128)(2,1)S(1)}, u32[]{:S(2)}, u32[]{:S(2)}) collective-permute-start(bf16[256,768]{1,0:T(8,128)(2,1)} %get-tuple-element.201.refs_2_), channel_id=1, source_target_pairs={{0,1},{1,0},{2,3},{3,2},{4,5},{5,4},{6,7},{7,6},{8,9},{9,8},{10,11... | collective-permute-start | bytes 1179656 | tf_op jit(solution)/shard_map/ppermute | solution.py:661
  112.8 10.3 %collective-permute-start.20 = (bf16[256,768]{1,0:T(8,128)(2,1)}, bf16[256,768]{1,0:T(8,128)(2,1)S(1)}, u32[]{:S(2)}, u32[]{:S(2)}) collective-permute-start(bf16[256,768]{1,0:T(8,128)(2,1)} %get-tuple-element.205.refs_2_), channel_id=1, source_target_pairs={{0,1},{1,0},{2,3},{3,2},{4,5},{5,4},{6,7},{7,6},{8,9},{9,8},{10,11... | collective-permute-start | bytes 1179656 | tf_op jit(solution)/shard_map/ppermute | solution.py:661
  131.3 19.7 %collective-permute-start.22 = (bf16[256,768]{1,0:T(8,128)(2,1)}, bf16[256,768]{1,0:T(8,128)(2,1)S(1)}, u32[]{:S(2)}, u32[]{:S(2)}) collective-permute-start(bf16[256,768]{1,0:T(8,128)(2,1)} %get-tuple-element.220.refs_3_), channel_id=1, source_target_pairs={{0,1},{1,0},{2,3},{3,2},{4,5},{5,4},{6,7},{7,6},{8,9},{9,8},{10,11... | collective-permute-start | bytes 1179656 | tf_op jit(solution)/shard_map/ppermute | solution.py:661
  132.6 18.4 %collective-permute-start.21 = (bf16[256,768]{1,0:T(8,128)(2,1)S(1)}, bf16[256,768]{1,0:T(8,128)(2,1)S(1)}, u32[]{:S(2)}, u32[]{:S(2)}) collective-permute-start(bf16[256,768]{1,0:T(8,128)(2,1)S(1)} %copy-done.61), channel_id=1, source_target_pairs={{0,1},{1,0},{2,3},{3,2},{4,5},{5,4},{6,7},{7,6},{8,9},{9,8},{10,11... | collective-permute-start | bytes 1179656 | tf_op jit(solution)/shard_map/ppermute | solution.py:661
  140.7 37.0 %collective-permute-start.24 = (bf16[1568,768]{1,0:T(8,128)(2,1)}, bf16[1568,768]{1,0:T(8,128)(2,1)S(1)}, u32[]{:S(2)}, u32[]{:S(2)}) collective-permute-start(bf16[1568,768]{1,0:T(8,128)(2,1)} %get-tuple-element.237), channel_id=1, source_target_pairs={{0,16},{16,0},{1,17},{17,1},{2,18},{18,2},{3,19},{19,3},{4,20},{20... | collective-permute-start | bytes 7225352 | tf_op jit(solution)/shard_map/ppermute | solution.py:661
  174.1 10.1 %collective-permute-start.25 = (bf16[256,768]{1,0:T(8,128)(2,1)S(1)}, bf16[256,768]{1,0:T(8,128)(2,1)S(1)}, u32[]{:S(2)}, u32[]{:S(2)}) collective-permute-start(bf16[256,768]{1,0:T(8,128)(2,1)S(1)} %copy-done.45), channel_id=1, source_target_pairs={{0,1},{1,0},{2,3},{3,2},{4,5},{5,4},{6,7},{7,6},{8,9},{9,8},{10,11... | collective-permute-start | bytes 1179656 | tf_op jit(solution)/shard_map/ppermute | solution.py:661
  178.6 14.9 %collective-permute-start.26 = (bf16[384,768]{1,0:T(8,128)(2,1)}, bf16[384,768]{1,0:T(8,128)(2,1)}, u32[]{:S(2)}, u32[]{:S(2)}) collective-permute-start(bf16[384,768]{1,0:T(8,128)(2,1)} %slice_add_fusion.10), channel_id=1, source_target_pairs={{0,2},{2,0},{4,6},{6,4},{8,10},{10,8},{12,14},{14,12},{1,3},{3,1},... | collective-permute-start | bytes 1769480 | tf_op jit(solution)/shard_map/ppermute | solution.py:675
  179.6 17.1 %collective-permute-start.27 = (bf16[256,768]{1,0:T(8,128)(2,1)S(1)}, bf16[256,768]{1,0:T(8,128)(2,1)S(1)}, u32[]{:S(2)}, u32[]{:S(2)}) collective-permute-start(bf16[256,768]{1,0:T(8,128)(2,1)S(1)} %copy-done.44), channel_id=1, source_target_pairs={{0,1},{1,0},{2,3},{3,2},{4,5},{5,4},{6,7},{7,6},{8,9},{9,8},{10,11... | collective-permute-start | bytes 1179656 | tf_op jit(solution)/shard_map/ppermute | solution.py:661
  180.7 34.4 %collective-permute-start.28 = (bf16[400,768]{1,0:T(8,128)(2,1)S(1)}, bf16[400,768]{1,0:T(8,128)(2,1)}, u32[]{:S(2)}, u32[]{:S(2)}) collective-permute-start(bf16[400,768]{1,0:T(8,128)(2,1)S(1)} %slice_add_fusion.3), channel_id=1, source_target_pairs={{0,2},{2,0},{4,6},{6,4},{8,10},{10,8},{12,14},{14,12},{1,3},{3,1},... | collective-permute-start | bytes 1843208 | tf_op jit(solution)/shard_map/ppermute | solution.py:675
  181.4 64.5 %collective-permute-start.36 = (bf16[784,384]{1,0:T(8,128)(2,1)}, bf16[784,384]{1,0:T(8,128)(2,1)}, u32[]{:S(2)}, u32[]{:S(2)}) collective-permute-start(bf16[784,384]{1,0:T(8,128)(2,1)} %slice_add_fusion.7), channel_id=1, source_target_pairs={{0,2},{2,0},{4,6},{6,4},{8,10},{10,8},{12,14},{14,12},{1,3},{3,1},... | collective-permute-start | bytes 1806344 | tf_op jit(solution)/shard_map/ppermute | solution.py:675
  192.2 26.7 %collective-permute-start.29 = (bf16[256,768]{1,0:T(8,128)(2,1)}, bf16[256,768]{1,0:T(8,128)(2,1)}, u32[]{:S(2)}, u32[]{:S(2)}) collective-permute-start(bf16[256,768]{1,0:T(8,128)(2,1)} %get-tuple-element.261.refs_2_), channel_id=1, source_target_pairs={{0,1},{1,0},{2,3},{3,2},{4,5},{5,4},{6,7},{7,6},{8,9},{9,8},{10,11... | collective-permute-start | bytes 1179656 | tf_op jit(solution)/shard_map/ppermute | solution.py:661
  195.4 53.4 %collective-permute-start.37 = (bf16[384,768]{1,0:T(8,128)(2,1)}, bf16[384,768]{1,0:T(8,128)(2,1)}, u32[]{:S(2)}, u32[]{:S(2)}) collective-permute-start(bf16[384,768]{1,0:T(8,128)(2,1)} %fusion.5), channel_id=1, source_target_pairs={{0,4},{2,6},{12,8},{14,10},{1,5},{3,7},{13,9},{15,11},{16,20},{18,... | collective-permute-start | bytes 1769480 | tf_op jit(solution)/shard_map/ppermute | solution.py:950
  204.7 15.5 %collective-permute-start.30 = (bf16[256,768]{1,0:T(8,128)(2,1)}, bf16[256,768]{1,0:T(8,128)(2,1)S(1)}, u32[]{:S(2)}, u32[]{:S(2)}) collective-permute-start(bf16[256,768]{1,0:T(8,128)(2,1)} %get-tuple-element.262.refs_3_), channel_id=1, source_target_pairs={{0,1},{1,0},{2,3},{3,2},{4,5},{5,4},{6,7},{7,6},{8,9},{9,8},{10,11... | collective-permute-start | bytes 1179656 | tf_op jit(solution)/shard_map/ppermute | solution.py:661
  215.1 30.3 %collective-permute-start.35 = (bf16[1568,768]{1,0:T(8,128)(2,1)}, bf16[1568,768]{1,0:T(8,128)(2,1)S(1)}, u32[]{:S(2)}, u32[]{:S(2)}) collective-permute-start(bf16[1568,768]{1,0:T(8,128)(2,1)} %get-tuple-element.282), channel_id=1, source_target_pairs={{0,16},{16,0},{1,17},{17,1},{2,18},{18,2},{3,19},{19,3},{4,20},{20... | collective-permute-start | bytes 7225352 | tf_op jit(solution)/shard_map/ppermute | solution.py:661
  218.9 23.0 %collective-permute-start.34 = (bf16[400,768]{1,0:T(8,128)(2,1)S(1)}, bf16[400,768]{1,0:T(8,128)(2,1)S(1)}, u32[]{:S(2)}, u32[]{:S(2)}) collective-permute-start(bf16[400,768]{1,0:T(8,128)(2,1)S(1)} %fusion.1), channel_id=1, source_target_pairs={{0,4},{2,6},{12,8},{14,10},{1,5},{3,7},{13,9},{15,11},{16,20},{18,... | collective-permute-start | bytes 1843208 | tf_op jit(solution)/shard_map/ppermute | solution.py:950
  240.5 10.8 %collective-permute-start.38 = (bf16[1568,384]{1,0:T(8,128)(2,1)}, bf16[1568,384]{1,0:T(8,128)(2,1)S(1)}, u32[]{:S(2)}, u32[]{:S(2)}) collective-permute-start(bf16[1568,384]{1,0:T(8,128)(2,1)} %get-tuple-element.286), channel_id=1, source_target_pairs={{0,16},{16,0},{1,17},{17,1},{2,18},{18,2},{3,19},{19,3},{4,20},{20... | collective-permute-start | bytes 3612680 | tf_op jit(solution)/shard_map/ppermute | solution.py:661
  242.0 21.9 %collective-permute-start.40 = (bf16[400,768]{1,0:T(8,128)(2,1)S(1)}, bf16[400,768]{1,0:T(8,128)(2,1)S(1)}, u32[]{:S(2)}, u32[]{:S(2)}) collective-permute-start(bf16[400,768]{1,0:T(8,128)(2,1)S(1)} %add.120), channel_id=1, source_target_pairs={{4,8},{6,10},{8,4},{10,6},{5,9},{7,11},{9,5},{11,7},{20,24},{22,26... | collective-permute-start | bytes 1843208 | tf_op jit(solution)/shard_map/ppermute | solution.py:950
  245.5 20.7 %collective-permute-start.41 = (bf16[400,768]{1,0:T(8,128)(2,1)S(1)}, bf16[400,768]{1,0:T(8,128)(2,1)S(1)}, u32[]{:S(2)}, u32[]{:S(2)}) collective-permute-start(bf16[400,768]{1,0:T(8,128)(2,1)S(1)} %slice_add_fusion.1), channel_id=1, source_target_pairs={{0,2},{2,0},{4,6},{6,4},{8,10},{10,8},{12,14},{14,12},{1,3},{3,1},... | collective-permute-start | bytes 1843208 | tf_op jit(solution)/shard_map/ppermute | solution.py:675
  247.5 16.3 %collective-permute-start.39 = (bf16[784,384]{1,0:T(8,128)(2,1)S(1)}, bf16[784,384]{1,0:T(8,128)(2,1)S(1)}, u32[]{:S(2)}, u32[]{:S(2)}) collective-permute-start(bf16[784,384]{1,0:T(8,128)(2,1)S(1)} %fusion.3), channel_id=1, source_target_pairs={{0,4},{2,6},{12,8},{14,10},{1,5},{3,7},{13,9},{15,11},{16,20},{18,... | collective-permute-start | bytes 1806344 | tf_op jit(solution)/shard_map/ppermute | solution.py:950
  248.9 23.9 %collective-permute-start.43 = (bf16[384,768]{1,0:T(8,128)(2,1)S(1)}, bf16[384,768]{1,0:T(8,128)(2,1)S(1)}, u32[]{:S(2)}, u32[]{:S(2)}) collective-permute-start(bf16[384,768]{1,0:T(8,128)(2,1)S(1)} %slice_add_fusion.8), channel_id=1, source_target_pairs={{0,2},{2,0},{4,6},{6,4},{8,10},{10,8},{12,14},{14,12},{1,3},{3,1},... | collective-permute-start | bytes 1769480 | tf_op jit(solution)/shard_map/ppermute | solution.py:675
  251.3 22.7 %collective-permute-start.44 = (bf16[384,768]{1,0:T(8,128)(2,1)S(1)}, bf16[384,768]{1,0:T(8,128)(2,1)S(1)}, u32[]{:S(2)}, u32[]{:S(2)}) collective-permute-start(bf16[384,768]{1,0:T(8,128)(2,1)S(1)} %add.124), channel_id=1, source_target_pairs={{4,8},{6,10},{8,4},{10,6},{5,9},{7,11},{9,5},{11,7},{20,24},{22,26... | collective-permute-start | bytes 1769480 | tf_op jit(solution)/shard_map/ppermute | solution.py:950
  264.1 14.8 %collective-permute-start.42 = (bf16[400,768]{1,0:T(8,128)(2,1)S(1)}, bf16[400,768]{1,0:T(8,128)(2,1)}, u32[]{:S(2)}, u32[]{:S(2)}) collective-permute-start(bf16[400,768]{1,0:T(8,128)(2,1)S(1)} %add.127), channel_id=1, source_target_pairs={{4,0},{6,2},{8,12},{10,14},{5,1},{7,3},{9,13},{11,15},{20,16},{22,... | collective-permute-start | bytes 1843208 | tf_op jit(solution)/shard_map/ppermute | solution.py:950
  266.3 15.6 %collective-permute-start.45 = (bf16[400,768]{1,0:T(8,128)(2,1)S(1)}, bf16[400,768]{1,0:T(8,128)(2,1)}, u32[]{:S(2)}, u32[]{:S(2)}) collective-permute-start(bf16[400,768]{1,0:T(8,128)(2,1)S(1)} %fusion), channel_id=1, source_target_pairs={{0,4},{2,6},{12,8},{14,10},{1,5},{3,7},{13,9},{15,11},{16,20},{18,... | collective-permute-start | bytes 1843208 | tf_op jit(solution)/shard_map/ppermute | solution.py:950
  267.6 16.0 %collective-permute-start.46 = (bf16[784,384]{1,0:T(8,128)(2,1)S(1)}, bf16[784,384]{1,0:T(8,128)(2,1)}, u32[]{:S(2)}, u32[]{:S(2)}) collective-permute-start(bf16[784,384]{1,0:T(8,128)(2,1)S(1)} %add.126), channel_id=1, source_target_pairs={{4,8},{6,10},{8,4},{10,6},{5,9},{7,11},{9,5},{11,7},{20,24},{22,26... | collective-permute-start | bytes 1806344 | tf_op jit(solution)/shard_map/ppermute | solution.py:950
  272.8 13.7 %collective-permute-start.47 = (bf16[784,384]{1,0:T(8,128)(2,1)}, bf16[784,384]{1,0:T(8,128)(2,1)}, u32[]{:S(2)}, u32[]{:S(2)}) collective-permute-start(bf16[784,384]{1,0:T(8,128)(2,1)} %slice_add_fusion.5), channel_id=1, source_target_pairs={{0,2},{2,0},{4,6},{6,4},{8,10},{10,8},{12,14},{14,12},{1,3},{3,1},... | collective-permute-start | bytes 1806344 | tf_op jit(solution)/shard_map/ppermute | solution.py:675
  275.0 16.6 %collective-permute-start.49 = (bf16[384,768]{1,0:T(8,128)(2,1)}, bf16[384,768]{1,0:T(8,128)(2,1)}, u32[]{:S(2)}, u32[]{:S(2)}) collective-permute-start(bf16[384,768]{1,0:T(8,128)(2,1)} %add.133), channel_id=1, source_target_pairs={{4,0},{6,2},{8,12},{10,14},{5,1},{7,3},{9,13},{11,15},{20,16},{22,... | collective-permute-start | bytes 1769480 | tf_op jit(solution)/shard_map/ppermute | solution.py:950
  278.9 27.7 %collective-permute-start.51 = (bf16[384,768]{1,0:T(8,128)(2,1)}, bf16[384,768]{1,0:T(8,128)(2,1)}, u32[]{:S(2)}, u32[]{:S(2)}) collective-permute-start(bf16[384,768]{1,0:T(8,128)(2,1)} %fusion.4), channel_id=1, source_target_pairs={{0,4},{2,6},{12,8},{14,10},{1,5},{3,7},{13,9},{15,11},{16,20},{18,... | collective-permute-start | bytes 1769480 | tf_op jit(solution)/shard_map/ppermute | solution.py:950
  287.7 24.6 %collective-permute-start.52 = (bf16[784,384]{1,0:T(8,128)(2,1)S(1)}, bf16[784,384]{1,0:T(8,128)(2,1)}, u32[]{:S(2)}, u32[]{:S(2)}) collective-permute-start(bf16[784,384]{1,0:T(8,128)(2,1)S(1)} %fusion.2), channel_id=1, source_target_pairs={{0,4},{2,6},{12,8},{14,10},{1,5},{3,7},{13,9},{15,11},{16,20},{18,... | collective-permute-start | bytes 1806344 | tf_op jit(solution)/shard_map/ppermute | solution.py:950
  289.0 14.8 %collective-permute-start.50 = (bf16[400,768]{1,0:T(8,128)(2,1)S(1)}, bf16[400,768]{1,0:T(8,128)(2,1)}, u32[]{:S(2)}, u32[]{:S(2)}) collective-permute-start(bf16[400,768]{1,0:T(8,128)(2,1)S(1)} %add.134), channel_id=1, source_target_pairs={{4,8},{6,10},{8,4},{10,6},{5,9},{7,11},{9,5},{11,7},{20,24},{22,26... | collective-permute-start | bytes 1843208 | tf_op jit(solution)/shard_map/ppermute | solution.py:950
  292.8 18.3 %collective-permute-start.67 = (bf16[384,768]{1,0:T(8,128)(2,1)S(1)}, bf16[384,768]{1,0:T(8,128)(2,1)}, u32[]{:S(2)}, u32[]{:S(2)}) collective-permute-start(bf16[384,768]{1,0:T(8,128)(2,1)S(1)} %broadcast_select_fusion.5.refs_13_), channel_id=1, source_target_pairs={{0,2},{2,0},{4,6},{6,4},{8,10},{10,8},{12,14},{14,12},{1,3},{3,1},... | collective-permute-start | bytes 1769480 | tf_op jit(solution)/shard_map/ppermute | solution.py:675
  292.8 19.7 %collective-permute-start.48 = (bf16[784,384]{1,0:T(8,128)(2,1)S(1)}, bf16[784,384]{1,0:T(8,128)(2,1)}, u32[]{:S(2)}, u32[]{:S(2)}) collective-permute-start(bf16[784,384]{1,0:T(8,128)(2,1)S(1)} %add.135), channel_id=1, source_target_pairs={{4,0},{6,2},{8,12},{10,14},{5,1},{7,3},{9,13},{11,15},{20,16},{22,... | collective-permute-start | bytes 1806344 | tf_op jit(solution)/shard_map/ppermute | solution.py:950
  305.1 21.1 %collective-permute-start.53 = (bf16[400,768]{1,0:T(8,128)(2,1)S(1)}, bf16[400,768]{1,0:T(8,128)(2,1)S(1)}, u32[]{:S(2)}, u32[]{:S(2)}) collective-permute-start(bf16[400,768]{1,0:T(8,128)(2,1)S(1)} %add.138), channel_id=1, source_target_pairs={{4,0},{6,2},{8,12},{10,14},{5,1},{7,3},{9,13},{11,15},{20,16},{22,... | collective-permute-start | bytes 1843208 | tf_op jit(solution)/shard_map/ppermute | solution.py:950
  307.9 13.2 %collective-permute-start.54 = (bf16[384,768]{1,0:T(8,128)(2,1)S(1)}, bf16[384,768]{1,0:T(8,128)(2,1)S(1)}, u32[]{:S(2)}, u32[]{:S(2)}) collective-permute-start(bf16[384,768]{1,0:T(8,128)(2,1)S(1)} %add.139), channel_id=1, source_target_pairs={{4,8},{6,10},{8,4},{10,6},{5,9},{7,11},{9,5},{11,7},{20,24},{22,26... | collective-permute-start | bytes 1769480 | tf_op jit(solution)/shard_map/ppermute | solution.py:950
  311.0 13.8 %collective-permute-start.32 = (bf16[256,768]{1,0:T(8,128)(2,1)S(1)}, bf16[256,768]{1,0:T(8,128)(2,1)S(1)}, u32[]{:S(2)}, u32[]{:S(2)}) collective-permute-start(bf16[256,768]{1,0:T(8,128)(2,1)S(1)} %constant_dynamic-slice_fusion), channel_id=1, source_target_pairs={{0,16},{1,17},{2,18},{3,19},{4,20},{5,21},{6,22},{7,23},{8,24},{9,... | collective-permute-start | bytes 1179656 | tf_op jit(solution)/shard_map/ppermute | solution.py:1035
  312.3 15.3 %collective-permute-start.64 = (bf16[400,768]{1,0:T(8,128)(2,1)S(1)}, bf16[400,768]{1,0:T(8,128)(2,1)S(1)}, u32[]{:S(2)}, u32[]{:S(2)}) collective-permute-start(bf16[400,768]{1,0:T(8,128)(2,1)S(1)} %broadcast_select_fusion.1.refs_9_), channel_id=1, source_target_pairs={{0,2},{2,0},{4,6},{6,4},{8,10},{10,8},{12,14},{14,12},{1,3},{3,1},... | collective-permute-start | bytes 1843208 | tf_op jit(solution)/shard_map/ppermute | solution.py:675
  312.5 15.1 %collective-permute-start.31 = (bf16[256,768]{1,0:T(8,128)(2,1)S(1)}, bf16[256,768]{1,0:T(8,128)(2,1)S(1)}, u32[]{:S(2)}, u32[]{:S(2)}) collective-permute-start(bf16[256,768]{1,0:T(8,128)(2,1)S(1)} %broadcast_select_fusion.6), channel_id=1, source_target_pairs={{0,1},{1,0},{2,3},{3,2},{4,5},{5,4},{6,7},{7,6},{8,9},{9,8},{10,11... | collective-permute-start | bytes 1179656 | tf_op jit(solution)/shard_map/ppermute | solution.py:661
  321.1 12.9 %collective-permute-start.55 = (bf16[784,384]{1,0:T(8,128)(2,1)S(1)}, bf16[784,384]{1,0:T(8,128)(2,1)S(1)}, u32[]{:S(2)}, u32[]{:S(2)}) collective-permute-start(bf16[784,384]{1,0:T(8,128)(2,1)S(1)} %add.140), channel_id=1, source_target_pairs={{4,8},{6,10},{8,4},{10,6},{5,9},{7,11},{9,5},{11,7},{20,24},{22,26... | collective-permute-start | bytes 1806344 | tf_op jit(solution)/shard_map/ppermute | solution.py:950
  327.6 21.1 %collective-permute-start.58 = (bf16[400,768]{1,0:T(8,128)(2,1)S(1)}, bf16[400,768]{1,0:T(8,128)(2,1)S(1)}, u32[]{:S(2)}, u32[]{:S(2)}) collective-permute-start(bf16[400,768]{1,0:T(8,128)(2,1)S(1)} %broadcast_select_fusion.refs_1_), channel_id=1, source_target_pairs={{0,2},{2,0},{4,6},{6,4},{8,10},{10,8},{12,14},{14,12},{1,3},{3,1},... | collective-permute-start | bytes 1843208 | tf_op jit(solution)/shard_map/ppermute | solution.py:675
  327.7 19.7 %collective-permute-start.69 = (bf16[384,768]{1,0:T(8,128)(2,1)}, bf16[384,768]{1,0:T(8,128)(2,1)}, u32[]{:S(2)}, u32[]{:S(2)}) collective-permute-start(bf16[384,768]{1,0:T(8,128)(2,1)} %collective-permute-done.67.refs_14_), channel_id=1, source_target_pairs={{0,16},{1,17},{2,18},{3,19},{4,20},{5,21},{6,22},{7,23},{8,24},{9,... | collective-permute-start | bytes 1769480 | tf_op jit(solution)/shard_map/ppermute | solution.py:960
  334.0 17.7 %collective-permute-start.73 = (bf16[784,384]{1,0:T(8,128)(2,1)S(1)}, bf16[784,384]{1,0:T(8,128)(2,1)}, u32[]{:S(2)}, u32[]{:S(2)}) collective-permute-start(bf16[784,384]{1,0:T(8,128)(2,1)S(1)} %broadcast_select_fusion.3.refs_5_), channel_id=1, source_target_pairs={{0,2},{2,0},{4,6},{6,4},{8,10},{10,8},{12,14},{14,12},{1,3},{3,1},... | collective-permute-start | bytes 1806344 | tf_op jit(solution)/shard_map/ppermute | solution.py:675
  334.2 18.8 %collective-permute-start.56 = (bf16[784,384]{1,0:T(8,128)(2,1)S(1)}, bf16[784,384]{1,0:T(8,128)(2,1)S(1)}, u32[]{:S(2)}, u32[]{:S(2)}) collective-permute-start(bf16[784,384]{1,0:T(8,128)(2,1)S(1)} %add.142), channel_id=1, source_target_pairs={{4,0},{6,2},{8,12},{10,14},{5,1},{7,3},{9,13},{11,15},{20,16},{22,... | collective-permute-start | bytes 1806344 | tf_op jit(solution)/shard_map/ppermute | solution.py:950
  336.1 29.0 %collective-permute-start.59 = (bf16[400,768]{1,0:T(8,128)(2,1)S(1)}, bf16[400,768]{1,0:T(8,128)(2,1)S(1)}, u32[]{:S(2)}, u32[]{:S(2)}) collective-permute-start(bf16[400,768]{1,0:T(8,128)(2,1)S(1)} %broadcast_select_fusion.refs_1_), channel_id=1, source_target_pairs={{16,0},{17,1},{18,2},{19,3},{20,4},{21,5},{22,6},{23,7},{24,8},{25... | collective-permute-start | bytes 1843208 | tf_op jit(solution)/shard_map/ppermute | solution.py:960
  347.4 25.1 %collective-permute-start.65 = (bf16[400,768]{1,0:T(8,128)(2,1)S(1)}, bf16[400,768]{1,0:T(8,128)(2,1)S(1)}, u32[]{:S(2)}, u32[]{:S(2)}) collective-permute-start(bf16[400,768]{1,0:T(8,128)(2,1)S(1)} %broadcast_select_fusion.1.refs_9_), channel_id=1, source_target_pairs={{0,16},{1,17},{2,18},{3,19},{4,20},{5,21},{6,22},{7,23},{8,24},{9,... | collective-permute-start | bytes 1843208 | tf_op jit(solution)/shard_map/ppermute | solution.py:960
  348.7 16.5 %collective-permute-start.61 = (bf16[384,768]{1,0:T(8,128)(2,1)S(1)}, bf16[384,768]{1,0:T(8,128)(2,1)S(1)}, u32[]{:S(2)}, u32[]{:S(2)}) collective-permute-start(bf16[384,768]{1,0:T(8,128)(2,1)S(1)} %broadcast_select_fusion.4.refs_5_), channel_id=1, source_target_pairs={{0,2},{2,0},{4,6},{6,4},{8,10},{10,8},{12,14},{14,12},{1,3},{3,1},... | collective-permute-start | bytes 1769480 | tf_op jit(solution)/shard_map/ppermute | solution.py:675
  351.8 23.2 %collective-permute-start.66 = (bf16[400,768]{1,0:T(8,128)(2,1)S(1)}, bf16[400,768]{1,0:T(8,128)(2,1)S(1)}, u32[]{:S(2)}, u32[]{:S(2)}) collective-permute-start(bf16[400,768]{1,0:T(8,128)(2,1)S(1)} %collective-permute-done.64.refs_10_), channel_id=1, source_target_pairs={{0,16},{1,17},{2,18},{3,19},{4,20},{5,21},{6,22},{7,23},{8,24},{9,... | collective-permute-start | bytes 1843208 | tf_op jit(solution)/shard_map/ppermute | solution.py:960
  353.1 24.6 %collective-permute-start.60 = (bf16[400,768]{1,0:T(8,128)(2,1)S(1)}, bf16[400,768]{1,0:T(8,128)(2,1)S(1)}, u32[]{:S(2)}, u32[]{:S(2)}) collective-permute-start(bf16[400,768]{1,0:T(8,128)(2,1)S(1)} %collective-permute-done.58.refs_2_), channel_id=1, source_target_pairs={{16,0},{17,1},{18,2},{19,3},{20,4},{21,5},{22,6},{23,7},{24,8},{25... | collective-permute-start | bytes 1843208 | tf_op jit(solution)/shard_map/ppermute | solution.py:960
  365.1 20.7 %collective-permute-start.70 = (bf16[784,384]{1,0:T(8,128)(2,1)S(1)}, bf16[784,384]{1,0:T(8,128)(2,1)S(1)}, u32[]{:S(2)}, u32[]{:S(2)}) collective-permute-start(bf16[784,384]{1,0:T(8,128)(2,1)S(1)} %broadcast_select_fusion.2.refs_1_), channel_id=1, source_target_pairs={{0,2},{2,0},{4,6},{6,4},{8,10},{10,8},{12,14},{14,12},{1,3},{3,1},... | collective-permute-start | bytes 1806344 | tf_op jit(solution)/shard_map/ppermute | solution.py:675
  365.2 11.1 %collective-permute-start.62 = (bf16[384,768]{1,0:T(8,128)(2,1)S(1)}, bf16[384,768]{1,0:T(8,128)(2,1)S(1)}, u32[]{:S(2)}, u32[]{:S(2)}) collective-permute-start(bf16[384,768]{1,0:T(8,128)(2,1)S(1)} %broadcast_select_fusion.4.refs_5_), channel_id=1, source_target_pairs={{16,0},{17,1},{18,2},{19,3},{20,4},{21,5},{22,6},{23,7},{24,8},{25... | collective-permute-start | bytes 1769480 | tf_op jit(solution)/shard_map/ppermute | solution.py:960
  375.0 15.3 %collective-permute-start.33 = (bf16[256,768]{1,0:T(8,128)(2,1)S(1)}, bf16[256,768]{1,0:T(8,128)(2,1)S(1)}, u32[]{:S(2)}, u32[]{:S(2)}) collective-permute-start(bf16[256,768]{1,0:T(8,128)(2,1)S(1)} %get-tuple-element.337), channel_id=1, source_target_pairs={{16,0},{17,1},{18,2},{19,3},{20,4},{21,5},{22,6},{23,7},{24,8},{25... | collective-permute-start | bytes 1179656 | tf_op jit(solution)/shard_map/ppermute | solution.py:1036
  376.4 15.0 %collective-permute-start.74 = (bf16[784,384]{1,0:T(8,128)(2,1)S(1)}, bf16[784,384]{1,0:T(8,128)(2,1)S(1)}, u32[]{:S(2)}, u32[]{:S(2)}) collective-permute-start(bf16[784,384]{1,0:T(8,128)(2,1)S(1)} %broadcast_select_fusion.3.refs_5_), channel_id=1, source_target_pairs={{0,16},{1,17},{2,18},{3,19},{4,20},{5,21},{6,22},{7,23},{8,24},{9,... | collective-permute-start | bytes 1806344 | tf_op jit(solution)/shard_map/ppermute | solution.py:960
  377.7 13.7 %collective-permute-start.75 = (bf16[784,384]{1,0:T(8,128)(2,1)}, bf16[784,384]{1,0:T(8,128)(2,1)S(1)}, u32[]{:S(2)}, u32[]{:S(2)}) collective-permute-start(bf16[784,384]{1,0:T(8,128)(2,1)} %collective-permute-done.73.refs_6_), channel_id=1, source_target_pairs={{0,16},{1,17},{2,18},{3,19},{4,20},{5,21},{6,22},{7,23},{8,24},{9,... | collective-permute-start | bytes 1806344 | tf_op jit(solution)/shard_map/ppermute | solution.py:960
  (80 other events, 780.0 us)

commit v2 on v1

--- a/solution.py
+++ b/solution.py
@@ -145,7 +145,7 @@
             r_out[h, :, cols] = inverse
             ot_out[hs, cols] = dot(vt_s[hs, :], raised) * inverse
 
-    loop(heads, attend, 2)
+    loop(heads, attend, 3)
     wait(3)
 
     for i, p_out in enumerate(p_outs):
@@ -411,7 +411,7 @@
         vh_s[h] = grad_v.astype(BF)
         qh_s[h] = grad_k.astype(BF)
 
-    loop(heads, attend, 2)
+    loop(heads, attend, 3)
     for i in range(3):
         wait_fetch(i, source, held, sems)
 

time: 406 us -> 405 us (level)
  no operation moved by 1% of the time
where the time goes in v2:
time: 405 us; the launch traced here: 398 us
  Pallas kernels  146 us (36%)
  starting transfers between devices  140 us (35%)
  waiting for transfers between devices  70.5 us (17%)
  other arithmetic  23.8 us (6%)
  local copies, waits for them, and re-layouts  15.2 us (4%)
    pallas_call x18, Pallas kernels, call(): pl.pallas_call(body, grid=(1,) if 'c' in spaces else (), out_shape=[jax.S...  146 us
    ppermute x12, starting transfers between devices, share(): lax.ppermute(part, 'section', [route])  44.7 us
    ppermute x18, starting transfers between devices, step(): lax.ppermute(mine, 'batch', STAGES[stage][1])  39.6 us
    ppermute x26, starting transfers between devices, swap(): return lax.ppermute(block, axis, [(0, 1), (1, 0)])  36.3 us
    ppermute x18, waiting for transfers between devices, step(): lax.ppermute(mine, 'batch', STAGES[stage][1])  29 us
    ppermute x26, waiting for transfers between devices, swap(): return lax.ppermute(block, axis, [(0, 1), (1, 0)])  28.4 us
    add x24, other arithmetic, add(): sums.append(sum(terms[1:], ordered(terms[0], last)))  19.6 us
    ppermute x6, starting transfers between devices, across(): lax.ppermute(block, ('section', 'tensor'), [(a[0] * 2 + a[1], b[0] * 2 +...  12.9 us
  transfers between devices with their start and end apart: 76, of which 22 were waited for; matrix products, arithmetic and copies ran while one was open for 7% of the time, Pallas kernels for 29%

profile of v2, /device:TPU:11, one launch (start us, length us, event | category | flops | bytes accessed | tf_op | source)
XLA Modules:
  0.0 397.8 jit_solution(5624890206916752769)
XLA Ops:
  2.8 1.4 collective-permute-start.3
  5.7 3.2 collective-permute-start.5
  10.2 2.8 collective-permute-start.7
  13.0 3.5 collective-permute-done.4.refs_4_
  20.8 12.6 %shard_map.288 = (bf16[512,768]{1,0:T(8,128)(2,1)}, bf16[512,384]{1,0:T(8,128)(2,1)}, bf16[512,384]{1,0:T(8,128)(2,1)}, bf16[512,384]{1,0:T(8,128)(2,1)}, bf16[6...) custom-call(s32[7]{0:T(128)} %pad_add_fusion.refs_0_, ...), custom_call_target="tpu_custom_call" | custom-call | flops 32212254720 | bytes 167772160 | tf_op jit(solution)/shard_map/pallas_call | solution.py:614
  34.9 8.7 %collective-permute-done.11.refs_3_ = bf16[256,768]{1,0:T(8,128)(2,1)S(1)} collective-permute-done((bf16[256,768]{1,0:T(8,128)(2,1)}, bf16[256,768]{1,0:T(8,128)(2,1)S(1)}, u32[]{:S(2)}, u32[]{:S(2)}) %collective-permute-start.11) | collective-permute-done | bytes 393248 | tf_op jit(solution)/shard_map/ppermute | solution.py:661
  44.4 5.9 %shard_map.289 = (f32[512,768]{1,0:T(8,128)}, f32[512,1]{1,0:T(8,128)}, bf16[512,768]{1,0:T(8,128)(2,1)}, bf16[512,1536]{1,0:T(8,128)(2,1)}, bf16[512,1536]{1,0:T(8,128)(2,1)}, /*index=5*/bf16[256,768]{1,0:T(8,128)(2,1)}) custom-call(s32[7]{0:T(128)} %pad_add_fusion.refs_0_, bf16[512,768]{1,0:T(8,128)(2,1)} %get-tuple-element.177.refs_1_, ...), custom_call_target="tpu_custom_call" | custom-call | tf_op jit(solution)/shard_map/pallas_call | solution.py:614
  50.3 1.7 collective-permute-done.10.refs_3_
  52.8 6.0 %shard_map.290 = (f32[512,768]{1,0:T(8,128)}, f32[512,1]{1,0:T(8,128)}, bf16[512,768]{1,0:T(8,128)(2,1)}, bf16[512,1536]{1,0:T(8,128)(2,1)}, bf16[512,1536]{1,0:T(8,128)(2,1)}, /*index=5*/bf16[256,768]{1,0:T(8,128)(2,1)}) custom-call(s32[7]{0:T(128)} %pad_add_fusion.refs_0_, ...), custom_call_target="tpu_custom_call", output_to_operand_aliasing={{0}: (9, {}), {1}: (10, {}), {2}: (11, {}), {3}: (12, {}), ... | custom-call | tf_op jit(solution)/shard_map/pallas_call | solution.py:614
  60.4 4.0 %collective-permute-start.14 = (bf16[256,768]{1,0:T(8,128)(2,1)S(1)}, bf16[256,768]{1,0:T(8,128)(2,1)S(1)}, u32[]{:S(2)}, u32[]{:S(2)}) collective-permute-start(bf16[256,768]{1,0:T(8,128)(2,1)S(1)} %copy-done.43), channel_id=1, source_target_pairs={{16,0},{17,1},{18,2},{19,3},{20,4},{21,5},{22,6},{23,7},{24,8},{25... | collective-permute-start | bytes 1179656 | tf_op jit(solution)/shard_map/ppermute | solution.py:665
  64.4 2.4 collective-permute-start.13
  66.8 2.4 collective-permute-start.12
  69.3 7.3 %collective-permute-done.15.refs_4_ = bf16[256,768]{1,0:T(8,128)(2,1)S(1)} collective-permute-done((bf16[256,768]{1,0:T(8,128)(2,1)S(1)}, bf16[256,768]{1,0:T(8,128)(2,1)S(1)}, u32[]{:S(2)}, u32[]{:S(2)}) %collective-permute-start.15) | collective-permute-done | bytes 393248 | tf_op jit(solution)/shard_map/ppermute | solution.py:661
  77.3 13.6 %shard_map.291 = (f32[512,768]{1,0:T(8,128)}, f32[512,1]{1,0:T(8,128)}, bf16[512,768]{1,0:T(8,128)(2,1)}, bf16[512,384]{1,0:T(8,128)(2,1)}, bf16[512,384]{1,0:T(...) custom-call(s32[7]{0:T(128)} %pad_add_fusion.refs_0_, ...), custom_call_target="tpu_custom_call" | custom-call | flops 32212254720 | bytes 167772160 | tf_op jit(solution)/shard_map/pallas_call | solution.py:614
  92.5 5.3 %collective-permute-done.18.refs_3_ = bf16[256,768]{1,0:T(8,128)(2,1)S(1)} collective-permute-done((bf16[256,768]{1,0:T(8,128)(2,1)}, bf16[256,768]{1,0:T(8,128)(2,1)S(1)}, u32[]{:S(2)}, u32[]{:S(2)}) %collective-permute-start.18) | collective-permute-done | bytes 393248 | tf_op jit(solution)/shard_map/ppermute | solution.py:661
  98.6 5.9 %shard_map.292 = (f32[512,768]{1,0:T(8,128)}, f32[512,1]{1,0:T(8,128)}, bf16[512,768]{1,0:T(8,128)(2,1)}, bf16[512,1536]{1,0:T(8,128)(2,1)}, bf16[512,1536]{1,0:T(8,128)(2,1)}, /*index=5*/bf16[256,768]{1,0:T(8,128)(2,1)}) custom-call(s32[7]{0:T(128)} %pad_add_fusion.refs_0_, bf16[512,768]{1,0:T(8,128)(2,1)} %get-tuple-element.192.refs_1_, ...), custom_call_target="tpu_custom_call" | custom-call | tf_op jit(solution)/shard_map/pallas_call | solution.py:614
  106.6 5.9 %shard_map.293 = (f32[512,768]{1,0:T(8,128)}, f32[512,1]{1,0:T(8,128)}, bf16[512,768]{1,0:T(8,128)(2,1)}, bf16[512,1536]{1,0:T(8,128)(2,1)}, bf16[512,1536]{1,0:T(8,128)(2,1)}, /*index=5*/bf16[256,768]{1,0:T(8,128)(2,1)}) custom-call(s32[7]{0:T(128)} %pad_add_fusion.refs_0_, ...), custom_call_target="tpu_custom_call", output_to_operand_aliasing={{0}: (9, {}), {1}: (10, {}), {2}: (11, {}), {3}: (12, {}), ... | custom-call | tf_op jit(solution)/shard_map/pallas_call | solution.py:614
  115.4 7.4 %shard_map.294 = (bf16[512,768]{1,0:T(8,128)(2,1)}, f32[512,768]{1,0:T(8,128)}, bf16[512,768]{1,0:T(8,128)(2,1)}, bf16[512,1536]{1,0:T(8,128)(2,1)}, bf16[256,768]{1,0:T(8,128)(2,1)}, /*index=5*/f32[8,768]{1,0:T(8,128)}) custom-call(s32[7]{0:T(128)} %pad_add_fusion.refs_0_, f32[512,768]{1,0:T(8,128)} %get-tuple-element.200.refs_1_.refs_6_, ...), custom_call_target="tpu_custom_call" | custom-call | tf_op jit(solution)/shard_map/pallas_call | solution.py:614
  123.6 7.5 %shard_map.295 = (bf16[512,768]{1,0:T(8,128)(2,1)}, f32[512,768]{1,0:T(8,128)}, bf16[512,768]{1,0:T(8,128)(2,1)}, bf16[512,1536]{1,0:T(8,128)(2,1)}, bf16[256,768]{1,0:T(8,128)(2,1)}, /*index=5*/f32[8,768]{1,0:T(8,128)}) custom-call(s32[7]{0:T(128)} %pad_add_fusion.refs_0_, ...), custom_call_target="tpu_custom_call", output_to_operand_aliasing={{0}: (15, {}), {1}: (16, {}), {2}: (17, {}), {3}: (18, {})} | custom-call | tf_op jit(solution)/shard_map/pallas_call | solution.py:614
  132.6 8.4 %shard_map.296 = (bf16[1568,768]{1,0:T(8,128)(2,1)}, bf16[1568,768]{1,0:T(8,128)(2,1)}) custom-call(s32[7]{0:T(128)} %pad_add_fusion.refs_0_, bf16[512,1536]{1,0:T(8,128)(2,1)} %get-tuple-element.212.refs_1_, bf16[512,768]{1,0:T(8,128)(2,1)} %get-tuple-element.213.refs_2_, bf16[512,1536]{1,0:T(8,128)(2,1)} %get-tuple-element.214.refs_3_, ...), custom_call_target="tpu_custom_call" | custom-call | tf_op jit(solution)/shard_map/pallas_call | solution.py:614
  141.0 10.3 %collective-permute-start.24 = (bf16[1568,768]{1,0:T(8,128)(2,1)}, bf16[1568,768]{1,0:T(8,128)(2,1)S(1)}, u32[]{:S(2)}, u32[]{:S(2)}) collective-permute-start(bf16[1568,768]{1,0:T(8,128)(2,1)} %get-tuple-element.237), channel_id=1, source_target_pairs={{0,16},{16,0},{1,17},{17,1},{2,18},{18,2},{3,19},{19,3},{4,20},{20... | collective-permute-start | bytes 7225352 | tf_op jit(solution)/shard_map/ppermute | solution.py:661
  152.2 13.5 %shard_map.297 = (f32[512,768]{1,0:T(8,128)}, bf16[512,768]{1,0:T(8,128)(2,1)}, bf16[512,1152]{1,0:T(8,128)(2,1)}, bf16[256,768]{1,0:T(8,128)(2,1)}, bf16[256,768]{1,0:T(8,128)(2,1)}, /*index=5*/f32[8,768]{1,0:T(8,128)}) custom-call(s32[7]{0:T(128)} %pad_add_fusion.refs_0_, f32[512,768]{1,0:T(8,128)} %get-tuple-element.218.refs_1_, ...), custom_call_target="tpu_custom_call" | custom-call | flops 40265318400 | bytes 167772160 | tf_op jit(solution)/shard_map/pallas_call | solution.py:614
  165.7 5.9 %shard_map.298 = (bf16[1568,384]{1,0:T(8,128)(2,1)}, bf16[1568,384]{1,0:T(8,128)(2,1)}) custom-call(s32[7]{0:T(128)} %pad_add_fusion.refs_0_, bf16[512,768]{1,0:T(8,128)(2,1)} %get-tuple-element.192.refs_1_, bf16[512,1152]{1,0:T(8,128)(2,1)} %get-tuple-element.230.refs_2_, bf16[512,384]{1,0:T(8,128)(2,1)} %get-tuple-element.231.refs_3_, ...), custom_call_target="tpu_custom_call" | custom-call | tf_op jit(solution)/shard_map/pallas_call | solution.py:614
  171.6 1.6 collective-permute-start.23
  174.6 1.4 collective-permute-done.23
  181.5 2.0 collective-permute-done.25.refs_3_
  184.2 7.2 %shard_map.299 = (f32[512,768]{1,0:T(8,128)}, bf16[512,768]{1,0:T(8,128)(2,1)}, bf16[512,1536]{1,0:T(8,128)(2,1)}, bf16[256,768]{1,0:T(8,128)(2,1)}, f32[8,768]{1,0:T(8,128)}) custom-call(s32[7]{0:T(128)} %pad_add_fusion.refs_0_, f32[512,768]{1,0:T(8,128)} %get-tuple-element.239.refs_1_, bf16[256,768]{1,0:T(8,128)(2,1)} %get-tuple-element.240.refs_2_, ...), custom_call_target="tpu_custom_call" | custom-call | tf_op jit(solution)/shard_map/pallas_call | solution.py:614
  192.7 2.0 fusion.5
  196.7 7.2 %shard_map.300 = (f32[512,768]{1,0:T(8,128)}, bf16[512,768]{1,0:T(8,128)(2,1)}, bf16[512,1536]{1,0:T(8,128)(2,1)}, bf16[256,768]{1,0:T(8,128)(2,1)}, f32[8,768]{1,0:T(8,128)}) custom-call(s32[7]{0:T(128)} %pad_add_fusion.refs_0_, f32[512,768]{1,0:T(8,128)} %get-tuple-element.239.refs_1_, ...), custom_call_target="tpu_custom_call", output_to_operand_aliasing={{0}: (13, {}), {1}: (14, {}), {2}: (15, {})} | custom-call | tf_op jit(solution)/shard_map/pallas_call | solution.py:614
  205.0 7.9 %shard_map.301 = (bf16[1568,768]{1,0:T(8,128)(2,1)}, bf16[1568,768]{1,0:T(8,128)(2,1)}) custom-call(s32[7]{0:T(128)} %pad_add_fusion.refs_0_, bf16[512,1536]{1,0:T(8,128)(2,1)} %get-tuple-element.254.refs_1_, bf16[512,768]{1,0:T(8,128)(2,1)} %get-tuple-element.255.refs_2_, bf16[512,1536]{1,0:T(8,128)(2,1)} %get-tuple-element.256.refs_3_, ...), custom_call_target="tpu_custom_call" | custom-call | tf_op jit(solution)/shard_map/pallas_call | solution.py:614
  212.9 1.3 fusion.8
  214.3 2.6 collective-permute-start.35
  220.1 13.5 %shard_map.302 = (f32[512,768]{1,0:T(8,128)}, bf16[512,768]{1,0:T(8,128)(2,1)}, bf16[512,1152]{1,0:T(8,128)(2,1)}, bf16[256,768]{1,0:T(8,128)(2,1)}, bf16[256,768]{1,0:T(8,128)(2,1)}, /*index=5*/f32[8,768]{1,0:T(8,128)}) custom-call(s32[7]{0:T(128)} %pad_add_fusion.refs_0_, f32[512,768]{1,0:T(8,128)} %get-tuple-element.260.refs_1_, ...), custom_call_target="tpu_custom_call" | custom-call | flops 40265318400 | bytes 167772160 | tf_op jit(solution)/shard_map/pallas_call | solution.py:614
  233.7 5.7 %shard_map.303 = (bf16[1568,384]{1,0:T(8,128)(2,1)}, bf16[1568,384]{1,0:T(8,128)(2,1)}) custom-call(s32[7]{0:T(128)} %pad_add_fusion.refs_0_, bf16[512,768]{1,0:T(8,128)(2,1)} %get-tuple-element.177.refs_1_, bf16[512,1152]{1,0:T(8,128)(2,1)} %get-tuple-element.276.refs_2_, bf16[512,384]{1,0:T(8,128)(2,1)} %get-tuple-element.277.refs_3_, ...), custom_call_target="tpu_custom_call" | custom-call | tf_op jit(solution)/shard_map/pallas_call | solution.py:614
  240.9 3.3 collective-permute-start.40
  244.7 1.7 fusion.3
  248.8 1.4 add.124
  250.2 2.1 collective-permute-start.44
  253.2 9.5 %collective-permute-done.39 = bf16[784,384]{1,0:T(8,128)(2,1)S(1)} collective-permute-done((bf16[784,384]{1,0:T(8,128)(2,1)S(1)}, bf16[784,384]{1,0:T(8,128)(2,1)S(1)}, u32[]{:S(2)}, u32[]{:S(2)}) %collective-permute-start.39) | collective-permute-done | bytes 602144 | tf_op jit(solution)/shard_map/ppermute | solution.py:950
  263.0 2.1 collective-permute-start.42
  266.5 2.1 collective-permute-start.46
  268.6 3.1 collective-permute-done.43
  273.8 3.9 collective-permute-start.49
  279.1 1.7 collective-permute-done.45
  283.7 1.7 collective-permute-done.47
  287.9 2.8 collective-permute-start.50
  291.9 4.7 %collective-permute-start.48 = (bf16[784,384]{1,0:T(8,128)(2,1)S(1)}, bf16[784,384]{1,0:T(8,128)(2,1)}, u32[]{:S(2)}, u32[]{:S(2)}) collective-permute-start(bf16[784,384]{1,0:T(8,128)(2,1)S(1)} %add.135), channel_id=1, source_target_pairs={{4,0},{6,2},{8,12},{10,14},{5,1},{7,3},{9,13},{11,15},{20,16},{22,... | collective-permute-start | bytes 1806344 | tf_op jit(solution)/shard_map/ppermute | solution.py:950
  296.7 6.0 %collective-permute-done.50 = bf16[400,768]{1,0:T(8,128)(2,1)} collective-permute-done((bf16[400,768]{1,0:T(8,128)(2,1)S(1)}, bf16[400,768]{1,0:T(8,128)(2,1)}, u32[]{:S(2)}, u32[]{:S(2)}) %collective-permute-start.50) | collective-permute-done | bytes 614432 | tf_op jit(solution)/shard_map/ppermute | solution.py:950
  303.9 1.5 collective-permute-start.53
  305.4 1.4 add.139
  306.8 3.1 collective-permute-start.54
  312.6 1.5 add.140
  314.1 5.9 %collective-permute-done.54 = bf16[384,768]{1,0:T(8,128)(2,1)S(1)} collective-permute-done((bf16[384,768]{1,0:T(8,128)(2,1)S(1)}, bf16[384,768]{1,0:T(8,128)(2,1)S(1)}, u32[]{:S(2)}, u32[]{:S(2)}) %collective-permute-start.54) | collective-permute-done | bytes 589856 | tf_op jit(solution)/shard_map/ppermute | solution.py:950
  320.0 3.5 collective-permute-start.55
  327.9 5.0 %collective-permute-done.55 = bf16[784,384]{1,0:T(8,128)(2,1)S(1)} collective-permute-done((bf16[784,384]{1,0:T(8,128)(2,1)S(1)}, bf16[784,384]{1,0:T(8,128)(2,1)S(1)}, u32[]{:S(2)}, u32[]{:S(2)}) %collective-permute-start.55) | collective-permute-done | bytes 602144 | tf_op jit(solution)/shard_map/ppermute | solution.py:950
  333.1 1.5 collective-permute-start.56
  335.0 11.2 %collective-permute-start.59 = (bf16[400,768]{1,0:T(8,128)(2,1)S(1)}, bf16[400,768]{1,0:T(8,128)(2,1)S(1)}, u32[]{:S(2)}, u32[]{:S(2)}) collective-permute-start(bf16[400,768]{1,0:T(8,128)(2,1)S(1)} %broadcast_select_fusion.refs_1_), channel_id=1, source_target_pairs={{16,0},{17,1},{18,2},{19,3},{20,4},{21,5},{22,6},{23,7},{24,8},{25... | collective-permute-start | bytes 1843208 | tf_op jit(solution)/shard_map/ppermute | solution.py:960
  347.7 3.0 collective-permute-done.73.refs_6_
  351.9 11.9 %collective-permute-start.60 = (bf16[400,768]{1,0:T(8,128)(2,1)S(1)}, bf16[400,768]{1,0:T(8,128)(2,1)S(1)}, u32[]{:S(2)}, u32[]{:S(2)}) collective-permute-start(bf16[400,768]{1,0:T(8,128)(2,1)S(1)} %collective-permute-done.58.refs_2_), channel_id=1, source_target_pairs={{16,0},{17,1},{18,2},{19,3},{20,4},{21,5},{22,6},{23,7},{24,8},{25... | collective-permute-start | bytes 1843208 | tf_op jit(solution)/shard_map/ppermute | solution.py:960
  364.1 7.3 %collective-permute-start.62 = (bf16[384,768]{1,0:T(8,128)(2,1)S(1)}, bf16[384,768]{1,0:T(8,128)(2,1)S(1)}, u32[]{:S(2)}, u32[]{:S(2)}) collective-permute-start(bf16[384,768]{1,0:T(8,128)(2,1)S(1)} %broadcast_select_fusion.4.refs_5_), channel_id=1, source_target_pairs={{16,0},{17,1},{18,2},{19,3},{20,4},{21,5},{22,6},{23,7},{24,8},{25... | collective-permute-start | bytes 1769480 | tf_op jit(solution)/shard_map/ppermute | solution.py:960
  371.4 2.1 collective-permute-start.63
  377.9 6.8 %shard_map.304 = (f32[1536,768]{1,0:T(8,128)}, f32[768,1536]{1,0:T(8,128)}, f32[1,768]{1,0:T(1,128)}, f32[1,768]{1,0:T(1,128)}, f32[1,768]{1,0:T(1,128)}, /*index=5*/f32[1,1536]{1,0:T(1,128)}) custom-call(s32[7]{0:T(128)} %pad_add_fusion.refs_0_, bf16[400,768]{1,0:T(8,128)(2,1)} %copy-done.6, bf16[400,768]{1,0:T(8,128)(2,1)} %copy-done.26, ...), custom_call_target="tpu_custom_call" | custom-call | tf_op jit(solution)/shard_map/pallas_call | solution.py:614
  384.8 3.1 collective-permute-start.71
  392.3 5.2 %shard_map.305 = (f32[768,384]{1,0:T(8,128)}, f32[768,384]{1,0:T(8,128)}, f32[768,384]{1,0:T(8,128)}, f32[384,768]{1,0:T(8,128)}, f32[1,768]{1,0:T(1,128)}, /*in...) custom-call(s32[7]{0:T(128)} %pad_add_fusion.refs_0_, bf16[784,384]{1,0:T(8,128)(2,1)} %copy-done.11, ...), custom_call_target="tpu_custom_call" | custom-call | tf_op jit(solution)/shard_map/pallas_call | solution.py:614
  (293 shorter events, 77.3 us)
Async XLA Ops:
  0.8 15.7 %collective-permute-start = (bf16[768,1536]{1,0:T(8,128)(2,1)}, bf16[768,1536]{1,0:T(8,128)(2,1)S(1)}, u32[]{:S(2)}, u32[]{:S(2)}) collective-permute-start(bf16[768,1536]{1,0:T(8,128)(2,1)} %bitcast.27), channel_id=1, source_target_pairs={{0,16},{16,0},{1,17},{17,1},{2,18},{18,2},{3,19},{19,3},{4,20},{20... | collective-permute-start | bytes 7077896 | tf_op jit(solution)/shard_map/ppermute | solution.py:661
  1.5 15.5 %collective-permute-start.1 = (bf16[1536,768]{1,0:T(8,128)(2,1)}, bf16[1536,768]{1,0:T(8,128)(2,1)}, u32[]{:S(2)}, u32[]{:S(2)}) collective-permute-start(bf16[1536,768]{1,0:T(8,128)(2,1)} %bitcast.36), channel_id=1, source_target_pairs={{0,16},{16,0},{1,17},{17,1},{2,18},{18,2},{3,19},{19,3},{4,20},{20... | collective-permute-start | bytes 7077896 | tf_op jit(solution)/shard_map/ppermute | solution.py:661
  4.2 12.3 %collective-permute-start.4 = (bf16[256,768]{1,0:T(8,128)(2,1)S(1)}, bf16[256,768]{1,0:T(8,128)(2,1)}, u32[]{:S(2)}, u32[]{:S(2)}) collective-permute-start(bf16[256,768]{1,0:T(8,128)(2,1)S(1)} %get-tuple-element.186.refs_5_), channel_id=1, source_target_pairs={{0,17},{1,16},{2,19},{3,18},{4,21},{5,20},{6,23},{7,22},{8,25},{9,... | collective-permute-start | bytes 1179656 | tf_op jit(solution)/shard_map/ppermute | solution.py:665
  9.9 10.9 %collective-permute-start.6 = (bf16[768,384]{1,0:T(8,128)(2,1)}, bf16[768,384]{1,0:T(8,128)(2,1)}, u32[]{:S(2)}, u32[]{:S(2)}) collective-permute-start(bf16[768,384]{1,0:T(8,128)(2,1)} %bitcast.51), channel_id=1, source_target_pairs={{0,16},{16,0},{1,17},{17,1},{2,18},{18,2},{3,19},{19,3},{4,20},{20... | collective-permute-start | bytes 1769480 | tf_op jit(solution)/shard_map/ppermute | solution.py:661
  10.2 10.6 %collective-permute-start.7 = (bf16[768,384]{1,0:T(8,128)(2,1)}, bf16[768,384]{1,0:T(8,128)(2,1)}, u32[]{:S(2)}, u32[]{:S(2)}) collective-permute-start(bf16[768,384]{1,0:T(8,128)(2,1)} %bitcast.56), channel_id=1, source_target_pairs={{0,16},{16,0},{1,17},{17,1},{2,18},{18,2},{3,19},{19,3},{4,20},{20... | collective-permute-start | bytes 1769480 | tf_op jit(solution)/shard_map/ppermute | solution.py:661
  33.4 10.3 %collective-permute-start.11 = (bf16[256,768]{1,0:T(8,128)(2,1)}, bf16[256,768]{1,0:T(8,128)(2,1)S(1)}, u32[]{:S(2)}, u32[]{:S(2)}) collective-permute-start(bf16[256,768]{1,0:T(8,128)(2,1)} %get-tuple-element.179.refs_2_), channel_id=1, source_target_pairs={{0,1},{1,0},{2,3},{3,2},{4,5},{5,4},{6,7},{7,6},{8,9},{9,8},{10,11... | collective-permute-start | bytes 1179656 | tf_op jit(solution)/shard_map/ppermute | solution.py:661
  34.7 17.4 %collective-permute-start.10 = (bf16[256,768]{1,0:T(8,128)(2,1)}, bf16[256,768]{1,0:T(8,128)(2,1)S(1)}, u32[]{:S(2)}, u32[]{:S(2)}) collective-permute-start(bf16[256,768]{1,0:T(8,128)(2,1)} %get-tuple-element.178.refs_2_), channel_id=1, source_target_pairs={{0,1},{1,0},{2,3},{3,2},{4,5},{5,4},{6,7},{7,6},{8,9},{9,8},{10,11... | collective-permute-start | bytes 1179656 | tf_op jit(solution)/shard_map/ppermute | solution.py:661
  58.8 10.4 %collective-permute-start.16 = (bf16[256,768]{1,0:T(8,128)(2,1)}, bf16[256,768]{1,0:T(8,128)(2,1)S(1)}, u32[]{:S(2)}, u32[]{:S(2)}) collective-permute-start(bf16[256,768]{1,0:T(8,128)(2,1)} %get-tuple-element.191.refs_3_), channel_id=1, source_target_pairs={{0,1},{1,0},{2,3},{3,2},{4,5},{5,4},{6,7},{7,6},{8,9},{9,8},{10,11... | collective-permute-start | bytes 1179656 | tf_op jit(solution)/shard_map/ppermute | solution.py:661
  60.1 16.5 %collective-permute-start.15 = (bf16[256,768]{1,0:T(8,128)(2,1)S(1)}, bf16[256,768]{1,0:T(8,128)(2,1)S(1)}, u32[]{:S(2)}, u32[]{:S(2)}) collective-permute-start(bf16[256,768]{1,0:T(8,128)(2,1)S(1)} %copy-done.63), channel_id=1, source_target_pairs={{0,1},{1,0},{2,3},{3,2},{4,5},{5,4},{6,7},{7,6},{8,9},{9,8},{10,11... | collective-permute-start | bytes 1179656 | tf_op jit(solution)/shard_map/ppermute | solution.py:661
  60.4 32.1 %collective-permute-start.14 = (bf16[256,768]{1,0:T(8,128)(2,1)S(1)}, bf16[256,768]{1,0:T(8,128)(2,1)S(1)}, u32[]{:S(2)}, u32[]{:S(2)}) collective-permute-start(bf16[256,768]{1,0:T(8,128)(2,1)S(1)} %copy-done.43), channel_id=1, source_target_pairs={{16,0},{17,1},{18,2},{19,3},{20,4},{21,5},{22,6},{23,7},{24,8},{25... | collective-permute-start | bytes 1179656 | tf_op jit(solution)/shard_map/ppermute | solution.py:665
  64.4 28.1 %collective-permute-start.13 = (bf16[256,768]{1,0:T(8,128)(2,1)S(1)}, bf16[256,768]{1,0:T(8,128)(2,1)S(1)}, u32[]{:S(2)}, u32[]{:S(2)}) collective-permute-start(bf16[256,768]{1,0:T(8,128)(2,1)S(1)} %copy-done.43), channel_id=1, source_target_pairs={{16,1},{17,0},{18,3},{19,2},{20,5},{21,4},{22,7},{23,6},{24,9},{25... | collective-permute-start | bytes 1179656 | tf_op jit(solution)/shard_map/ppermute | solution.py:665
  66.8 25.6 %collective-permute-start.12 = (bf16[256,768]{1,0:T(8,128)(2,1)S(1)}, bf16[256,768]{1,0:T(8,128)(2,1)S(1)}, u32[]{:S(2)}, u32[]{:S(2)}) collective-permute-start(bf16[256,768]{1,0:T(8,128)(2,1)S(1)} %get-tuple-element.186.refs_5_), channel_id=1, source_target_pairs={{16,17},{17,16},{18,19},{19,18},{20,21},{21,20},{22,23},{23,22},{2... | collective-permute-start | bytes 1179656 | tf_op jit(solution)/shard_map/ppermute | solution.py:665
  92.2 13.6 %collective-permute-start.17 = (bf16[256,768]{1,0:T(8,128)(2,1)}, bf16[256,768]{1,0:T(8,128)(2,1)S(1)}, u32[]{:S(2)}, u32[]{:S(2)}) collective-permute-start(bf16[256,768]{1,0:T(8,128)(2,1)} %get-tuple-element.193.refs_2_), channel_id=1, source_target_pairs={{0,1},{1,0},{2,3},{3,2},{4,5},{5,4},{6,7},{7,6},{8,9},{9,8},{10,11... | collective-permute-start | bytes 1179656 | tf_op jit(solution)/shard_map/ppermute | solution.py:661
  104.5 10.1 %collective-permute-start.19 = (bf16[256,768]{1,0:T(8,128)(2,1)}, bf16[256,768]{1,0:T(8,128)(2,1)S(1)}, u32[]{:S(2)}, u32[]{:S(2)}) collective-permute-start(bf16[256,768]{1,0:T(8,128)(2,1)} %get-tuple-element.201.refs_2_), channel_id=1, source_target_pairs={{0,1},{1,0},{2,3},{3,2},{4,5},{5,4},{6,7},{7,6},{8,9},{9,8},{10,11... | collective-permute-start | bytes 1179656 | tf_op jit(solution)/shard_map/ppermute | solution.py:661
  112.5 10.3 %collective-permute-start.20 = (bf16[256,768]{1,0:T(8,128)(2,1)}, bf16[256,768]{1,0:T(8,128)(2,1)S(1)}, u32[]{:S(2)}, u32[]{:S(2)}) collective-permute-start(bf16[256,768]{1,0:T(8,128)(2,1)} %get-tuple-element.205.refs_2_), channel_id=1, source_target_pairs={{0,1},{1,0},{2,3},{3,2},{4,5},{5,4},{6,7},{7,6},{8,9},{9,8},{10,11... | collective-permute-start | bytes 1179656 | tf_op jit(solution)/shard_map/ppermute | solution.py:661
  131.1 20.2 %collective-permute-start.22 = (bf16[256,768]{1,0:T(8,128)(2,1)}, bf16[256,768]{1,0:T(8,128)(2,1)S(1)}, u32[]{:S(2)}, u32[]{:S(2)}) collective-permute-start(bf16[256,768]{1,0:T(8,128)(2,1)} %get-tuple-element.220.refs_3_), channel_id=1, source_target_pairs={{0,1},{1,0},{2,3},{3,2},{4,5},{5,4},{6,7},{7,6},{8,9},{9,8},{10,11... | collective-permute-start | bytes 1179656 | tf_op jit(solution)/shard_map/ppermute | solution.py:661
  132.4 18.9 %collective-permute-start.21 = (bf16[256,768]{1,0:T(8,128)(2,1)S(1)}, bf16[256,768]{1,0:T(8,128)(2,1)S(1)}, u32[]{:S(2)}, u32[]{:S(2)}) collective-permute-start(bf16[256,768]{1,0:T(8,128)(2,1)S(1)} %copy-done.61), channel_id=1, source_target_pairs={{0,1},{1,0},{2,3},{3,2},{4,5},{5,4},{6,7},{7,6},{8,9},{9,8},{10,11... | collective-permute-start | bytes 1179656 | tf_op jit(solution)/shard_map/ppermute | solution.py:661
  141.0 35.9 %collective-permute-start.24 = (bf16[1568,768]{1,0:T(8,128)(2,1)}, bf16[1568,768]{1,0:T(8,128)(2,1)S(1)}, u32[]{:S(2)}, u32[]{:S(2)}) collective-permute-start(bf16[1568,768]{1,0:T(8,128)(2,1)} %get-tuple-element.237), channel_id=1, source_target_pairs={{0,16},{16,0},{1,17},{17,1},{2,18},{18,2},{3,19},{19,3},{4,20},{20... | collective-permute-start | bytes 7225352 | tf_op jit(solution)/shard_map/ppermute | solution.py:661
  173.3 10.1 %collective-permute-start.25 = (bf16[256,768]{1,0:T(8,128)(2,1)S(1)}, bf16[256,768]{1,0:T(8,128)(2,1)S(1)}, u32[]{:S(2)}, u32[]{:S(2)}) collective-permute-start(bf16[256,768]{1,0:T(8,128)(2,1)S(1)} %copy-done.45), channel_id=1, source_target_pairs={{0,1},{1,0},{2,3},{3,2},{4,5},{5,4},{6,7},{7,6},{8,9},{9,8},{10,11... | collective-permute-start | bytes 1179656 | tf_op jit(solution)/shard_map/ppermute | solution.py:661
  177.8 14.9 %collective-permute-start.26 = (bf16[384,768]{1,0:T(8,128)(2,1)}, bf16[384,768]{1,0:T(8,128)(2,1)}, u32[]{:S(2)}, u32[]{:S(2)}) collective-permute-start(bf16[384,768]{1,0:T(8,128)(2,1)} %slice_add_fusion.10), channel_id=1, source_target_pairs={{0,2},{2,0},{4,6},{6,4},{8,10},{10,8},{12,14},{14,12},{1,3},{3,1},... | collective-permute-start | bytes 1769480 | tf_op jit(solution)/shard_map/ppermute | solution.py:675
  178.8 17.1 %collective-permute-start.27 = (bf16[256,768]{1,0:T(8,128)(2,1)S(1)}, bf16[256,768]{1,0:T(8,128)(2,1)S(1)}, u32[]{:S(2)}, u32[]{:S(2)}) collective-permute-start(bf16[256,768]{1,0:T(8,128)(2,1)S(1)} %copy-done.44), channel_id=1, source_target_pairs={{0,1},{1,0},{2,3},{3,2},{4,5},{5,4},{6,7},{7,6},{8,9},{9,8},{10,11... | collective-permute-start | bytes 1179656 | tf_op jit(solution)/shard_map/ppermute | solution.py:661
  179.9 34.4 %collective-permute-start.28 = (bf16[400,768]{1,0:T(8,128)(2,1)S(1)}, bf16[400,768]{1,0:T(8,128)(2,1)}, u32[]{:S(2)}, u32[]{:S(2)}) collective-permute-start(bf16[400,768]{1,0:T(8,128)(2,1)S(1)} %slice_add_fusion.3), channel_id=1, source_target_pairs={{0,2},{2,0},{4,6},{6,4},{8,10},{10,8},{12,14},{14,12},{1,3},{3,1},... | collective-permute-start | bytes 1843208 | tf_op jit(solution)/shard_map/ppermute | solution.py:675
  180.6 64.1 %collective-permute-start.36 = (bf16[784,384]{1,0:T(8,128)(2,1)}, bf16[784,384]{1,0:T(8,128)(2,1)}, u32[]{:S(2)}, u32[]{:S(2)}) collective-permute-start(bf16[784,384]{1,0:T(8,128)(2,1)} %slice_add_fusion.7), channel_id=1, source_target_pairs={{0,2},{2,0},{4,6},{6,4},{8,10},{10,8},{12,14},{14,12},{1,3},{3,1},... | collective-permute-start | bytes 1806344 | tf_op jit(solution)/shard_map/ppermute | solution.py:675
  191.4 26.7 %collective-permute-start.29 = (bf16[256,768]{1,0:T(8,128)(2,1)}, bf16[256,768]{1,0:T(8,128)(2,1)}, u32[]{:S(2)}, u32[]{:S(2)}) collective-permute-start(bf16[256,768]{1,0:T(8,128)(2,1)} %get-tuple-element.261.refs_2_), channel_id=1, source_target_pairs={{0,1},{1,0},{2,3},{3,2},{4,5},{5,4},{6,7},{7,6},{8,9},{9,8},{10,11... | collective-permute-start | bytes 1179656 | tf_op jit(solution)/shard_map/ppermute | solution.py:661
  194.6 53.1 %collective-permute-start.37 = (bf16[384,768]{1,0:T(8,128)(2,1)}, bf16[384,768]{1,0:T(8,128)(2,1)}, u32[]{:S(2)}, u32[]{:S(2)}) collective-permute-start(bf16[384,768]{1,0:T(8,128)(2,1)} %fusion.5), channel_id=1, source_target_pairs={{0,4},{2,6},{12,8},{14,10},{1,5},{3,7},{13,9},{15,11},{16,20},{18,... | collective-permute-start | bytes 1769480 | tf_op jit(solution)/shard_map/ppermute | solution.py:950
  203.9 15.5 %collective-permute-start.30 = (bf16[256,768]{1,0:T(8,128)(2,1)}, bf16[256,768]{1,0:T(8,128)(2,1)S(1)}, u32[]{:S(2)}, u32[]{:S(2)}) collective-permute-start(bf16[256,768]{1,0:T(8,128)(2,1)} %get-tuple-element.262.refs_3_), channel_id=1, source_target_pairs={{0,1},{1,0},{2,3},{3,2},{4,5},{5,4},{6,7},{7,6},{8,9},{9,8},{10,11... | collective-permute-start | bytes 1179656 | tf_op jit(solution)/shard_map/ppermute | solution.py:661
  214.3 30.0 %collective-permute-start.35 = (bf16[1568,768]{1,0:T(8,128)(2,1)}, bf16[1568,768]{1,0:T(8,128)(2,1)S(1)}, u32[]{:S(2)}, u32[]{:S(2)}) collective-permute-start(bf16[1568,768]{1,0:T(8,128)(2,1)} %get-tuple-element.282), channel_id=1, source_target_pairs={{0,16},{16,0},{1,17},{17,1},{2,18},{18,2},{3,19},{19,3},{4,20},{20... | collective-permute-start | bytes 7225352 | tf_op jit(solution)/shard_map/ppermute | solution.py:661
  218.1 22.7 %collective-permute-start.34 = (bf16[400,768]{1,0:T(8,128)(2,1)S(1)}, bf16[400,768]{1,0:T(8,128)(2,1)S(1)}, u32[]{:S(2)}, u32[]{:S(2)}) collective-permute-start(bf16[400,768]{1,0:T(8,128)(2,1)S(1)} %fusion.1), channel_id=1, source_target_pairs={{0,4},{2,6},{12,8},{14,10},{1,5},{3,7},{13,9},{15,11},{16,20},{18,... | collective-permute-start | bytes 1843208 | tf_op jit(solution)/shard_map/ppermute | solution.py:950
  239.3 10.9 %collective-permute-start.38 = (bf16[1568,384]{1,0:T(8,128)(2,1)}, bf16[1568,384]{1,0:T(8,128)(2,1)S(1)}, u32[]{:S(2)}, u32[]{:S(2)}) collective-permute-start(bf16[1568,384]{1,0:T(8,128)(2,1)} %get-tuple-element.286), channel_id=1, source_target_pairs={{0,16},{16,0},{1,17},{17,1},{2,18},{18,2},{3,19},{19,3},{4,20},{20... | collective-permute-start | bytes 3612680 | tf_op jit(solution)/shard_map/ppermute | solution.py:661
  240.9 21.9 %collective-permute-start.40 = (bf16[400,768]{1,0:T(8,128)(2,1)S(1)}, bf16[400,768]{1,0:T(8,128)(2,1)S(1)}, u32[]{:S(2)}, u32[]{:S(2)}) collective-permute-start(bf16[400,768]{1,0:T(8,128)(2,1)S(1)} %add.120), channel_id=1, source_target_pairs={{4,8},{6,10},{8,4},{10,6},{5,9},{7,11},{9,5},{11,7},{20,24},{22,26... | collective-permute-start | bytes 1843208 | tf_op jit(solution)/shard_map/ppermute | solution.py:950
  244.4 20.8 %collective-permute-start.41 = (bf16[400,768]{1,0:T(8,128)(2,1)S(1)}, bf16[400,768]{1,0:T(8,128)(2,1)S(1)}, u32[]{:S(2)}, u32[]{:S(2)}) collective-permute-start(bf16[400,768]{1,0:T(8,128)(2,1)S(1)} %slice_add_fusion.1), channel_id=1, source_target_pairs={{0,2},{2,0},{4,6},{6,4},{8,10},{10,8},{12,14},{14,12},{1,3},{3,1},... | collective-permute-start | bytes 1843208 | tf_op jit(solution)/shard_map/ppermute | solution.py:675
  246.4 16.3 %collective-permute-start.39 = (bf16[784,384]{1,0:T(8,128)(2,1)S(1)}, bf16[784,384]{1,0:T(8,128)(2,1)S(1)}, u32[]{:S(2)}, u32[]{:S(2)}) collective-permute-start(bf16[784,384]{1,0:T(8,128)(2,1)S(1)} %fusion.3), channel_id=1, source_target_pairs={{0,4},{2,6},{12,8},{14,10},{1,5},{3,7},{13,9},{15,11},{16,20},{18,... | collective-permute-start | bytes 1806344 | tf_op jit(solution)/shard_map/ppermute | solution.py:950
  247.8 23.9 %collective-permute-start.43 = (bf16[384,768]{1,0:T(8,128)(2,1)S(1)}, bf16[384,768]{1,0:T(8,128)(2,1)S(1)}, u32[]{:S(2)}, u32[]{:S(2)}) collective-permute-start(bf16[384,768]{1,0:T(8,128)(2,1)S(1)} %slice_add_fusion.8), channel_id=1, source_target_pairs={{0,2},{2,0},{4,6},{6,4},{8,10},{10,8},{12,14},{14,12},{1,3},{3,1},... | collective-permute-start | bytes 1769480 | tf_op jit(solution)/shard_map/ppermute | solution.py:675
  250.2 22.6 %collective-permute-start.44 = (bf16[384,768]{1,0:T(8,128)(2,1)S(1)}, bf16[384,768]{1,0:T(8,128)(2,1)S(1)}, u32[]{:S(2)}, u32[]{:S(2)}) collective-permute-start(bf16[384,768]{1,0:T(8,128)(2,1)S(1)} %add.124), channel_id=1, source_target_pairs={{4,8},{6,10},{8,4},{10,6},{5,9},{7,11},{9,5},{11,7},{20,24},{22,26... | collective-permute-start | bytes 1769480 | tf_op jit(solution)/shard_map/ppermute | solution.py:950
  263.0 14.7 %collective-permute-start.42 = (bf16[400,768]{1,0:T(8,128)(2,1)S(1)}, bf16[400,768]{1,0:T(8,128)(2,1)}, u32[]{:S(2)}, u32[]{:S(2)}) collective-permute-start(bf16[400,768]{1,0:T(8,128)(2,1)S(1)} %add.127), channel_id=1, source_target_pairs={{4,0},{6,2},{8,12},{10,14},{5,1},{7,3},{9,13},{11,15},{20,16},{22,... | collective-permute-start | bytes 1843208 | tf_op jit(solution)/shard_map/ppermute | solution.py:950
  265.2 15.6 %collective-permute-start.45 = (bf16[400,768]{1,0:T(8,128)(2,1)S(1)}, bf16[400,768]{1,0:T(8,128)(2,1)}, u32[]{:S(2)}, u32[]{:S(2)}) collective-permute-start(bf16[400,768]{1,0:T(8,128)(2,1)S(1)} %fusion), channel_id=1, source_target_pairs={{0,4},{2,6},{12,8},{14,10},{1,5},{3,7},{13,9},{15,11},{16,20},{18,... | collective-permute-start | bytes 1843208 | tf_op jit(solution)/shard_map/ppermute | solution.py:950
  266.5 16.0 %collective-permute-start.46 = (bf16[784,384]{1,0:T(8,128)(2,1)S(1)}, bf16[784,384]{1,0:T(8,128)(2,1)}, u32[]{:S(2)}, u32[]{:S(2)}) collective-permute-start(bf16[784,384]{1,0:T(8,128)(2,1)S(1)} %add.126), channel_id=1, source_target_pairs={{4,8},{6,10},{8,4},{10,6},{5,9},{7,11},{9,5},{11,7},{20,24},{22,26... | collective-permute-start | bytes 1806344 | tf_op jit(solution)/shard_map/ppermute | solution.py:950
  271.7 13.7 %collective-permute-start.47 = (bf16[784,384]{1,0:T(8,128)(2,1)}, bf16[784,384]{1,0:T(8,128)(2,1)}, u32[]{:S(2)}, u32[]{:S(2)}) collective-permute-start(bf16[784,384]{1,0:T(8,128)(2,1)} %slice_add_fusion.5), channel_id=1, source_target_pairs={{0,2},{2,0},{4,6},{6,4},{8,10},{10,8},{12,14},{14,12},{1,3},{3,1},... | collective-permute-start | bytes 1806344 | tf_op jit(solution)/shard_map/ppermute | solution.py:675
  273.8 16.9 %collective-permute-start.49 = (bf16[384,768]{1,0:T(8,128)(2,1)}, bf16[384,768]{1,0:T(8,128)(2,1)}, u32[]{:S(2)}, u32[]{:S(2)}) collective-permute-start(bf16[384,768]{1,0:T(8,128)(2,1)} %add.133), channel_id=1, source_target_pairs={{4,0},{6,2},{8,12},{10,14},{5,1},{7,3},{9,13},{11,15},{20,16},{22,... | collective-permute-start | bytes 1769480 | tf_op jit(solution)/shard_map/ppermute | solution.py:950
  277.7 27.7 %collective-permute-start.51 = (bf16[384,768]{1,0:T(8,128)(2,1)}, bf16[384,768]{1,0:T(8,128)(2,1)}, u32[]{:S(2)}, u32[]{:S(2)}) collective-permute-start(bf16[384,768]{1,0:T(8,128)(2,1)} %fusion.4), channel_id=1, source_target_pairs={{0,4},{2,6},{12,8},{14,10},{1,5},{3,7},{13,9},{15,11},{16,20},{18,... | collective-permute-start | bytes 1769480 | tf_op jit(solution)/shard_map/ppermute | solution.py:950
  286.6 24.6 %collective-permute-start.52 = (bf16[784,384]{1,0:T(8,128)(2,1)S(1)}, bf16[784,384]{1,0:T(8,128)(2,1)}, u32[]{:S(2)}, u32[]{:S(2)}) collective-permute-start(bf16[784,384]{1,0:T(8,128)(2,1)S(1)} %fusion.2), channel_id=1, source_target_pairs={{0,4},{2,6},{12,8},{14,10},{1,5},{3,7},{13,9},{15,11},{16,20},{18,... | collective-permute-start | bytes 1806344 | tf_op jit(solution)/shard_map/ppermute | solution.py:950
  287.9 14.8 %collective-permute-start.50 = (bf16[400,768]{1,0:T(8,128)(2,1)S(1)}, bf16[400,768]{1,0:T(8,128)(2,1)}, u32[]{:S(2)}, u32[]{:S(2)}) collective-permute-start(bf16[400,768]{1,0:T(8,128)(2,1)S(1)} %add.134), channel_id=1, source_target_pairs={{4,8},{6,10},{8,4},{10,6},{5,9},{7,11},{9,5},{11,7},{20,24},{22,26... | collective-permute-start | bytes 1843208 | tf_op jit(solution)/shard_map/ppermute | solution.py:950
  291.9 18.1 %collective-permute-start.67 = (bf16[384,768]{1,0:T(8,128)(2,1)S(1)}, bf16[384,768]{1,0:T(8,128)(2,1)}, u32[]{:S(2)}, u32[]{:S(2)}) collective-permute-start(bf16[384,768]{1,0:T(8,128)(2,1)S(1)} %broadcast_select_fusion.5.refs_13_), channel_id=1, source_target_pairs={{0,2},{2,0},{4,6},{6,4},{8,10},{10,8},{12,14},{14,12},{1,3},{3,1},... | collective-permute-start | bytes 1769480 | tf_op jit(solution)/shard_map/ppermute | solution.py:675
  291.9 19.4 %collective-permute-start.48 = (bf16[784,384]{1,0:T(8,128)(2,1)S(1)}, bf16[784,384]{1,0:T(8,128)(2,1)}, u32[]{:S(2)}, u32[]{:S(2)}) collective-permute-start(bf16[784,384]{1,0:T(8,128)(2,1)S(1)} %add.135), channel_id=1, source_target_pairs={{4,0},{6,2},{8,12},{10,14},{5,1},{7,3},{9,13},{11,15},{20,16},{22,... | collective-permute-start | bytes 1806344 | tf_op jit(solution)/shard_map/ppermute | solution.py:950
  303.9 21.1 %collective-permute-start.53 = (bf16[400,768]{1,0:T(8,128)(2,1)S(1)}, bf16[400,768]{1,0:T(8,128)(2,1)S(1)}, u32[]{:S(2)}, u32[]{:S(2)}) collective-permute-start(bf16[400,768]{1,0:T(8,128)(2,1)S(1)} %add.138), channel_id=1, source_target_pairs={{4,0},{6,2},{8,12},{10,14},{5,1},{7,3},{9,13},{11,15},{20,16},{22,... | collective-permute-start | bytes 1843208 | tf_op jit(solution)/shard_map/ppermute | solution.py:950
  306.8 13.2 %collective-permute-start.54 = (bf16[384,768]{1,0:T(8,128)(2,1)S(1)}, bf16[384,768]{1,0:T(8,128)(2,1)S(1)}, u32[]{:S(2)}, u32[]{:S(2)}) collective-permute-start(bf16[384,768]{1,0:T(8,128)(2,1)S(1)} %add.139), channel_id=1, source_target_pairs={{4,8},{6,10},{8,4},{10,6},{5,9},{7,11},{9,5},{11,7},{20,24},{22,26... | collective-permute-start | bytes 1769480 | tf_op jit(solution)/shard_map/ppermute | solution.py:950
  309.9 13.8 %collective-permute-start.32 = (bf16[256,768]{1,0:T(8,128)(2,1)S(1)}, bf16[256,768]{1,0:T(8,128)(2,1)S(1)}, u32[]{:S(2)}, u32[]{:S(2)}) collective-permute-start(bf16[256,768]{1,0:T(8,128)(2,1)S(1)} %constant_dynamic-slice_fusion), channel_id=1, source_target_pairs={{0,16},{1,17},{2,18},{3,19},{4,20},{5,21},{6,22},{7,23},{8,24},{9,... | collective-permute-start | bytes 1179656 | tf_op jit(solution)/shard_map/ppermute | solution.py:1035
  311.2 15.3 %collective-permute-start.64 = (bf16[400,768]{1,0:T(8,128)(2,1)S(1)}, bf16[400,768]{1,0:T(8,128)(2,1)S(1)}, u32[]{:S(2)}, u32[]{:S(2)}) collective-permute-start(bf16[400,768]{1,0:T(8,128)(2,1)S(1)} %broadcast_select_fusion.1.refs_9_), channel_id=1, source_target_pairs={{0,2},{2,0},{4,6},{6,4},{8,10},{10,8},{12,14},{14,12},{1,3},{3,1},... | collective-permute-start | bytes 1843208 | tf_op jit(solution)/shard_map/ppermute | solution.py:675
  311.4 15.1 %collective-permute-start.31 = (bf16[256,768]{1,0:T(8,128)(2,1)S(1)}, bf16[256,768]{1,0:T(8,128)(2,1)S(1)}, u32[]{:S(2)}, u32[]{:S(2)}) collective-permute-start(bf16[256,768]{1,0:T(8,128)(2,1)S(1)} %broadcast_select_fusion.6), channel_id=1, source_target_pairs={{0,1},{1,0},{2,3},{3,2},{4,5},{5,4},{6,7},{7,6},{8,9},{9,8},{10,11... | collective-permute-start | bytes 1179656 | tf_op jit(solution)/shard_map/ppermute | solution.py:661
  320.0 12.9 %collective-permute-start.55 = (bf16[784,384]{1,0:T(8,128)(2,1)S(1)}, bf16[784,384]{1,0:T(8,128)(2,1)S(1)}, u32[]{:S(2)}, u32[]{:S(2)}) collective-permute-start(bf16[784,384]{1,0:T(8,128)(2,1)S(1)} %add.140), channel_id=1, source_target_pairs={{4,8},{6,10},{8,4},{10,6},{5,9},{7,11},{9,5},{11,7},{20,24},{22,26... | collective-permute-start | bytes 1806344 | tf_op jit(solution)/shard_map/ppermute | solution.py:950
  326.5 21.1 %collective-permute-start.58 = (bf16[400,768]{1,0:T(8,128)(2,1)S(1)}, bf16[400,768]{1,0:T(8,128)(2,1)S(1)}, u32[]{:S(2)}, u32[]{:S(2)}) collective-permute-start(bf16[400,768]{1,0:T(8,128)(2,1)S(1)} %broadcast_select_fusion.refs_1_), channel_id=1, source_target_pairs={{0,2},{2,0},{4,6},{6,4},{8,10},{10,8},{12,14},{14,12},{1,3},{3,1},... | collective-permute-start | bytes 1843208 | tf_op jit(solution)/shard_map/ppermute | solution.py:675
  326.6 19.7 %collective-permute-start.69 = (bf16[384,768]{1,0:T(8,128)(2,1)}, bf16[384,768]{1,0:T(8,128)(2,1)}, u32[]{:S(2)}, u32[]{:S(2)}) collective-permute-start(bf16[384,768]{1,0:T(8,128)(2,1)} %collective-permute-done.67.refs_14_), channel_id=1, source_target_pairs={{0,16},{1,17},{2,18},{3,19},{4,20},{5,21},{6,22},{7,23},{8,24},{9,... | collective-permute-start | bytes 1769480 | tf_op jit(solution)/shard_map/ppermute | solution.py:960
  332.9 17.7 %collective-permute-start.73 = (bf16[784,384]{1,0:T(8,128)(2,1)S(1)}, bf16[784,384]{1,0:T(8,128)(2,1)}, u32[]{:S(2)}, u32[]{:S(2)}) collective-permute-start(bf16[784,384]{1,0:T(8,128)(2,1)S(1)} %broadcast_select_fusion.3.refs_5_), channel_id=1, source_target_pairs={{0,2},{2,0},{4,6},{6,4},{8,10},{10,8},{12,14},{14,12},{1,3},{3,1},... | collective-permute-start | bytes 1806344 | tf_op jit(solution)/shard_map/ppermute | solution.py:675
  333.1 18.8 %collective-permute-start.56 = (bf16[784,384]{1,0:T(8,128)(2,1)S(1)}, bf16[784,384]{1,0:T(8,128)(2,1)S(1)}, u32[]{:S(2)}, u32[]{:S(2)}) collective-permute-start(bf16[784,384]{1,0:T(8,128)(2,1)S(1)} %add.142), channel_id=1, source_target_pairs={{4,0},{6,2},{8,12},{10,14},{5,1},{7,3},{9,13},{11,15},{20,16},{22,... | collective-permute-start | bytes 1806344 | tf_op jit(solution)/shard_map/ppermute | solution.py:950
  335.0 29.0 %collective-permute-start.59 = (bf16[400,768]{1,0:T(8,128)(2,1)S(1)}, bf16[400,768]{1,0:T(8,128)(2,1)S(1)}, u32[]{:S(2)}, u32[]{:S(2)}) collective-permute-start(bf16[400,768]{1,0:T(8,128)(2,1)S(1)} %broadcast_select_fusion.refs_1_), channel_id=1, source_target_pairs={{16,0},{17,1},{18,2},{19,3},{20,4},{21,5},{22,6},{23,7},{24,8},{25... | collective-permute-start | bytes 1843208 | tf_op jit(solution)/shard_map/ppermute | solution.py:960
  346.3 25.1 %collective-permute-start.65 = (bf16[400,768]{1,0:T(8,128)(2,1)S(1)}, bf16[400,768]{1,0:T(8,128)(2,1)S(1)}, u32[]{:S(2)}, u32[]{:S(2)}) collective-permute-start(bf16[400,768]{1,0:T(8,128)(2,1)S(1)} %broadcast_select_fusion.1.refs_9_), channel_id=1, source_target_pairs={{0,16},{1,17},{2,18},{3,19},{4,20},{5,21},{6,22},{7,23},{8,24},{9,... | collective-permute-start | bytes 1843208 | tf_op jit(solution)/shard_map/ppermute | solution.py:960
  347.6 16.5 %collective-permute-start.61 = (bf16[384,768]{1,0:T(8,128)(2,1)S(1)}, bf16[384,768]{1,0:T(8,128)(2,1)S(1)}, u32[]{:S(2)}, u32[]{:S(2)}) collective-permute-start(bf16[384,768]{1,0:T(8,128)(2,1)S(1)} %broadcast_select_fusion.4.refs_5_), channel_id=1, source_target_pairs={{0,2},{2,0},{4,6},{6,4},{8,10},{10,8},{12,14},{14,12},{1,3},{3,1},... | collective-permute-start | bytes 1769480 | tf_op jit(solution)/shard_map/ppermute | solution.py:675
  350.6 23.2 %collective-permute-start.66 = (bf16[400,768]{1,0:T(8,128)(2,1)S(1)}, bf16[400,768]{1,0:T(8,128)(2,1)S(1)}, u32[]{:S(2)}, u32[]{:S(2)}) collective-permute-start(bf16[400,768]{1,0:T(8,128)(2,1)S(1)} %collective-permute-done.64.refs_10_), channel_id=1, source_target_pairs={{0,16},{1,17},{2,18},{3,19},{4,20},{5,21},{6,22},{7,23},{8,24},{9,... | collective-permute-start | bytes 1843208 | tf_op jit(solution)/shard_map/ppermute | solution.py:960
  351.9 24.6 %collective-permute-start.60 = (bf16[400,768]{1,0:T(8,128)(2,1)S(1)}, bf16[400,768]{1,0:T(8,128)(2,1)S(1)}, u32[]{:S(2)}, u32[]{:S(2)}) collective-permute-start(bf16[400,768]{1,0:T(8,128)(2,1)S(1)} %collective-permute-done.58.refs_2_), channel_id=1, source_target_pairs={{16,0},{17,1},{18,2},{19,3},{20,4},{21,5},{22,6},{23,7},{24,8},{25... | collective-permute-start | bytes 1843208 | tf_op jit(solution)/shard_map/ppermute | solution.py:960
  364.0 20.7 %collective-permute-start.70 = (bf16[784,384]{1,0:T(8,128)(2,1)S(1)}, bf16[784,384]{1,0:T(8,128)(2,1)S(1)}, u32[]{:S(2)}, u32[]{:S(2)}) collective-permute-start(bf16[784,384]{1,0:T(8,128)(2,1)S(1)} %broadcast_select_fusion.2.refs_1_), channel_id=1, source_target_pairs={{0,2},{2,0},{4,6},{6,4},{8,10},{10,8},{12,14},{14,12},{1,3},{3,1},... | collective-permute-start | bytes 1806344 | tf_op jit(solution)/shard_map/ppermute | solution.py:675
  364.1 11.1 %collective-permute-start.62 = (bf16[384,768]{1,0:T(8,128)(2,1)S(1)}, bf16[384,768]{1,0:T(8,128)(2,1)S(1)}, u32[]{:S(2)}, u32[]{:S(2)}) collective-permute-start(bf16[384,768]{1,0:T(8,128)(2,1)S(1)} %broadcast_select_fusion.4.refs_5_), channel_id=1, source_target_pairs={{16,0},{17,1},{18,2},{19,3},{20,4},{21,5},{22,6},{23,7},{24,8},{25... | collective-permute-start | bytes 1769480 | tf_op jit(solution)/shard_map/ppermute | solution.py:960
  373.9 15.3 %collective-permute-start.33 = (bf16[256,768]{1,0:T(8,128)(2,1)S(1)}, bf16[256,768]{1,0:T(8,128)(2,1)S(1)}, u32[]{:S(2)}, u32[]{:S(2)}) collective-permute-start(bf16[256,768]{1,0:T(8,128)(2,1)S(1)} %get-tuple-element.337), channel_id=1, source_target_pairs={{16,0},{17,1},{18,2},{19,3},{20,4},{21,5},{22,6},{23,7},{24,8},{25... | collective-permute-start | bytes 1179656 | tf_op jit(solution)/shard_map/ppermute | solution.py:1036
  375.2 15.0 %collective-permute-start.74 = (bf16[784,384]{1,0:T(8,128)(2,1)S(1)}, bf16[784,384]{1,0:T(8,128)(2,1)S(1)}, u32[]{:S(2)}, u32[]{:S(2)}) collective-permute-start(bf16[784,384]{1,0:T(8,128)(2,1)S(1)} %broadcast_select_fusion.3.refs_5_), channel_id=1, source_target_pairs={{0,16},{1,17},{2,18},{3,19},{4,20},{5,21},{6,22},{7,23},{8,24},{9,... | collective-permute-start | bytes 1806344 | tf_op jit(solution)/shard_map/ppermute | solution.py:960
  376.6 13.7 %collective-permute-start.75 = (bf16[784,384]{1,0:T(8,128)(2,1)}, bf16[784,384]{1,0:T(8,128)(2,1)S(1)}, u32[]{:S(2)}, u32[]{:S(2)}) collective-permute-start(bf16[784,384]{1,0:T(8,128)(2,1)} %collective-permute-done.73.refs_6_), channel_id=1, source_target_pairs={{0,16},{1,17},{2,18},{3,19},{4,20},{5,21},{6,22},{7,23},{8,24},{9,... | collective-permute-start | bytes 1806344 | tf_op jit(solution)/shard_map/ppermute | solution.py:960
  (80 other events, 777.3 us)
